TPU v7x, 512 devices: a whole 4x8x8 slice. The times are simulated.
512 devices in a mesh: layer: 2 (over core), row: 16 (over y, x_lo), col: 16 (over x_hi, z).
Axes of the slice: x: 4 (x_hi: 2, x_lo: 2; x = x_hi * 2 + x_lo), y: 8, z: 8, core: 2. Of those that a mesh axis runs over, the one named last changes fastest.
Arguments:
- amplitudes: bfloat16 [896, 73728], P('row', ('layer', 'col')), may hold values from -6 to 6
- integrals: bfloat16 [73728, 2048], P(('layer', 'row'), 'col'), may hold values from -0.0234375 to 0.0234375
- other_terms: float32 [896, 2048], P('row', 'col'), may hold values from -6 to 6
- occ_energy: float32 [896], P('row'), may hold values from -4 to -1
- virt_energy: float32 [2048], P('col'), may hold values from 0.5 to 6
Outputs:
- new_amplitudes: float32 [896, 2048], P('row', 'col')
All inputs are finite; a program needn't handle non-finite values.
Results may differ from a plain program's by a relative error of at most 0.0003.
Values may be sent and summed in bfloat16 or wider, within the bound.
No kernel may reach another device: no remote copies, remote signals or barrier semaphores. Data moves between devices by JAX's collectives and lax.ppermute only.
A program may use at most 64 MiB of HBM per device.

v0:
```python
import jax
import jax.numpy as jnp
from jax import lax
from jax.sharding import PartitionSpec as P


def passed_along(block, axis, distance):
    devices = range(lax.axis_size(axis))
    route = [((i - distance) % len(devices), i) for i in devices]
    return lax.ppermute(block, axis, route)


def body(amplitudes, integrals, other_terms, occ_energy, virt_energy):
    grid = lax.axis_size("row")
    row_index = lax.axis_index("row")
    col_index = lax.axis_index("col")
    left = amplitudes
    right = integrals
    for level in range(grid.bit_length() - 1):
        moved_left = passed_along(left, "col", -(1 << level))
        left = jnp.where((row_index >> level) % 2 == 1, moved_left, left)
        moved_right = passed_along(right, "row", -(1 << level))
        right = jnp.where((col_index >> level) % 2 == 1, moved_right, right)
    start_total = jnp.dot(left, right, preferred_element_type=jnp.float32)

    def one_turn(step, carry):
        total, left_now, right_now = carry
        left_now = passed_along(left_now, "col", -1)
        right_now = passed_along(right_now, "row", -1)
        total = total + jnp.dot(left_now, right_now, preferred_element_type=jnp.float32)
        return (total, left_now, right_now)

    partial_ladder, left, right = lax.fori_loop(0, grid - 1, one_turn, (start_total, left, right))
    ladder = lax.psum(partial_ladder, "layer")
    denominator = occ_energy[:, None] - virt_energy[None, :]
    return (ladder + other_terms) / denominator


def solution(mesh):
    in_specs = (
        P("row", ("layer", "col")),
        P(("layer", "row"), "col"),
        P("row", "col"),
        P("row"),
        P("col"),
    )
    out_specs = P("row", "col")
    return jax.shard_map(body, mesh=mesh, in_specs=in_specs, out_specs=out_specs, check_vma=False)
```

profile of v0, /device:TPU:25, one launch (start us, length us, event | category | flops | bytes accessed | tf_op | source)
XLA Modules:
  0.0 453.6 jit_solution(101270196984452820)
XLA Ops:
  0.0 13.2 %collective-permute-start.2 = (bf16[56,2304]{1,0:T(8,128)(2,1)}, bf16[56,2304]{1,0:T(8,128)(2,1)S(1)}, u32[]{:S(2)}, u32[]{:S(2)}) collective-permute-start(bf16[56,2304]{1,0:T(8,128)(2,1)} %param.7), channel_id=1, source_target_pairs={{1,0},{2,1},{3,2},{4,3},{5,4},{6,5},{7,6},{8,7},{9,8},{10,9},{11,1... | collective-permute-start | bytes 774152 | tf_op jit(solution)/shard_map/ppermute | solution.py:10
  15.4 4.5 collective-permute-done.2
  23.4 5.8 %collective-permute-done.6 = bf16[2304,128]{1,0:T(8,128)(2,1)S(1)} collective-permute-done((bf16[2304,128]{1,0:T(8,128)(2,1)}, bf16[2304,128]{1,0:T(8,128)(2,1)S(1)}, u32[]{:S(2)}, u32[]{:S(2)}) %collective-permute-start.6) | collective-permute-done | bytes 589856 | tf_op jit(solution)/shard_map/ppermute | solution.py:10
  36.9 8.5 %collective-permute-done.7 = bf16[2304,128]{1,0:T(8,128)(2,1)S(1)} collective-permute-done((bf16[2304,128]{1,0:T(8,128)(2,1)S(1)}, bf16[2304,128]{1,0:T(8,128)(2,1)S(1)}, u32[]{:S(2)}, u32[]{:S(2)}) %collective-permute-start.7) | collective-permute-done | bytes 589856 | tf_op jit(solution)/shard_map/ppermute | solution.py:10
  51.7 24.0 %collective-permute-done.8 = bf16[2304,128]{1,0:T(8,128)(2,1)S(1)} collective-permute-done((bf16[2304,128]{1,0:T(8,128)(2,1)S(1)}, bf16[2304,128]{1,0:T(8,128)(2,1)S(1)}, u32[]{:S(2)}, u32[]{:S(2)}) %collective-permute-start.8) | collective-permute-done | bytes 589856 | tf_op jit(solution)/shard_map/ppermute | solution.py:10
  75.8 4.4 collective-permute-start.9
  80.3 29.1 %collective-permute-done.9 = bf16[2304,128]{1,0:T(8,128)(2,1)S(1)} collective-permute-done((bf16[2304,128]{1,0:T(8,128)(2,1)S(1)}, bf16[2304,128]{1,0:T(8,128)(2,1)S(1)}, u32[]{:S(2)}, u32[]{:S(2)}) %collective-permute-start.9) | collective-permute-done | bytes 589856 | tf_op jit(solution)/shard_map/ppermute | solution.py:10
  109.7 316.2 %while.14 = (s32[]{:T(128)}, f32[56,128]{1,0:T(8,128)S(1)}, bf16[56,2304]{1,0:T(8,128)(2,1)S(1)}, bf16[2304,128]{1,0:T(8,128)(2,1)S(1)}, s32[]{:T(128)}) while((s32[]{:T(128)}, f32[56,128]{1,0:T(8,128)S(1)}, bf16[56,2304]{1,0:T(8,128)(2,1)S(1)}, bf16[2304,128]{1,0:T(8,128)(2,1)S(1)}, s32[]{:T(128)}) %tuple.18), condition=%wide.region_1.2_spmd, body=%wide.region_0.1_spmd.sunk | while | flops 33037312 | bytes 5992589 | solution.py:33
  111.6 14.9 %collective-permute-start = (bf16[56,2304]{1,0:T(8,128)(2,1)S(1)}, bf16[56,2304]{1,0:T(8,128)(2,1)S(1)}, u32[]{:S(2)}, u32[]{:S(2)}) collective-permute-start(bf16[56,2304]{1,0:T(8,128)(2,1)S(1)} %get-tuple-element.68), channel_id=1, source_target_pairs={{1,0},{2,1},{3,2},{4,3},{5,4},{6,5},{7,6},{8,7},{9,8},{10,9},{11,1... | collective-permute-start | bytes 774152 | tf_op jit(solution)/shard_map/while/body/eval_jaxpr/ppermute | solution.py:10
  126.6 6.6 %collective-permute-done = bf16[56,2304]{1,0:T(8,128)(2,1)S(1)} collective-permute-done((bf16[56,2304]{1,0:T(8,128)(2,1)S(1)}, bf16[56,2304]{1,0:T(8,128)(2,1)S(1)}, u32[]{:S(2)}, u32[]{:S(2)}) %collective-permute-start) | collective-permute-done | bytes 258080 | tf_op jit(solution)/shard_map/while/body/eval_jaxpr/ppermute | solution.py:10
  135.5 14.0 %collective-permute-start = (bf16[56,2304]{1,0:T(8,128)(2,1)S(1)}, bf16[56,2304]{1,0:T(8,128)(2,1)S(1)}, u32[]{:S(2)}, u32[]{:S(2)}) collective-permute-start(bf16[56,2304]{1,0:T(8,128)(2,1)S(1)} %get-tuple-element.68), channel_id=1, source_target_pairs={{1,0},{2,1},{3,2},{4,3},{5,4},{6,5},{7,6},{8,7},{9,8},{10,9},{11,1... | collective-permute-start | bytes 774152 | tf_op jit(solution)/shard_map/while/body/eval_jaxpr/ppermute | solution.py:10
  149.5 5.1 %collective-permute-done = bf16[56,2304]{1,0:T(8,128)(2,1)S(1)} collective-permute-done((bf16[56,2304]{1,0:T(8,128)(2,1)S(1)}, bf16[56,2304]{1,0:T(8,128)(2,1)S(1)}, u32[]{:S(2)}, u32[]{:S(2)}) %collective-permute-start) | collective-permute-done | bytes 258080 | tf_op jit(solution)/shard_map/while/body/eval_jaxpr/ppermute | solution.py:10
  156.8 14.5 %collective-permute-start = (bf16[56,2304]{1,0:T(8,128)(2,1)S(1)}, bf16[56,2304]{1,0:T(8,128)(2,1)S(1)}, u32[]{:S(2)}, u32[]{:S(2)}) collective-permute-start(bf16[56,2304]{1,0:T(8,128)(2,1)S(1)} %get-tuple-element.68), channel_id=1, source_target_pairs={{1,0},{2,1},{3,2},{4,3},{5,4},{6,5},{7,6},{8,7},{9,8},{10,9},{11,1... | collective-permute-start | bytes 774152 | tf_op jit(solution)/shard_map/while/body/eval_jaxpr/ppermute | solution.py:10
  171.3 6.6 %collective-permute-done = bf16[56,2304]{1,0:T(8,128)(2,1)S(1)} collective-permute-done((bf16[56,2304]{1,0:T(8,128)(2,1)S(1)}, bf16[56,2304]{1,0:T(8,128)(2,1)S(1)}, u32[]{:S(2)}, u32[]{:S(2)}) %collective-permute-start) | collective-permute-done | bytes 258080 | tf_op jit(solution)/shard_map/while/body/eval_jaxpr/ppermute | solution.py:10
  180.2 10.5 %collective-permute-start = (bf16[56,2304]{1,0:T(8,128)(2,1)S(1)}, bf16[56,2304]{1,0:T(8,128)(2,1)S(1)}, u32[]{:S(2)}, u32[]{:S(2)}) collective-permute-start(bf16[56,2304]{1,0:T(8,128)(2,1)S(1)} %get-tuple-element.68), channel_id=1, source_target_pairs={{1,0},{2,1},{3,2},{4,3},{5,4},{6,5},{7,6},{8,7},{9,8},{10,9},{11,1... | collective-permute-start | bytes 774152 | tf_op jit(solution)/shard_map/while/body/eval_jaxpr/ppermute | solution.py:10
  196.8 15.4 %collective-permute-start = (bf16[56,2304]{1,0:T(8,128)(2,1)S(1)}, bf16[56,2304]{1,0:T(8,128)(2,1)S(1)}, u32[]{:S(2)}, u32[]{:S(2)}) collective-permute-start(bf16[56,2304]{1,0:T(8,128)(2,1)S(1)} %get-tuple-element.68), channel_id=1, source_target_pairs={{1,0},{2,1},{3,2},{4,3},{5,4},{6,5},{7,6},{8,7},{9,8},{10,9},{11,1... | collective-permute-start | bytes 774152 | tf_op jit(solution)/shard_map/while/body/eval_jaxpr/ppermute | solution.py:10
  217.7 15.2 %collective-permute-start = (bf16[56,2304]{1,0:T(8,128)(2,1)S(1)}, bf16[56,2304]{1,0:T(8,128)(2,1)S(1)}, u32[]{:S(2)}, u32[]{:S(2)}) collective-permute-start(bf16[56,2304]{1,0:T(8,128)(2,1)S(1)} %get-tuple-element.68), channel_id=1, source_target_pairs={{1,0},{2,1},{3,2},{4,3},{5,4},{6,5},{7,6},{8,7},{9,8},{10,9},{11,1... | collective-permute-start | bytes 774152 | tf_op jit(solution)/shard_map/while/body/eval_jaxpr/ppermute | solution.py:10
  238.4 15.4 %collective-permute-start = (bf16[56,2304]{1,0:T(8,128)(2,1)S(1)}, bf16[56,2304]{1,0:T(8,128)(2,1)S(1)}, u32[]{:S(2)}, u32[]{:S(2)}) collective-permute-start(bf16[56,2304]{1,0:T(8,128)(2,1)S(1)} %get-tuple-element.68), channel_id=1, source_target_pairs={{1,0},{2,1},{3,2},{4,3},{5,4},{6,5},{7,6},{8,7},{9,8},{10,9},{11,1... | collective-permute-start | bytes 774152 | tf_op jit(solution)/shard_map/while/body/eval_jaxpr/ppermute | solution.py:10
  259.3 15.2 %collective-permute-start = (bf16[56,2304]{1,0:T(8,128)(2,1)S(1)}, bf16[56,2304]{1,0:T(8,128)(2,1)S(1)}, u32[]{:S(2)}, u32[]{:S(2)}) collective-permute-start(bf16[56,2304]{1,0:T(8,128)(2,1)S(1)} %get-tuple-element.68), channel_id=1, source_target_pairs={{1,0},{2,1},{3,2},{4,3},{5,4},{6,5},{7,6},{8,7},{9,8},{10,9},{11,1... | collective-permute-start | bytes 774152 | tf_op jit(solution)/shard_map/while/body/eval_jaxpr/ppermute | solution.py:10
  280.6 12.4 %collective-permute-start = (bf16[56,2304]{1,0:T(8,128)(2,1)S(1)}, bf16[56,2304]{1,0:T(8,128)(2,1)S(1)}, u32[]{:S(2)}, u32[]{:S(2)}) collective-permute-start(bf16[56,2304]{1,0:T(8,128)(2,1)S(1)} %get-tuple-element.68), channel_id=1, source_target_pairs={{1,0},{2,1},{3,2},{4,3},{5,4},{6,5},{7,6},{8,7},{9,8},{10,9},{11,1... | collective-permute-start | bytes 774152 | tf_op jit(solution)/shard_map/while/body/eval_jaxpr/ppermute | solution.py:10
  299.1 9.7 %collective-permute-start = (bf16[56,2304]{1,0:T(8,128)(2,1)S(1)}, bf16[56,2304]{1,0:T(8,128)(2,1)S(1)}, u32[]{:S(2)}, u32[]{:S(2)}) collective-permute-start(bf16[56,2304]{1,0:T(8,128)(2,1)S(1)} %get-tuple-element.68), channel_id=1, source_target_pairs={{1,0},{2,1},{3,2},{4,3},{5,4},{6,5},{7,6},{8,7},{9,8},{10,9},{11,1... | collective-permute-start | bytes 774152 | tf_op jit(solution)/shard_map/while/body/eval_jaxpr/ppermute | solution.py:10
  314.2 9.9 %collective-permute-start = (bf16[56,2304]{1,0:T(8,128)(2,1)S(1)}, bf16[56,2304]{1,0:T(8,128)(2,1)S(1)}, u32[]{:S(2)}, u32[]{:S(2)}) collective-permute-start(bf16[56,2304]{1,0:T(8,128)(2,1)S(1)} %get-tuple-element.68), channel_id=1, source_target_pairs={{1,0},{2,1},{3,2},{4,3},{5,4},{6,5},{7,6},{8,7},{9,8},{10,9},{11,1... | collective-permute-start | bytes 774152 | tf_op jit(solution)/shard_map/while/body/eval_jaxpr/ppermute | solution.py:10
  324.2 3.8 collective-permute-done
  330.9 12.5 %collective-permute-start = (bf16[56,2304]{1,0:T(8,128)(2,1)S(1)}, bf16[56,2304]{1,0:T(8,128)(2,1)S(1)}, u32[]{:S(2)}, u32[]{:S(2)}) collective-permute-start(bf16[56,2304]{1,0:T(8,128)(2,1)S(1)} %get-tuple-element.68), channel_id=1, source_target_pairs={{1,0},{2,1},{3,2},{4,3},{5,4},{6,5},{7,6},{8,7},{9,8},{10,9},{11,1... | collective-permute-start | bytes 774152 | tf_op jit(solution)/shard_map/while/body/eval_jaxpr/ppermute | solution.py:10
  343.4 7.6 %collective-permute-done = bf16[56,2304]{1,0:T(8,128)(2,1)S(1)} collective-permute-done((bf16[56,2304]{1,0:T(8,128)(2,1)S(1)}, bf16[56,2304]{1,0:T(8,128)(2,1)S(1)}, u32[]{:S(2)}, u32[]{:S(2)}) %collective-permute-start) | collective-permute-done | bytes 258080 | tf_op jit(solution)/shard_map/while/body/eval_jaxpr/ppermute | solution.py:10
  353.3 16.3 %collective-permute-start = (bf16[56,2304]{1,0:T(8,128)(2,1)S(1)}, bf16[56,2304]{1,0:T(8,128)(2,1)S(1)}, u32[]{:S(2)}, u32[]{:S(2)}) collective-permute-start(bf16[56,2304]{1,0:T(8,128)(2,1)S(1)} %get-tuple-element.68), channel_id=1, source_target_pairs={{1,0},{2,1},{3,2},{4,3},{5,4},{6,5},{7,6},{8,7},{9,8},{10,9},{11,1... | collective-permute-start | bytes 774152 | tf_op jit(solution)/shard_map/while/body/eval_jaxpr/ppermute | solution.py:10
  369.6 8.8 %collective-permute-done = bf16[56,2304]{1,0:T(8,128)(2,1)S(1)} collective-permute-done((bf16[56,2304]{1,0:T(8,128)(2,1)S(1)}, bf16[56,2304]{1,0:T(8,128)(2,1)S(1)}, u32[]{:S(2)}, u32[]{:S(2)}) %collective-permute-start) | collective-permute-done | bytes 258080 | tf_op jit(solution)/shard_map/while/body/eval_jaxpr/ppermute | solution.py:10
  380.7 13.6 %collective-permute-start = (bf16[56,2304]{1,0:T(8,128)(2,1)S(1)}, bf16[56,2304]{1,0:T(8,128)(2,1)S(1)}, u32[]{:S(2)}, u32[]{:S(2)}) collective-permute-start(bf16[56,2304]{1,0:T(8,128)(2,1)S(1)} %get-tuple-element.68), channel_id=1, source_target_pairs={{1,0},{2,1},{3,2},{4,3},{5,4},{6,5},{7,6},{8,7},{9,8},{10,9},{11,1... | collective-permute-start | bytes 774152 | tf_op jit(solution)/shard_map/while/body/eval_jaxpr/ppermute | solution.py:10
  394.3 7.8 %collective-permute-done = bf16[56,2304]{1,0:T(8,128)(2,1)S(1)} collective-permute-done((bf16[56,2304]{1,0:T(8,128)(2,1)S(1)}, bf16[56,2304]{1,0:T(8,128)(2,1)S(1)}, u32[]{:S(2)}, u32[]{:S(2)}) %collective-permute-start) | collective-permute-done | bytes 258080 | tf_op jit(solution)/shard_map/while/body/eval_jaxpr/ppermute | solution.py:10
  404.4 14.8 %collective-permute-start = (bf16[56,2304]{1,0:T(8,128)(2,1)S(1)}, bf16[56,2304]{1,0:T(8,128)(2,1)S(1)}, u32[]{:S(2)}, u32[]{:S(2)}) collective-permute-start(bf16[56,2304]{1,0:T(8,128)(2,1)S(1)} %get-tuple-element.68), channel_id=1, source_target_pairs={{1,0},{2,1},{3,2},{4,3},{5,4},{6,5},{7,6},{8,7},{9,8},{10,9},{11,1... | collective-permute-start | bytes 774152 | tf_op jit(solution)/shard_map/while/body/eval_jaxpr/ppermute | solution.py:10
  419.3 6.3 %collective-permute-done = bf16[56,2304]{1,0:T(8,128)(2,1)S(1)} collective-permute-done((bf16[56,2304]{1,0:T(8,128)(2,1)S(1)}, bf16[56,2304]{1,0:T(8,128)(2,1)S(1)}, u32[]{:S(2)}, u32[]{:S(2)}) %collective-permute-start) | collective-permute-done | bytes 258080 | tf_op jit(solution)/shard_map/while/body/eval_jaxpr/ppermute | solution.py:10
  426.0 26.9 %psum.7 = f32[56,128]{1,0:T(8,128)S(1)} all-reduce(f32[56,128]{1,0:T(8,128)S(1)} %get-tuple-element.27), channel_id=1, replica_groups=mesh['layer'=2,'row'=16,'col'=16] {'layer'}, use_global_device_ids=true, to_apply=%region_2.3 | all-reduce | flops 7168 | bytes 57344 | tf_op jit(solution)/shard_map/psum | solution.py:34
  (109 shorter events, 78.8 us)
Async XLA Ops:
  0.0 19.9 %collective-permute-start.2 = (bf16[56,2304]{1,0:T(8,128)(2,1)}, bf16[56,2304]{1,0:T(8,128)(2,1)S(1)}, u32[]{:S(2)}, u32[]{:S(2)}) collective-permute-start(bf16[56,2304]{1,0:T(8,128)(2,1)} %param.7), channel_id=1, source_target_pairs={{1,0},{2,1},{3,2},{4,3},{5,4},{6,5},{7,6},{8,7},{9,8},{10,9},{11,1... | collective-permute-start | bytes 774152 | tf_op jit(solution)/shard_map/ppermute | solution.py:10
  13.3 16.0 %collective-permute-start.6 = (bf16[2304,128]{1,0:T(8,128)(2,1)}, bf16[2304,128]{1,0:T(8,128)(2,1)S(1)}, u32[]{:S(2)}, u32[]{:S(2)}) collective-permute-start(bf16[2304,128]{1,0:T(8,128)(2,1)} %param.8), channel_id=1, source_target_pairs={{16,0},{32,16},{48,32},{64,48},{80,64},{96,80},{112,96},{128,112},... | collective-permute-start | bytes 1769480 | tf_op jit(solution)/shard_map/ppermute | solution.py:10
  29.3 16.1 %collective-permute-start.7 = (bf16[2304,128]{1,0:T(8,128)(2,1)S(1)}, bf16[2304,128]{1,0:T(8,128)(2,1)S(1)}, u32[]{:S(2)}, u32[]{:S(2)}) collective-permute-start(bf16[2304,128]{1,0:T(8,128)(2,1)S(1)} %broadcast_select_fusion), channel_id=1, source_target_pairs={{32,0},{48,16},{64,32},{80,48},{96,64},{112,80},{128,96},{144,112}... | collective-permute-start | bytes 1769480 | tf_op jit(solution)/shard_map/ppermute | solution.py:10
  45.5 30.2 %collective-permute-start.8 = (bf16[2304,128]{1,0:T(8,128)(2,1)S(1)}, bf16[2304,128]{1,0:T(8,128)(2,1)S(1)}, u32[]{:S(2)}, u32[]{:S(2)}) collective-permute-start(bf16[2304,128]{1,0:T(8,128)(2,1)S(1)} %broadcast_select_fusion.1), channel_id=1, source_target_pairs={{64,0},{80,16},{96,32},{112,48},{128,64},{144,80},{160,96},{176,11... | collective-permute-start | bytes 1769480 | tf_op jit(solution)/shard_map/ppermute | solution.py:10
  49.8 30.5 %collective-permute-start.5 = (bf16[56,2304]{1,0:T(8,128)(2,1)S(1)}, bf16[56,2304]{1,0:T(8,128)(2,1)S(1)}, u32[]{:S(2)}, u32[]{:S(2)}) collective-permute-start(bf16[56,2304]{1,0:T(8,128)(2,1)S(1)} %broadcast_select_fusion.6), channel_id=1, source_target_pairs={{8,0},{9,1},{10,2},{11,3},{12,4},{13,5},{14,6},{15,7},{0,8},{1,9},... | collective-permute-start | bytes 774152 | tf_op jit(solution)/shard_map/ppermute | solution.py:10
  75.8 33.6 %collective-permute-start.9 = (bf16[2304,128]{1,0:T(8,128)(2,1)S(1)}, bf16[2304,128]{1,0:T(8,128)(2,1)S(1)}, u32[]{:S(2)}, u32[]{:S(2)}) collective-permute-start(bf16[2304,128]{1,0:T(8,128)(2,1)S(1)} %broadcast_select_fusion.2), channel_id=1, source_target_pairs={{128,0},{144,16},{160,32},{176,48},{192,64},{208,80},{224,96},{240... | collective-permute-start | bytes 1769480 | tf_op jit(solution)/shard_map/ppermute | solution.py:10
  109.7 23.5 %collective-permute-start.1 = (bf16[2304,128]{1,0:T(8,128)(2,1)S(1)}, bf16[2304,128]{1,0:T(8,128)(2,1)S(1)}, u32[]{:S(2)}, u32[]{:S(2)}) collective-permute-start(bf16[2304,128]{1,0:T(8,128)(2,1)S(1)} %get-tuple-element.69), channel_id=1, source_target_pairs={{16,0},{32,16},{48,32},{64,48},{80,64},{96,80},{112,96},{128,112},... | collective-permute-start | bytes 1769480 | tf_op jit(solution)/shard_map/while/body/eval_jaxpr/ppermute | solution.py:10
  111.6 21.6 %collective-permute-start = (bf16[56,2304]{1,0:T(8,128)(2,1)S(1)}, bf16[56,2304]{1,0:T(8,128)(2,1)S(1)}, u32[]{:S(2)}, u32[]{:S(2)}) collective-permute-start(bf16[56,2304]{1,0:T(8,128)(2,1)S(1)} %get-tuple-element.68), channel_id=1, source_target_pairs={{1,0},{2,1},{3,2},{4,3},{5,4},{6,5},{7,6},{8,7},{9,8},{10,9},{11,1... | collective-permute-start | bytes 774152 | tf_op jit(solution)/shard_map/while/body/eval_jaxpr/ppermute | solution.py:10
  133.5 21.0 %collective-permute-start.1 = (bf16[2304,128]{1,0:T(8,128)(2,1)S(1)}, bf16[2304,128]{1,0:T(8,128)(2,1)S(1)}, u32[]{:S(2)}, u32[]{:S(2)}) collective-permute-start(bf16[2304,128]{1,0:T(8,128)(2,1)S(1)} %get-tuple-element.69), channel_id=1, source_target_pairs={{16,0},{32,16},{48,32},{64,48},{80,64},{96,80},{112,96},{128,112},... | collective-permute-start | bytes 1769480 | tf_op jit(solution)/shard_map/while/body/eval_jaxpr/ppermute | solution.py:10
  135.5 19.1 %collective-permute-start = (bf16[56,2304]{1,0:T(8,128)(2,1)S(1)}, bf16[56,2304]{1,0:T(8,128)(2,1)S(1)}, u32[]{:S(2)}, u32[]{:S(2)}) collective-permute-start(bf16[56,2304]{1,0:T(8,128)(2,1)S(1)} %get-tuple-element.68), channel_id=1, source_target_pairs={{1,0},{2,1},{3,2},{4,3},{5,4},{6,5},{7,6},{8,7},{9,8},{10,9},{11,1... | collective-permute-start | bytes 774152 | tf_op jit(solution)/shard_map/while/body/eval_jaxpr/ppermute | solution.py:10
  154.9 23.1 %collective-permute-start.1 = (bf16[2304,128]{1,0:T(8,128)(2,1)S(1)}, bf16[2304,128]{1,0:T(8,128)(2,1)S(1)}, u32[]{:S(2)}, u32[]{:S(2)}) collective-permute-start(bf16[2304,128]{1,0:T(8,128)(2,1)S(1)} %get-tuple-element.69), channel_id=1, source_target_pairs={{16,0},{32,16},{48,32},{64,48},{80,64},{96,80},{112,96},{128,112},... | collective-permute-start | bytes 1769480 | tf_op jit(solution)/shard_map/while/body/eval_jaxpr/ppermute | solution.py:10
  156.8 21.1 %collective-permute-start = (bf16[56,2304]{1,0:T(8,128)(2,1)S(1)}, bf16[56,2304]{1,0:T(8,128)(2,1)S(1)}, u32[]{:S(2)}, u32[]{:S(2)}) collective-permute-start(bf16[56,2304]{1,0:T(8,128)(2,1)S(1)} %get-tuple-element.68), channel_id=1, source_target_pairs={{1,0},{2,1},{3,2},{4,3},{5,4},{6,5},{7,6},{8,7},{9,8},{10,9},{11,1... | collective-permute-start | bytes 774152 | tf_op jit(solution)/shard_map/while/body/eval_jaxpr/ppermute | solution.py:10
  178.3 16.3 %collective-permute-start.1 = (bf16[2304,128]{1,0:T(8,128)(2,1)S(1)}, bf16[2304,128]{1,0:T(8,128)(2,1)S(1)}, u32[]{:S(2)}, u32[]{:S(2)}) collective-permute-start(bf16[2304,128]{1,0:T(8,128)(2,1)S(1)} %get-tuple-element.69), channel_id=1, source_target_pairs={{16,0},{32,16},{48,32},{64,48},{80,64},{96,80},{112,96},{128,112},... | collective-permute-start | bytes 1769480 | tf_op jit(solution)/shard_map/while/body/eval_jaxpr/ppermute | solution.py:10
  194.8 20.6 %collective-permute-start.1 = (bf16[2304,128]{1,0:T(8,128)(2,1)S(1)}, bf16[2304,128]{1,0:T(8,128)(2,1)S(1)}, u32[]{:S(2)}, u32[]{:S(2)}) collective-permute-start(bf16[2304,128]{1,0:T(8,128)(2,1)S(1)} %get-tuple-element.69), channel_id=1, source_target_pairs={{16,0},{32,16},{48,32},{64,48},{80,64},{96,80},{112,96},{128,112},... | collective-permute-start | bytes 1769480 | tf_op jit(solution)/shard_map/while/body/eval_jaxpr/ppermute | solution.py:10
  196.8 18.7 %collective-permute-start = (bf16[56,2304]{1,0:T(8,128)(2,1)S(1)}, bf16[56,2304]{1,0:T(8,128)(2,1)S(1)}, u32[]{:S(2)}, u32[]{:S(2)}) collective-permute-start(bf16[56,2304]{1,0:T(8,128)(2,1)S(1)} %get-tuple-element.68), channel_id=1, source_target_pairs={{1,0},{2,1},{3,2},{4,3},{5,4},{6,5},{7,6},{8,7},{9,8},{10,9},{11,1... | collective-permute-start | bytes 774152 | tf_op jit(solution)/shard_map/while/body/eval_jaxpr/ppermute | solution.py:10
  215.8 20.4 %collective-permute-start.1 = (bf16[2304,128]{1,0:T(8,128)(2,1)S(1)}, bf16[2304,128]{1,0:T(8,128)(2,1)S(1)}, u32[]{:S(2)}, u32[]{:S(2)}) collective-permute-start(bf16[2304,128]{1,0:T(8,128)(2,1)S(1)} %get-tuple-element.69), channel_id=1, source_target_pairs={{16,0},{32,16},{48,32},{64,48},{80,64},{96,80},{112,96},{128,112},... | collective-permute-start | bytes 1769480 | tf_op jit(solution)/shard_map/while/body/eval_jaxpr/ppermute | solution.py:10
  217.7 18.4 %collective-permute-start = (bf16[56,2304]{1,0:T(8,128)(2,1)S(1)}, bf16[56,2304]{1,0:T(8,128)(2,1)S(1)}, u32[]{:S(2)}, u32[]{:S(2)}) collective-permute-start(bf16[56,2304]{1,0:T(8,128)(2,1)S(1)} %get-tuple-element.68), channel_id=1, source_target_pairs={{1,0},{2,1},{3,2},{4,3},{5,4},{6,5},{7,6},{8,7},{9,8},{10,9},{11,1... | collective-permute-start | bytes 774152 | tf_op jit(solution)/shard_map/while/body/eval_jaxpr/ppermute | solution.py:10
  236.5 20.6 %collective-permute-start.1 = (bf16[2304,128]{1,0:T(8,128)(2,1)S(1)}, bf16[2304,128]{1,0:T(8,128)(2,1)S(1)}, u32[]{:S(2)}, u32[]{:S(2)}) collective-permute-start(bf16[2304,128]{1,0:T(8,128)(2,1)S(1)} %get-tuple-element.69), channel_id=1, source_target_pairs={{16,0},{32,16},{48,32},{64,48},{80,64},{96,80},{112,96},{128,112},... | collective-permute-start | bytes 1769480 | tf_op jit(solution)/shard_map/while/body/eval_jaxpr/ppermute | solution.py:10
  238.4 18.6 %collective-permute-start = (bf16[56,2304]{1,0:T(8,128)(2,1)S(1)}, bf16[56,2304]{1,0:T(8,128)(2,1)S(1)}, u32[]{:S(2)}, u32[]{:S(2)}) collective-permute-start(bf16[56,2304]{1,0:T(8,128)(2,1)S(1)} %get-tuple-element.68), channel_id=1, source_target_pairs={{1,0},{2,1},{3,2},{4,3},{5,4},{6,5},{7,6},{8,7},{9,8},{10,9},{11,1... | collective-permute-start | bytes 774152 | tf_op jit(solution)/shard_map/while/body/eval_jaxpr/ppermute | solution.py:10
  257.3 21.0 %collective-permute-start.1 = (bf16[2304,128]{1,0:T(8,128)(2,1)S(1)}, bf16[2304,128]{1,0:T(8,128)(2,1)S(1)}, u32[]{:S(2)}, u32[]{:S(2)}) collective-permute-start(bf16[2304,128]{1,0:T(8,128)(2,1)S(1)} %get-tuple-element.69), channel_id=1, source_target_pairs={{16,0},{32,16},{48,32},{64,48},{80,64},{96,80},{112,96},{128,112},... | collective-permute-start | bytes 1769480 | tf_op jit(solution)/shard_map/while/body/eval_jaxpr/ppermute | solution.py:10
  259.3 19.0 %collective-permute-start = (bf16[56,2304]{1,0:T(8,128)(2,1)S(1)}, bf16[56,2304]{1,0:T(8,128)(2,1)S(1)}, u32[]{:S(2)}, u32[]{:S(2)}) collective-permute-start(bf16[56,2304]{1,0:T(8,128)(2,1)S(1)} %get-tuple-element.68), channel_id=1, source_target_pairs={{1,0},{2,1},{3,2},{4,3},{5,4},{6,5},{7,6},{8,7},{9,8},{10,9},{11,1... | collective-permute-start | bytes 774152 | tf_op jit(solution)/shard_map/while/body/eval_jaxpr/ppermute | solution.py:10
  278.7 18.2 %collective-permute-start.1 = (bf16[2304,128]{1,0:T(8,128)(2,1)S(1)}, bf16[2304,128]{1,0:T(8,128)(2,1)S(1)}, u32[]{:S(2)}, u32[]{:S(2)}) collective-permute-start(bf16[2304,128]{1,0:T(8,128)(2,1)S(1)} %get-tuple-element.69), channel_id=1, source_target_pairs={{16,0},{32,16},{48,32},{64,48},{80,64},{96,80},{112,96},{128,112},... | collective-permute-start | bytes 1769480 | tf_op jit(solution)/shard_map/while/body/eval_jaxpr/ppermute | solution.py:10
  280.6 16.2 %collective-permute-start = (bf16[56,2304]{1,0:T(8,128)(2,1)S(1)}, bf16[56,2304]{1,0:T(8,128)(2,1)S(1)}, u32[]{:S(2)}, u32[]{:S(2)}) collective-permute-start(bf16[56,2304]{1,0:T(8,128)(2,1)S(1)} %get-tuple-element.68), channel_id=1, source_target_pairs={{1,0},{2,1},{3,2},{4,3},{5,4},{6,5},{7,6},{8,7},{9,8},{10,9},{11,1... | collective-permute-start | bytes 774152 | tf_op jit(solution)/shard_map/while/body/eval_jaxpr/ppermute | solution.py:10
  312.3 15.7 %collective-permute-start.1 = (bf16[2304,128]{1,0:T(8,128)(2,1)S(1)}, bf16[2304,128]{1,0:T(8,128)(2,1)S(1)}, u32[]{:S(2)}, u32[]{:S(2)}) collective-permute-start(bf16[2304,128]{1,0:T(8,128)(2,1)S(1)} %get-tuple-element.69), channel_id=1, source_target_pairs={{16,0},{32,16},{48,32},{64,48},{80,64},{96,80},{112,96},{128,112},... | collective-permute-start | bytes 1769480 | tf_op jit(solution)/shard_map/while/body/eval_jaxpr/ppermute | solution.py:10
  328.4 22.6 %collective-permute-start.1 = (bf16[2304,128]{1,0:T(8,128)(2,1)S(1)}, bf16[2304,128]{1,0:T(8,128)(2,1)S(1)}, u32[]{:S(2)}, u32[]{:S(2)}) collective-permute-start(bf16[2304,128]{1,0:T(8,128)(2,1)S(1)} %get-tuple-element.69), channel_id=1, source_target_pairs={{16,0},{32,16},{48,32},{64,48},{80,64},{96,80},{112,96},{128,112},... | collective-permute-start | bytes 1769480 | tf_op jit(solution)/shard_map/while/body/eval_jaxpr/ppermute | solution.py:10
  330.9 20.1 %collective-permute-start = (bf16[56,2304]{1,0:T(8,128)(2,1)S(1)}, bf16[56,2304]{1,0:T(8,128)(2,1)S(1)}, u32[]{:S(2)}, u32[]{:S(2)}) collective-permute-start(bf16[56,2304]{1,0:T(8,128)(2,1)S(1)} %get-tuple-element.68), channel_id=1, source_target_pairs={{1,0},{2,1},{3,2},{4,3},{5,4},{6,5},{7,6},{8,7},{9,8},{10,9},{11,1... | collective-permute-start | bytes 774152 | tf_op jit(solution)/shard_map/while/body/eval_jaxpr/ppermute | solution.py:10
  351.3 27.1 %collective-permute-start.1 = (bf16[2304,128]{1,0:T(8,128)(2,1)S(1)}, bf16[2304,128]{1,0:T(8,128)(2,1)S(1)}, u32[]{:S(2)}, u32[]{:S(2)}) collective-permute-start(bf16[2304,128]{1,0:T(8,128)(2,1)S(1)} %get-tuple-element.69), channel_id=1, source_target_pairs={{16,0},{32,16},{48,32},{64,48},{80,64},{96,80},{112,96},{128,112},... | collective-permute-start | bytes 1769480 | tf_op jit(solution)/shard_map/while/body/eval_jaxpr/ppermute | solution.py:10
  353.3 25.2 %collective-permute-start = (bf16[56,2304]{1,0:T(8,128)(2,1)S(1)}, bf16[56,2304]{1,0:T(8,128)(2,1)S(1)}, u32[]{:S(2)}, u32[]{:S(2)}) collective-permute-start(bf16[56,2304]{1,0:T(8,128)(2,1)S(1)} %get-tuple-element.68), channel_id=1, source_target_pairs={{1,0},{2,1},{3,2},{4,3},{5,4},{6,5},{7,6},{8,7},{9,8},{10,9},{11,1... | collective-permute-start | bytes 774152 | tf_op jit(solution)/shard_map/while/body/eval_jaxpr/ppermute | solution.py:10
  378.8 23.4 %collective-permute-start.1 = (bf16[2304,128]{1,0:T(8,128)(2,1)S(1)}, bf16[2304,128]{1,0:T(8,128)(2,1)S(1)}, u32[]{:S(2)}, u32[]{:S(2)}) collective-permute-start(bf16[2304,128]{1,0:T(8,128)(2,1)S(1)} %get-tuple-element.69), channel_id=1, source_target_pairs={{16,0},{32,16},{48,32},{64,48},{80,64},{96,80},{112,96},{128,112},... | collective-permute-start | bytes 1769480 | tf_op jit(solution)/shard_map/while/body/eval_jaxpr/ppermute | solution.py:10
  380.7 21.4 %collective-permute-start = (bf16[56,2304]{1,0:T(8,128)(2,1)S(1)}, bf16[56,2304]{1,0:T(8,128)(2,1)S(1)}, u32[]{:S(2)}, u32[]{:S(2)}) collective-permute-start(bf16[56,2304]{1,0:T(8,128)(2,1)S(1)} %get-tuple-element.68), channel_id=1, source_target_pairs={{1,0},{2,1},{3,2},{4,3},{5,4},{6,5},{7,6},{8,7},{9,8},{10,9},{11,1... | collective-permute-start | bytes 774152 | tf_op jit(solution)/shard_map/while/body/eval_jaxpr/ppermute | solution.py:10
  402.5 23.1 %collective-permute-start.1 = (bf16[2304,128]{1,0:T(8,128)(2,1)S(1)}, bf16[2304,128]{1,0:T(8,128)(2,1)S(1)}, u32[]{:S(2)}, u32[]{:S(2)}) collective-permute-start(bf16[2304,128]{1,0:T(8,128)(2,1)S(1)} %get-tuple-element.69), channel_id=1, source_target_pairs={{16,0},{32,16},{48,32},{64,48},{80,64},{96,80},{112,96},{128,112},... | collective-permute-start | bytes 1769480 | tf_op jit(solution)/shard_map/while/body/eval_jaxpr/ppermute | solution.py:10
  404.4 21.2 %collective-permute-start = (bf16[56,2304]{1,0:T(8,128)(2,1)S(1)}, bf16[56,2304]{1,0:T(8,128)(2,1)S(1)}, u32[]{:S(2)}, u32[]{:S(2)}) collective-permute-start(bf16[56,2304]{1,0:T(8,128)(2,1)S(1)} %get-tuple-element.68), channel_id=1, source_target_pairs={{1,0},{2,1},{3,2},{4,3},{5,4},{6,5},{7,6},{8,7},{9,8},{10,9},{11,1... | collective-permute-start | bytes 774152 | tf_op jit(solution)/shard_map/while/body/eval_jaxpr/ppermute | solution.py:10
  (10 other events, 194.6 us)
where the time goes:
time: 455 us; the launch traced here: 454 us
  starting transfers between devices  264 us (58%)
  waiting for transfers between devices  155 us (34%)
  blocking collectives  26.9 us (6%)
    ppermute x38, starting transfers between devices, passed_along(): return lax.ppermute(block, axis, route)  264 us
    ppermute x38, waiting for transfers between devices, passed_along(): return lax.ppermute(block, axis, route)  155 us
    psum x1, blocking collectives, body(): ladder = lax.psum(partial_ladder, 'layer')  26.9 us
  transfers between devices with their start and end apart: 38, of which 22 were waited for; matrix products, arithmetic and copies ran while one was open for 0% of the time, Pallas kernels for 0%

commit v1 on v0

v1 whole, which is shorter than its diff:
```python
import jax
import jax.numpy as jnp
from jax import lax
from jax.experimental import pallas as pl
from jax.experimental.pallas import tpu as pltpu
from jax.sharding import Mesh
from jax.sharding import PartitionSpec as P

PARTS = {"l": 2, "yh": 4, "yl": 2, "xl": 2, "xh": 2, "zh": 4, "zl": 2}
FAR = ("yh", "zh")
PIECES = 16
ROWS = 56
LANES = 128
MAIN = PIECES * LANES
REST = 16
A_ROWS = 64
B_ROWS = LANES + REST
VMEM = 40 * 1024 * 1024


def pack_kernel(a_ref, b_ref, out_ref):
    lane_group = lax.broadcasted_iota(jnp.int32, (8, LANES), 1) // REST
    tail = a_ref[:, MAIN:].astype(jnp.float32)
    for s in range(PIECES):
        main = a_ref[:, s * LANES : (s + 1) * LANES].astype(jnp.float32)
        half, place = divmod(s, 8)
        rest = jnp.zeros((8, LANES), jnp.float32)
        for g in range(ROWS // 8):
            tile = tail[8 * g : 8 * g + 8, half * LANES : (half + 1) * LANES]
            shift = REST * (g - place) % LANES
            moved = pltpu.roll(tile, shift, 1) if shift else tile
            rest = jnp.where(lane_group == g, moved, rest)
        out_ref[s, 0:A_ROWS, :] = jnp.concatenate([main, rest], axis=0).astype(jnp.bfloat16)
        out_ref[s, A_ROWS : A_ROWS + LANES, :] = b_ref[s * LANES : (s + 1) * LANES, :]
        out_ref[s, A_ROWS + LANES :, :] = b_ref[MAIN + s * REST : MAIN + (s + 1) * REST, :]


def pack(a, b):
    return pl.pallas_call(
        pack_kernel,
        out_shape=jax.ShapeDtypeStruct((PIECES, A_ROWS + B_ROWS, LANES), jnp.bfloat16),
        in_specs=[pl.BlockSpec(memory_space=pltpu.VMEM)] * 2,
        out_specs=pl.BlockSpec(memory_space=pltpu.VMEM),
        compiler_params=pltpu.CompilerParams(vmem_limit_bytes=VMEM),
    )(a, b)


def multiply_kernel(place_ref, *refs):
    a_refs, b_refs, (out_ref, left, right, spread) = refs[:4], refs[4:8], refs[8:]
    my_yl, my_xl, my_xh, my_zl = (place_ref[i] for i in range(4))
    lane_group = lax.broadcasted_iota(jnp.int32, (4 * 8, LANES), 1) // REST
    tails = []
    for t in range(PIECES):
        dxh, dzl, b2, dyl = t >> 3, (t >> 2) & 1, (t >> 1) & 1, t & 1
        a_ref = a_refs[2 * dxh + dzl]
        zh = 2 * b2 + (my_yl ^ dyl)
        tail = []
        for yh in range(4):
            left[A_ROWS * yh : A_ROWS * (yh + 1), t * LANES : (t + 1) * LANES] = a_ref[4 * yh + zh]
            tail.append(a_ref[4 * yh + zh, A_ROWS - 16 :, :].astype(jnp.float32)[8:])
        tails.append(jnp.concatenate(tail, axis=0))
    spread[...] = jnp.zeros_like(spread)
    for half in range(2):
        for g in range(ROWS // 8):
            rest = jnp.zeros((4 * 8, LANES), jnp.float32)
            for place in range(8):
                shift = REST * (place - g) % LANES
                tile = tails[8 * half + place]
                moved = pltpu.roll(tile, shift, 1) if shift else tile
                rest = jnp.where(lane_group == place, moved, rest)
            for yh in range(4):
                spread[A_ROWS * yh + 8 * g : A_ROWS * yh + 8 * g + 8, half * LANES : (half + 1) * LANES] = rest[8 * yh : 8 * yh + 8]
    left[:, MAIN:] = spread[...].astype(jnp.bfloat16)

    def lay_right(same):
        for t in range(PIECES):
            dxh, dzl, b2, dyl = t >> 3, (t >> 2) & 1, (t >> 1) & 1, t & 1
            b_ref = b_refs[2 * dyl + (dzl if same else 1 - dzl)]
            yh = 2 * (my_xh ^ dxh) + b2
            for zh in range(4):
                columns = slice(zh * LANES, (zh + 1) * LANES)
                right[t * LANES : (t + 1) * LANES, columns] = b_ref[4 * yh + zh, 0:LANES, :]
                right[MAIN + t * REST : MAIN + (t + 1) * REST, columns] = b_ref[4 * yh + zh, LANES:, :]

    pl.when(my_zl == my_xl)(lambda: lay_right(True))
    pl.when(my_zl != my_xl)(lambda: lay_right(False))
    total = jnp.dot(left[...], right[...], preferred_element_type=jnp.float32)
    for yh in range(4):
        for zh in range(4):
            out_ref[4 * yh + zh] = total[A_ROWS * yh : A_ROWS * yh + ROWS, zh * LANES : (zh + 1) * LANES]


def multiply(place, a_slots, b_slots):
    depth = PIECES * (LANES + REST)
    return pl.pallas_call(
        multiply_kernel,
        out_shape=jax.ShapeDtypeStruct((PIECES, ROWS, LANES), jnp.float32),
        in_specs=[pl.BlockSpec(memory_space=pltpu.SMEM)] + [pl.BlockSpec(memory_space=pltpu.VMEM)] * 8,
        out_specs=pl.BlockSpec(memory_space=pltpu.VMEM),
        scratch_shapes=[
            pltpu.VMEM((4 * A_ROWS, depth), jnp.bfloat16),
            pltpu.VMEM((depth, 4 * LANES), jnp.bfloat16),
            pltpu.VMEM((4 * A_ROWS, 2 * LANES), jnp.float32),
        ],
        compiler_params=pltpu.CompilerParams(vmem_limit_bytes=VMEM),
    )(place, *a_slots, *b_slots)


def neighbours(block, axes):
    return [block] + [lax.ppermute(block, axes, [(i, i ^ d) for i in range(4)]) for d in (1, 2, 3)]


def body(amplitudes, integrals, other_terms, occ_energy, virt_energy):
    pieces = lax.all_to_all(pack(amplitudes, integrals), FAR, 0, 0, tiled=True)
    b_slots = neighbours(pieces[:, A_ROWS:], ("yl", "xl"))
    a_slots = neighbours(pieces[:, :A_ROWS], ("xh", "zl"))
    place = jnp.stack([lax.axis_index(n) for n in ("yl", "xl", "xh", "zl")]).astype(jnp.int32)
    partial = multiply(place, a_slots, b_slots)
    partial = lax.all_to_all(partial, FAR, 0, 0, tiled=True)
    ladder = lax.psum(jnp.sum(partial, axis=0), "l")
    denominator = occ_energy[:, None] - virt_energy[None, :]
    return (ladder + other_terms) / denominator


def solution(mesh):
    fine = Mesh(mesh.devices.reshape(tuple(PARTS.values())), tuple(PARTS))
    row, col = ("yh", "yl", "xl"), ("xh", "zh", "zl")
    in_specs = (P(row, ("l",) + col), P(("l",) + row, col), P(row, col), P(row), P(col))
    return jax.shard_map(body, mesh=fine, in_specs=in_specs, out_specs=P(row, col), check_vma=False)
```

time: 455 us -> 125 us (0.27)
  the two profiles are of different devices: /device:TPU:25 before, /device:TPU:1 now
where the time goes in v1:
time: 125 us
  blocking collectives  75.3 us (60%)
  waiting for transfers between devices  25.5 us (20%)
  starting transfers between devices  18.5 us (15%)
  Pallas kernels  2.25 us (2%)
  local copies, waits for them, and re-layouts  2.09 us (2%)
    all_to_all x1, blocking collectives, body(): pieces = lax.all_to_all(pack(amplitudes, integrals), FAR, 0, 0, tiled=True)  44.2 us
    all_to_all x1, blocking collectives, body(): partial = lax.all_to_all(partial, FAR, 0, 0, tiled=True)  27 us
    ppermute x6, waiting for transfers between devices, neighbours(): lax.ppermute(block, axes, [(i, i ^ d) for i in range(4)])  25.5 us
    ppermute x6, starting transfers between devices, neighbours(): lax.ppermute(block, axes, [(i, i ^ d) for i in range(4)])  18.5 us
    psum x1, blocking collectives, body(): ladder = lax.psum(jnp.sum(partial, axis=0), 'l')  4.15 us
  transfers between devices with their start and end apart: 6, of which 2 were waited for; matrix products, arithmetic and copies ran while one was open for 0% of the time, Pallas kernels for 0%

profile of v1, /device:TPU:1, one launch (start us, length us, event | category | flops | bytes accessed | tf_op | source)
XLA Modules:
  0.0 124.6 jit_solution(444334271662703729)
XLA Ops:
  0.0 0.0 copy-start
  0.0 1.1 copy-done
  1.1 0.0 copy-start.1
  1.1 0.9 copy-done.1
  2.0 0.2 shard_map.55
  2.2 44.2 %all_to_all.10 = bf16[16,208,128]{2,1,0:T(8,128)(2,1)S(1)} all-to-all(bf16[16,208,128]{2,1,0:T(8,128)(2,1)S(1)} %shard_map.55), channel_id=1, replica_groups=mesh['l'=2,'yh'=4,'yl'=2,'xl'=2,'xh'=2,'zh'=4,'zl'=2] {'yh','zh'}, dimensions={0} | all-to-all | bytes 1703936 | tf_op jit(solution)/shard_map/all_to_all | solution.py:114
  46.4 1.9 %collective-permute-start.5 = (bf16[16,144,128]{2,1,0:T(8,128)(2,1)S(1)}, bf16[16,144,128]{2,1,0:T(8,128)(2,1)S(1)}, u32[]{:S(2)}, u32[]{:S(2)}) collective-permute-start(bf16[16,144,128]{2,1,0:T(8,128)(2,1)S(1)} %slice.9.refs_4_), channel_id=1, source_target_pairs={{0,48},{16,32},{32,16},{48,0},{1,49},{17,33},{33,17},{49,1},{2,50}... | collective-permute-start | bytes 1769480 | tf_op jit(solution)/shard_map/ppermute | solution.py:110
  48.3 4.3 %collective-permute-start.4 = (bf16[16,144,128]{2,1,0:T(8,128)(2,1)S(1)}, bf16[16,144,128]{2,1,0:T(8,128)(2,1)S(1)}, u32[]{:S(2)}, u32[]{:S(2)}) collective-permute-start(bf16[16,144,128]{2,1,0:T(8,128)(2,1)S(1)} %slice.9.refs_4_), channel_id=1, source_target_pairs={{0,32},{16,48},{32,0},{48,16},{1,33},{17,49},{33,1},{49,17},{2,34}... | collective-permute-start | bytes 1769480 | tf_op jit(solution)/shard_map/ppermute | solution.py:110
  52.6 2.2 %collective-permute-start.3 = (bf16[16,144,128]{2,1,0:T(8,128)(2,1)S(1)}, bf16[16,144,128]{2,1,0:T(8,128)(2,1)S(1)}, u32[]{:S(2)}, u32[]{:S(2)}) collective-permute-start(bf16[16,144,128]{2,1,0:T(8,128)(2,1)S(1)} %slice.9.refs_4_), channel_id=1, source_target_pairs={{0,16},{16,0},{32,48},{48,32},{1,17},{17,1},{33,49},{49,33},{2,18}... | collective-permute-start | bytes 1769480 | tf_op jit(solution)/shard_map/ppermute | solution.py:110
  54.8 5.0 %collective-permute-start.2 = (bf16[16,64,128]{2,1,0:T(8,128)(2,1)S(1)}, bf16[16,64,128]{2,1,0:T(8,128)(2,1)S(1)}, u32[]{:S(2)}, u32[]{:S(2)}) collective-permute-start(bf16[16,64,128]{2,1,0:T(8,128)(2,1)S(1)} %slice.8.refs_0_), channel_id=1, source_target_pairs={{0,9},{1,8},{8,1},{9,0},{2,11},{3,10},{10,3},{11,2},{4,13},{5,12},... | collective-permute-start | bytes 786440 | tf_op jit(solution)/shard_map/ppermute | solution.py:110
  59.8 2.1 %collective-permute-start.1 = (bf16[16,64,128]{2,1,0:T(8,128)(2,1)S(1)}, bf16[16,64,128]{2,1,0:T(8,128)(2,1)S(1)}, u32[]{:S(2)}, u32[]{:S(2)}) collective-permute-start(bf16[16,64,128]{2,1,0:T(8,128)(2,1)S(1)} %slice.8.refs_0_), channel_id=1, source_target_pairs={{0,8},{1,9},{8,0},{9,1},{2,10},{3,11},{10,2},{11,3},{4,12},{5,13},... | collective-permute-start | bytes 786440 | tf_op jit(solution)/shard_map/ppermute | solution.py:110
  62.0 5.8 %collective-permute-done.2.refs_3_ = bf16[16,64,128]{2,1,0:T(8,128)(2,1)S(1)} collective-permute-done((bf16[16,64,128]{2,1,0:T(8,128)(2,1)S(1)}, bf16[16,64,128]{2,1,0:T(8,128)(2,1)S(1)}, u32[]{:S(2)}, u32[]{:S(2)}) %collective-permute-start.2) | collective-permute-done | bytes 262176 | tf_op jit(solution)/shard_map/ppermute | solution.py:110
  67.8 3.0 %collective-permute-start = (bf16[16,64,128]{2,1,0:T(8,128)(2,1)S(1)}, bf16[16,64,128]{2,1,0:T(8,128)(2,1)S(1)}, u32[]{:S(2)}, u32[]{:S(2)}) collective-permute-start(bf16[16,64,128]{2,1,0:T(8,128)(2,1)S(1)} %slice.8.refs_0_), channel_id=1, source_target_pairs={{0,1},{1,0},{8,9},{9,8},{2,3},{3,2},{10,11},{11,10},{4,5},{5,4},{1... | collective-permute-start | bytes 786440 | tf_op jit(solution)/shard_map/ppermute | solution.py:110
  70.8 0.1 pad_add_fusion.place_ref
  70.9 19.7 %collective-permute-done.1.refs_2_ = bf16[16,64,128]{2,1,0:T(8,128)(2,1)S(1)} collective-permute-done((bf16[16,64,128]{2,1,0:T(8,128)(2,1)S(1)}, bf16[16,64,128]{2,1,0:T(8,128)(2,1)S(1)}, u32[]{:S(2)}, u32[]{:S(2)}) %collective-permute-start.1) | collective-permute-done | bytes 262176 | tf_op jit(solution)/shard_map/ppermute | solution.py:110
  90.5 0.0 collective-permute-done.refs_1_
  90.5 0.0 collective-permute-done.5.refs_7_
  90.5 0.0 collective-permute-done.4.refs_6_
  90.5 0.0 collective-permute-done.3.refs_5_
  90.5 2.1 %shard_map.56 = f32[16,56,128]{2,1,0:T(8,128)S(1)} custom-call(s32[4]{0:T(128)S(1)} %pad_add_fusion.place_ref, bf16[16,64,128]{2,1,0:T(8,128)(2,1)S(1)} %slice.8.refs_0_, bf16[16,64,128]{2,1,0:T(8,128)(2,1)S(1)} %collective-permute-done.refs_1_, bf16[16,64,128]{2,1,0:T(8,128)(2,1)S(1)} %collective-permute-done.1.refs_2_, ...), custom_call_target="tpu_custom_call" | custom-call | tf_op jit(solution)/shard_map/pallas_call | solution.py:95
  92.6 27.0 %all_to_all.11 = f32[16,56,128]{2,1,0:T(8,128)S(1)} all-to-all(f32[16,56,128]{2,1,0:T(8,128)S(1)} %shard_map.56), channel_id=1, replica_groups=mesh['l'=2,'yh'=4,'yl'=2,'xl'=2,'xh'=2,'zh'=4,'zl'=2] {'yh','zh'}, dimensions={0} | all-to-all | bytes 917504 | tf_op jit(solution)/shard_map/all_to_all | solution.py:119
  119.6 0.0 copy-start.2
  119.7 0.0 copy-start.3
  119.7 0.0 copy-start.4
  119.7 4.1 %psum.7 = f32[56,128]{1,0:T(8,128)S(1)} all-reduce(f32[56,128]{1,0:T(8,128)S(1)} %reduce_sum.9), channel_id=1, replica_groups=mesh['l'=2,'yh'=4,'yl'=2,'xl'=2,'xh'=2,'zh'=4,'zl'=2] {'l'}, use_global_device_ids=true, to_apply=%region_1.0 | all-reduce | flops 7168 | bytes 57344 | tf_op jit(solution)/shard_map/psum | solution.py:120
  123.8 0.0 copy-done.2
  123.8 0.0 copy-done.3
  123.9 0.0 copy-done.4
  123.9 0.7 subtract_divide_fusion
  (3 shorter events, 0.1 us)
Async XLA Ops:
  0.0 1.1 copy-start
  1.1 0.9 copy-start.1
  46.4 44.1 %collective-permute-start.5 = (bf16[16,144,128]{2,1,0:T(8,128)(2,1)S(1)}, bf16[16,144,128]{2,1,0:T(8,128)(2,1)S(1)}, u32[]{:S(2)}, u32[]{:S(2)}) collective-permute-start(bf16[16,144,128]{2,1,0:T(8,128)(2,1)S(1)} %slice.9.refs_4_), channel_id=1, source_target_pairs={{0,48},{16,32},{32,16},{48,0},{1,49},{17,33},{33,17},{49,1},{2,50}... | collective-permute-start | bytes 1769480 | tf_op jit(solution)/shard_map/ppermute | solution.py:110
  48.3 42.2 %collective-permute-start.4 = (bf16[16,144,128]{2,1,0:T(8,128)(2,1)S(1)}, bf16[16,144,128]{2,1,0:T(8,128)(2,1)S(1)}, u32[]{:S(2)}, u32[]{:S(2)}) collective-permute-start(bf16[16,144,128]{2,1,0:T(8,128)(2,1)S(1)} %slice.9.refs_4_), channel_id=1, source_target_pairs={{0,32},{16,48},{32,0},{48,16},{1,33},{17,49},{33,1},{49,17},{2,34}... | collective-permute-start | bytes 1769480 | tf_op jit(solution)/shard_map/ppermute | solution.py:110
  52.6 37.9 %collective-permute-start.3 = (bf16[16,144,128]{2,1,0:T(8,128)(2,1)S(1)}, bf16[16,144,128]{2,1,0:T(8,128)(2,1)S(1)}, u32[]{:S(2)}, u32[]{:S(2)}) collective-permute-start(bf16[16,144,128]{2,1,0:T(8,128)(2,1)S(1)} %slice.9.refs_4_), channel_id=1, source_target_pairs={{0,16},{16,0},{32,48},{48,32},{1,17},{17,1},{33,49},{49,33},{2,18}... | collective-permute-start | bytes 1769480 | tf_op jit(solution)/shard_map/ppermute | solution.py:110
  54.8 12.9 %collective-permute-start.2 = (bf16[16,64,128]{2,1,0:T(8,128)(2,1)S(1)}, bf16[16,64,128]{2,1,0:T(8,128)(2,1)S(1)}, u32[]{:S(2)}, u32[]{:S(2)}) collective-permute-start(bf16[16,64,128]{2,1,0:T(8,128)(2,1)S(1)} %slice.8.refs_0_), channel_id=1, source_target_pairs={{0,9},{1,8},{8,1},{9,0},{2,11},{3,10},{10,3},{11,2},{4,13},{5,12},... | collective-permute-start | bytes 786440 | tf_op jit(solution)/shard_map/ppermute | solution.py:110
  59.8 30.7 %collective-permute-start.1 = (bf16[16,64,128]{2,1,0:T(8,128)(2,1)S(1)}, bf16[16,64,128]{2,1,0:T(8,128)(2,1)S(1)}, u32[]{:S(2)}, u32[]{:S(2)}) collective-permute-start(bf16[16,64,128]{2,1,0:T(8,128)(2,1)S(1)} %slice.8.refs_0_), channel_id=1, source_target_pairs={{0,8},{1,9},{8,0},{9,1},{2,10},{3,11},{10,2},{11,3},{4,12},{5,13},... | collective-permute-start | bytes 786440 | tf_op jit(solution)/shard_map/ppermute | solution.py:110
  67.8 22.8 %collective-permute-start = (bf16[16,64,128]{2,1,0:T(8,128)(2,1)S(1)}, bf16[16,64,128]{2,1,0:T(8,128)(2,1)S(1)}, u32[]{:S(2)}, u32[]{:S(2)}) collective-permute-start(bf16[16,64,128]{2,1,0:T(8,128)(2,1)S(1)} %slice.8.refs_0_), channel_id=1, source_target_pairs={{0,1},{1,0},{8,9},{9,8},{2,3},{3,2},{10,11},{11,10},{4,5},{5,4},{1... | collective-permute-start | bytes 786440 | tf_op jit(solution)/shard_map/ppermute | solution.py:110
  119.6 4.2 %copy-start.2 = (f32[56,128]{1,0:T(8,128)S(1)}, f32[56,128]{1,0:T(8,128)}, u32[]{:S(2)}) copy-start(f32[56,128]{1,0:T(8,128)} %param.7) | copy-start | bytes 86020
  119.7 4.2 %copy-start.3 = (f32[128]{0:T(128)S(1)}, f32[128]{0:T(128)}, u32[]{:S(2)}) copy-start(f32[128]{0:T(128)} %param.9) | copy-start | bytes 1540
  119.7 4.2 %copy-start.4 = (f32[56]{0:T(128)S(1)}, f32[56]{0:T(128)}, u32[]{:S(2)}) copy-start(f32[56]{0:T(128)} %param.8) | copy-start | bytes 676

commit v2 on v1

v2 whole, which is shorter than its diff:
```python
import jax
import jax.numpy as jnp
from jax import lax
from jax.experimental import pallas as pl
from jax.experimental.pallas import tpu as pltpu
from jax.sharding import Mesh
from jax.sharding import PartitionSpec as P

PARTS = {"l": 2, "yh": 4, "yl": 2, "xl": 2, "xh": 2, "zh": 4, "zl": 2}
NEAR = ("yl", "xl", "xh", "zl")
PIECES = 16
ROWS = 56
LANES = 128
MAIN = PIECES * LANES
REST = 16
A_ROWS = 64
B_ROWS = LANES + REST
VMEM = 40 * 1024 * 1024


def pack_kernel(a_ref, b_ref, out_ref):
    lane_group = lax.broadcasted_iota(jnp.int32, (8, LANES), 1) // REST
    tail = a_ref[:, MAIN:].astype(jnp.float32)
    for s in range(PIECES):
        main = a_ref[:, s * LANES : (s + 1) * LANES].astype(jnp.float32)
        half, place = divmod(s, 8)
        rest = jnp.zeros((8, LANES), jnp.float32)
        for g in range(ROWS // 8):
            tile = tail[8 * g : 8 * g + 8, half * LANES : (half + 1) * LANES]
            shift = REST * (g - place) % LANES
            moved = pltpu.roll(tile, shift, 1) if shift else tile
            rest = jnp.where(lane_group == g, moved, rest)
        out_ref[s, 0:A_ROWS, :] = jnp.concatenate([main, rest], axis=0).astype(jnp.bfloat16)
        out_ref[s, A_ROWS : A_ROWS + LANES, :] = b_ref[s * LANES : (s + 1) * LANES, :]
        out_ref[s, A_ROWS + LANES :, :] = b_ref[MAIN + s * REST : MAIN + (s + 1) * REST, :]


def pack(a, b):
    return pl.pallas_call(
        pack_kernel,
        out_shape=jax.ShapeDtypeStruct((PIECES, A_ROWS + B_ROWS, LANES), jnp.bfloat16),
        in_specs=[pl.BlockSpec(memory_space=pltpu.VMEM)] * 2,
        out_specs=pl.BlockSpec(memory_space=pltpu.VMEM),
        compiler_params=pltpu.CompilerParams(vmem_limit_bytes=VMEM),
    )(a, b)


def multiply_kernel(my_zh_ref, *refs):
    a_refs, (b_ref, out_ref, left, right, spread) = refs[:4], refs[4:]
    my_zh = my_zh_ref[0]
    lane_group = lax.broadcasted_iota(jnp.int32, (4 * 8, LANES), 1) // REST
    tails = []
    for t in range(PIECES):
        flip, b3, b0 = t >> 2, (t >> 1) & 1, t & 1
        zh = my_zh ^ flip
        b2, b1 = zh >> 1, zh & 1
        tail = []
        for r in range(4):
            piece = 4 * r + 2 * b3 + b0
            left[A_ROWS * r : A_ROWS * (r + 1), t * LANES : (t + 1) * LANES] = a_refs[flip][piece]
            tail.append(a_refs[flip][piece, A_ROWS - 16 :, :].astype(jnp.float32)[8:])
        tails.append(jnp.concatenate(tail, axis=0))
        for c in range(4):
            columns = slice(c * LANES, (c + 1) * LANES)
            piece = 4 * (2 * b1 + b0) + c
            right[t * LANES : (t + 1) * LANES, columns] = b_ref[2 * b3 + b2, piece, 0:LANES, :]
            right[MAIN + t * REST : MAIN + (t + 1) * REST, columns] = b_ref[2 * b3 + b2, piece, LANES:, :]
    spread[...] = jnp.zeros_like(spread)
    for half in range(2):
        for g in range(ROWS // 8):
            rest = jnp.zeros((4 * 8, LANES), jnp.float32)
            for place in range(8):
                shift = REST * (place - g) % LANES
                tile = tails[8 * half + place]
                moved = pltpu.roll(tile, shift, 1) if shift else tile
                rest = jnp.where(lane_group == place, moved, rest)
            for r in range(4):
                spread[A_ROWS * r + 8 * g : A_ROWS * r + 8 * g + 8, half * LANES : (half + 1) * LANES] = rest[8 * r : 8 * r + 8]
    left[:, MAIN:] = spread[...].astype(jnp.bfloat16)
    total = jnp.dot(left[...], right[...], preferred_element_type=jnp.float32)
    for r in range(4):
        for c in range(4):
            out_ref[4 * r + c] = total[A_ROWS * r : A_ROWS * r + ROWS, c * LANES : (c + 1) * LANES]


def multiply(my_zh, a_slots, b_slots):
    depth = PIECES * (LANES + REST)
    return pl.pallas_call(
        multiply_kernel,
        out_shape=jax.ShapeDtypeStruct((PIECES, ROWS, LANES), jnp.float32),
        in_specs=[pl.BlockSpec(memory_space=pltpu.SMEM)] + [pl.BlockSpec(memory_space=pltpu.VMEM)] * 5,
        out_specs=pl.BlockSpec(memory_space=pltpu.VMEM),
        scratch_shapes=[
            pltpu.VMEM((4 * A_ROWS, depth), jnp.bfloat16),
            pltpu.VMEM((depth, 4 * LANES), jnp.bfloat16),
            pltpu.VMEM((4 * A_ROWS, 2 * LANES), jnp.float32),
        ],
        compiler_params=pltpu.CompilerParams(vmem_limit_bytes=VMEM),
    )(my_zh, *a_slots, b_slots)


def body(amplitudes, integrals, other_terms, occ_energy, virt_energy):
    pieces = lax.all_to_all(pack(amplitudes, integrals), NEAR, 0, 0, tiled=True)
    a, b = pieces[:, :A_ROWS], pieces[:, A_ROWS:]
    a_slots = [a] + [lax.ppermute(a, "zh", [(i, i ^ d) for i in range(4)]) for d in (1, 2, 3)]
    b_slots = lax.all_to_all(jnp.broadcast_to(b[None], (4,) + b.shape), "yh", 0, 0, tiled=True)
    my_zh = lax.axis_index("zh").astype(jnp.int32)[None]
    partial = multiply(my_zh, a_slots, b_slots)
    partial = lax.all_to_all(partial, NEAR, 0, 0, tiled=True)
    ladder = lax.psum(jnp.sum(partial, axis=0), "l")
    denominator = occ_energy[:, None] - virt_energy[None, :]
    return (ladder + other_terms) / denominator


def solution(mesh):
    fine = Mesh(mesh.devices.reshape(tuple(PARTS.values())), tuple(PARTS))
    row, col = ("yh", "yl", "xl"), ("xh", "zh", "zl")
    in_specs = (P(row, ("l",) + col), P(("l",) + row, col), P(row, col), P(row), P(col))
    return jax.shard_map(body, mesh=fine, in_specs=in_specs, out_specs=P(row, col), check_vma=False)
```

time: 125 us -> 106 us (0.85)
  blocking collectives: 75.3 us -> 39.1 us
  waiting for transfers between devices: 25.5 us -> 38.3 us
  starting transfers between devices: 18.5 us -> 22.4 us
  local copies, waits for them, and re-layouts: 2.09 us -> 3.8 us
    all_to_all x2, blocking collectives: 71.2 us -> 33.1 us  [the longest x1 19.3 us: body(): pieces = lax.all_to_all(pack(amplitudes, integrals), NEAR, 0, 0, tiled=True)]
    all_to_all x0 -> x1, waiting for transfers between devices: none -> 16.5 us  [body(): lax.all_to_all(jnp.broadcast_to(b[None], (4,) + b.shape), 'yh', 0, 0, til...]
    all_to_all x0 -> x1, starting transfers between devices: none -> 6.76 us  [body(): lax.all_to_all(jnp.broadcast_to(b[None], (4,) + b.shape), 'yh', 0, 0, til...]
    ppermute x6 -> x3, waiting for transfers between devices: 25.5 us -> 21.8 us  [body(): lax.ppermute(a, 'zh', [(i, i ^ d) for i in range(4)])]
    ppermute x6 -> x3, starting transfers between devices: 18.5 us -> 15.7 us  [body(): lax.ppermute(a, 'zh', [(i, i ^ d) for i in range(4)])]
    psum x1, blocking collectives: 4.15 us -> 5.92 us  [body(): ladder = lax.psum(jnp.sum(partial, axis=0), 'l')]
    broadcast_in_dim x0 -> x1, local copies, waits for them, and re-layouts: none -> 1.72 us  [body(): jnp.broadcast_to(b[None], (4,) + b.shape)]
  transfers between devices with their start and end apart: 6 -> 4, of which waited for: 2 -> 3; matrix products, arithmetic and copies ran while one was open for 0% -> 0% of each run, Pallas kernels for 0% -> 0%
where the time goes in v2:
time: 106 us
  blocking collectives  39.1 us (37%)
  waiting for transfers between devices  38.3 us (36%)
  starting transfers between devices  22.4 us (21%)
  local copies, waits for them, and re-layouts  3.8 us (4%)
  Pallas kernels  1.25 us (1%)
    ppermute x3, waiting for transfers between devices, body(): lax.ppermute(a, 'zh', [(i, i ^ d) for i in range(4)])  21.8 us
    all_to_all x1, blocking collectives, body(): pieces = lax.all_to_all(pack(amplitudes, integrals), NEAR, 0, 0, tiled=True)  19.3 us
    all_to_all x1, waiting for transfers between devices, body(): lax.all_to_all(jnp.broadcast_to(b[None], (4,) + b.shape), 'yh', 0, 0, til...  16.5 us
    ppermute x3, starting transfers between devices, body(): lax.ppermute(a, 'zh', [(i, i ^ d) for i in range(4)])  15.7 us
    all_to_all x1, blocking collectives, body(): partial = lax.all_to_all(partial, NEAR, 0, 0, tiled=True)  13.8 us
    all_to_all x1, starting transfers between devices, body(): lax.all_to_all(jnp.broadcast_to(b[None], (4,) + b.shape), 'yh', 0, 0, til...  6.76 us
    psum x1, blocking collectives, body(): ladder = lax.psum(jnp.sum(partial, axis=0), 'l')  5.92 us
  transfers between devices with their start and end apart: 4, of which 3 were waited for; matrix products, arithmetic and copies ran while one was open for 0% of the time, Pallas kernels for 0%

profile of v2, /device:TPU:1, one launch (start us, length us, event | category | flops | bytes accessed | tf_op | source)
XLA Modules:
  0.0 105.7 jit_solution(5344162349884861219)
XLA Ops:
  0.0 0.0 copy-start
  0.0 1.1 %copy-done = bf16[2304,128]{1,0:T(8,128)(2,1)S(1)} copy-done((bf16[2304,128]{1,0:T(8,128)(2,1)S(1)}, bf16[2304,128]{1,0:T(8,128)(2,1)}, u32[]{:S(2)}) %copy-start) | copy-done | bytes 589848
  1.1 0.0 copy-start.1
  1.1 0.9 copy-done.1
  2.0 0.2 shard_map.55
  2.2 19.3 %all_to_all.15 = bf16[16,208,128]{2,1,0:T(8,128)(2,1)S(1)} all-to-all(bf16[16,208,128]{2,1,0:T(8,128)(2,1)S(1)} %shard_map.55), channel_id=1, replica_groups=mesh['l'=2,'yh'=4,'yl'=2,'xl'=2,'xh'=2,'zh'=4,'zl'=2] {'yl','xl','xh','zl'}, dimensions={0} | all-to-all | bytes 1703936 | tf_op jit(solution)/shard_map/all_to_all | solution.py:103
  21.6 1.7 %broadcast_in_dim.5 = bf16[4,16,144,128]{3,2,1,0:T(8,128)(2,1)} broadcast(bf16[16,144,128]{2,1,0:T(8,128)(2,1)S(1)} %slice.9), dimensions={1,2,3} | broadcast | bytes 2949120 | tf_op jit(solution)/shard_map/broadcast_in_dim | solution.py:106
  23.3 6.8 %all-to-all-start.1 = ((bf16[4,16,144,128]{3,2,1,0:T(8,128)(2,1)}), bf16[4,16,144,128]{3,2,1,0:T(8,128)(2,1)S(1)}, u32[]{:S(2)}, u32[]{:S(2)}) async-start(bf16[4,16,144,128]{3,2,1,0:T(8,128)(2,1)} %broadcast_in_dim.5), calls=%async_computation.1 | async-start | bytes 4718592 | tf_op jit(solution)/shard_map/all_to_all | solution.py:106
  30.1 5.8 %collective-permute-start = (bf16[16,64,128]{2,1,0:T(8,128)(2,1)S(1)}, bf16[16,64,128]{2,1,0:T(8,128)(2,1)S(1)}, u32[]{:S(2)}, u32[]{:S(2)}) collective-permute-start(bf16[16,64,128]{2,1,0:T(8,128)(2,1)S(1)} %slice.8.refs_0_), channel_id=1, source_target_pairs={{0,2},{2,0},{4,6},{6,4},{1,3},{3,1},{5,7},{7,5},{8,10},{10,8},{12,... | collective-permute-start | bytes 786440 | tf_op jit(solution)/shard_map/ppermute | solution.py:105
  35.9 7.9 %collective-permute-start.1 = (bf16[16,64,128]{2,1,0:T(8,128)(2,1)S(1)}, bf16[16,64,128]{2,1,0:T(8,128)(2,1)S(1)}, u32[]{:S(2)}, u32[]{:S(2)}) collective-permute-start(bf16[16,64,128]{2,1,0:T(8,128)(2,1)S(1)} %slice.8.refs_0_), channel_id=1, source_target_pairs={{0,4},{2,6},{4,0},{6,2},{1,5},{3,7},{5,1},{7,3},{8,12},{10,14},{12... | collective-permute-start | bytes 786440 | tf_op jit(solution)/shard_map/ppermute | solution.py:105
  43.8 1.9 %collective-permute-start.2 = (bf16[16,64,128]{2,1,0:T(8,128)(2,1)S(1)}, bf16[16,64,128]{2,1,0:T(8,128)(2,1)S(1)}, u32[]{:S(2)}, u32[]{:S(2)}) collective-permute-start(bf16[16,64,128]{2,1,0:T(8,128)(2,1)S(1)} %slice.8.refs_0_), channel_id=1, source_target_pairs={{0,6},{2,4},{4,2},{6,0},{1,7},{3,5},{5,3},{7,1},{8,14},{10,12},{12... | collective-permute-start | bytes 786440 | tf_op jit(solution)/shard_map/ppermute | solution.py:105
  45.8 12.8 %collective-permute-done.refs_1_ = bf16[16,64,128]{2,1,0:T(8,128)(2,1)S(1)} collective-permute-done((bf16[16,64,128]{2,1,0:T(8,128)(2,1)S(1)}, bf16[16,64,128]{2,1,0:T(8,128)(2,1)S(1)}, u32[]{:S(2)}, u32[]{:S(2)}) %collective-permute-start) | collective-permute-done | bytes 262176 | tf_op jit(solution)/shard_map/ppermute | solution.py:105
  58.5 0.0 collective-permute-done.1.refs_2_
  58.5 9.0 %collective-permute-done.2.refs_3_ = bf16[16,64,128]{2,1,0:T(8,128)(2,1)S(1)} collective-permute-done((bf16[16,64,128]{2,1,0:T(8,128)(2,1)S(1)}, bf16[16,64,128]{2,1,0:T(8,128)(2,1)S(1)}, u32[]{:S(2)}, u32[]{:S(2)}) %collective-permute-start.2) | collective-permute-done | bytes 262176 | tf_op jit(solution)/shard_map/ppermute | solution.py:105
  67.6 16.5 %all-to-all-done.1.refs_4_ = bf16[4,16,144,128]{3,2,1,0:T(8,128)(2,1)S(1)} async-done(((bf16[4,16,144,128]{3,2,1,0:T(8,128)(2,1)}), bf16[4,16,144,128]{3,2,1,0:T(8,128)(2,1)S(1)}, u32[]{:S(2)}, u32[]{:S(2)}) %all-to-all-start.1) | async-done | bytes 2359328 | tf_op jit(solution)/shard_map/all_to_all | solution.py:106
  84.1 0.0 copy-start.2
  84.1 0.0 copy-start.3
  84.1 0.0 copy-start.4
  84.1 1.1 %shard_map.56 = f32[16,56,128]{2,1,0:T(8,128)S(1)} custom-call(s32[1]{0:T(128)} %bitcast.my_zh_ref, bf16[16,64,128]{2,1,0:T(8,128)(2,1)S(1)} %slice.8.refs_0_, bf16[16,64,128]{2,1,0:T(8,128)(2,1)S(1)} %collective-permute-done.refs_1_, bf16[16,64,128]{2,1,0:T(8,128)(2,1)S(1)} %collective-permute-done.1.refs_2_, ...), custom_call_target="tpu_custom_call" | custom-call | tf_op jit(solution)/shard_map/pallas_call | solution.py:88
  85.2 13.8 %all_to_all.16 = f32[16,56,128]{2,1,0:T(8,128)S(1)} all-to-all(f32[16,56,128]{2,1,0:T(8,128)S(1)} %shard_map.56), channel_id=1, replica_groups=mesh['l'=2,'yh'=4,'yl'=2,'xl'=2,'xh'=2,'zh'=4,'zl'=2] {'yl','xl','xh','zl'}, dimensions={0} | all-to-all | bytes 917504 | tf_op jit(solution)/shard_map/all_to_all | solution.py:109
  99.0 5.9 %psum.7 = f32[56,128]{1,0:T(8,128)S(1)} all-reduce(f32[56,128]{1,0:T(8,128)S(1)} %reduce_sum.9), channel_id=1, replica_groups=mesh['l'=2,'yh'=4,'yl'=2,'xl'=2,'xh'=2,'zh'=4,'zl'=2] {'l'}, use_global_device_ids=true, to_apply=%region_1.0 | all-reduce | flops 7168 | bytes 57344 | tf_op jit(solution)/shard_map/psum | solution.py:110
  105.0 0.0 copy-done.2
  105.0 0.0 copy-done.3
  105.0 0.0 copy-done.4
  105.0 0.7 subtract_divide_fusion
  (3 shorter events, 0.1 us)
Async XLA Ops:
  0.0 1.1 %copy-start = (bf16[2304,128]{1,0:T(8,128)(2,1)S(1)}, bf16[2304,128]{1,0:T(8,128)(2,1)}, u32[]{:S(2)}) copy-start(bf16[2304,128]{1,0:T(8,128)(2,1)} %b_ref.1) | copy-start | bytes 1769476
  1.1 0.9 copy-start.1
  23.3 60.8 %all-to-all-start.1 = ((bf16[4,16,144,128]{3,2,1,0:T(8,128)(2,1)}), bf16[4,16,144,128]{3,2,1,0:T(8,128)(2,1)S(1)}, u32[]{:S(2)}, u32[]{:S(2)}) async-start(bf16[4,16,144,128]{3,2,1,0:T(8,128)(2,1)} %broadcast_in_dim.5), calls=%async_computation.1 | async-start | bytes 4718592 | tf_op jit(solution)/shard_map/all_to_all | solution.py:106
  30.1 28.5 %collective-permute-start = (bf16[16,64,128]{2,1,0:T(8,128)(2,1)S(1)}, bf16[16,64,128]{2,1,0:T(8,128)(2,1)S(1)}, u32[]{:S(2)}, u32[]{:S(2)}) collective-permute-start(bf16[16,64,128]{2,1,0:T(8,128)(2,1)S(1)} %slice.8.refs_0_), channel_id=1, source_target_pairs={{0,2},{2,0},{4,6},{6,4},{1,3},{3,1},{5,7},{7,5},{8,10},{10,8},{12,... | collective-permute-start | bytes 786440 | tf_op jit(solution)/shard_map/ppermute | solution.py:105
  35.9 22.7 %collective-permute-start.1 = (bf16[16,64,128]{2,1,0:T(8,128)(2,1)S(1)}, bf16[16,64,128]{2,1,0:T(8,128)(2,1)S(1)}, u32[]{:S(2)}, u32[]{:S(2)}) collective-permute-start(bf16[16,64,128]{2,1,0:T(8,128)(2,1)S(1)} %slice.8.refs_0_), channel_id=1, source_target_pairs={{0,4},{2,6},{4,0},{6,2},{1,5},{3,7},{5,1},{7,3},{8,12},{10,14},{12... | collective-permute-start | bytes 786440 | tf_op jit(solution)/shard_map/ppermute | solution.py:105
  43.8 23.7 %collective-permute-start.2 = (bf16[16,64,128]{2,1,0:T(8,128)(2,1)S(1)}, bf16[16,64,128]{2,1,0:T(8,128)(2,1)S(1)}, u32[]{:S(2)}, u32[]{:S(2)}) collective-permute-start(bf16[16,64,128]{2,1,0:T(8,128)(2,1)S(1)} %slice.8.refs_0_), channel_id=1, source_target_pairs={{0,6},{2,4},{4,2},{6,0},{1,7},{3,5},{5,3},{7,1},{8,14},{10,12},{12... | collective-permute-start | bytes 786440 | tf_op jit(solution)/shard_map/ppermute | solution.py:105
  84.1 20.9 %copy-start.2 = (f32[56,128]{1,0:T(8,128)S(1)}, f32[56,128]{1,0:T(8,128)}, u32[]{:S(2)}) copy-start(f32[56,128]{1,0:T(8,128)} %param.7) | copy-start | bytes 86020
  84.1 20.9 %copy-start.3 = (f32[128]{0:T(128)S(1)}, f32[128]{0:T(128)}, u32[]{:S(2)}) copy-start(f32[128]{0:T(128)} %param.9) | copy-start | bytes 1540
  84.1 20.9 %copy-start.4 = (f32[56]{0:T(128)S(1)}, f32[56]{0:T(128)}, u32[]{:S(2)}) copy-start(f32[56]{0:T(128)} %param.8) | copy-start | bytes 676

commit v3 on v2

--- a/solution.py
+++ b/solution.py
@@ -18,7 +18,7 @@
 VMEM = 40 * 1024 * 1024
 
 
-def pack_kernel(a_ref, b_ref, out_ref):
+def pack_kernel(a_ref, b_ref, a_out, b_out):
     lane_group = lax.broadcasted_iota(jnp.int32, (8, LANES), 1) // REST
     tail = a_ref[:, MAIN:].astype(jnp.float32)
     for s in range(PIECES):
@@ -30,17 +30,21 @@
             shift = REST * (g - place) % LANES
             moved = pltpu.roll(tile, shift, 1) if shift else tile
             rest = jnp.where(lane_group == g, moved, rest)
-        out_ref[s, 0:A_ROWS, :] = jnp.concatenate([main, rest], axis=0).astype(jnp.bfloat16)
-        out_ref[s, A_ROWS : A_ROWS + LANES, :] = b_ref[s * LANES : (s + 1) * LANES, :]
-        out_ref[s, A_ROWS + LANES :, :] = b_ref[MAIN + s * REST : MAIN + (s + 1) * REST, :]
+        a_out[s] = jnp.concatenate([main, rest], axis=0).astype(jnp.bfloat16)
+        for far in range(4):
+            b_out[far, s, 0:LANES, :] = b_ref[s * LANES : (s + 1) * LANES, :]
+            b_out[far, s, LANES:, :] = b_ref[MAIN + s * REST : MAIN + (s + 1) * REST, :]
 
 
 def pack(a, b):
     return pl.pallas_call(
         pack_kernel,
-        out_shape=jax.ShapeDtypeStruct((PIECES, A_ROWS + B_ROWS, LANES), jnp.bfloat16),
+        out_shape=[
+            jax.ShapeDtypeStruct((PIECES, A_ROWS, LANES), jnp.bfloat16),
+            jax.ShapeDtypeStruct((4, PIECES, B_ROWS, LANES), jnp.bfloat16),
+        ],
         in_specs=[pl.BlockSpec(memory_space=pltpu.VMEM)] * 2,
-        out_specs=pl.BlockSpec(memory_space=pltpu.VMEM),
+        out_specs=[pl.BlockSpec(memory_space=pltpu.VMEM)] * 2,
         compiler_params=pltpu.CompilerParams(vmem_limit_bytes=VMEM),
     )(a, b)
 
@@ -100,10 +104,10 @@
 
 
 def body(amplitudes, integrals, other_terms, occ_energy, virt_energy):
-    pieces = lax.all_to_all(pack(amplitudes, integrals), NEAR, 0, 0, tiled=True)
-    a, b = pieces[:, :A_ROWS], pieces[:, A_ROWS:]
+    a, b = pack(amplitudes, integrals)
+    b_slots = lax.all_to_all(b.reshape((4 * PIECES,) + b.shape[2:]), ("yh",) + NEAR, 0, 0, tiled=True).reshape(b.shape)
+    a = lax.all_to_all(a, NEAR, 0, 0, tiled=True)
     a_slots = [a] + [lax.ppermute(a, "zh", [(i, i ^ d) for i in range(4)]) for d in (1, 2, 3)]
-    b_slots = lax.all_to_all(jnp.broadcast_to(b[None], (4,) + b.shape), "yh", 0, 0, tiled=True)
     my_zh = lax.axis_index("zh").astype(jnp.int32)[None]
     partial = multiply(my_zh, a_slots, b_slots)
     partial = lax.all_to_all(partial, NEAR, 0, 0, tiled=True)

time: 106 us -> 103 us (0.972)
  blocking collectives: 39.1 us -> 34.6 us
  starting transfers between devices: 22.4 us -> 23.8 us
    all_to_all x1, waiting for transfers between devices: 16.5 us -> 0.01 us  [body(): lax.all_to_all(b.reshape((4 * PIECES,) + b.shape[2:]), ('yh',) + NEAR, 0,...]
    ppermute x3, waiting for transfers between devices: 21.8 us -> 38 us  [body(): lax.ppermute(a, 'zh', [(i, i ^ d) for i in range(4)])]
    all_to_all x1, blocking collectives: 19.3 us -> 14.4 us  [body(): a = lax.all_to_all(a, NEAR, 0, 0, tiled=True)]
    broadcast_in_dim x1 -> x0, local copies, waits for them, and re-layouts: 1.72 us -> none  [body(): jnp.broadcast_to(b[None], (4,) + b.shape)]
    unnamed x10 -> x12, local copies, waits for them, and re-layouts: 2.02 us -> 3.42 us
    all_to_all x1, starting transfers between devices: 6.76 us -> 8.13 us  [body(): lax.all_to_all(b.reshape((4 * PIECES,) + b.shape[2:]), ('yh',) + NEAR, 0,...]
    psum x1, blocking collectives: 5.92 us -> 7.08 us  [body(): ladder = lax.psum(jnp.sum(partial, axis=0), 'l')]
  transfers between devices with their start and end apart: 4 -> 4, of which waited for: 3 -> 2; matrix products, arithmetic and copies ran while one was open for 0% -> 0% of each run, Pallas kernels for 0% -> 0%
where the time goes in v3:
time: 103 us; the launch traced here: 102 us
  waiting for transfers between devices  38 us (37%)
  blocking collectives  34.6 us (34%)
  starting transfers between devices  23.8 us (23%)
  local copies, waits for them, and re-layouts  3.42 us (3%)
  Pallas kernels  1.45 us (1%)
    ppermute x3, waiting for transfers between devices, body(): lax.ppermute(a, 'zh', [(i, i ^ d) for i in range(4)])  38 us
    ppermute x3, starting transfers between devices, body(): lax.ppermute(a, 'zh', [(i, i ^ d) for i in range(4)])  15.7 us
    all_to_all x1, blocking collectives, body(): a = lax.all_to_all(a, NEAR, 0, 0, tiled=True)  14.4 us
    all_to_all x1, blocking collectives, body(): partial = lax.all_to_all(partial, NEAR, 0, 0, tiled=True)  13.1 us
    all_to_all x1, starting transfers between devices, body(): lax.all_to_all(b.reshape((4 * PIECES,) + b.shape[2:]), ('yh',) + NEAR, 0,...  8.13 us
    psum x1, blocking collectives, body(): ladder = lax.psum(jnp.sum(partial, axis=0), 'l')  7.08 us
    unnamed x12, local copies, waits for them, and re-layouts  3.42 us
  transfers between devices with their start and end apart: 4, of which 2 were waited for; matrix products, arithmetic and copies ran while one was open for 0% of the time, Pallas kernels for 0%

profile of v3, /device:TPU:1, one launch (start us, length us, event | category | flops | bytes accessed | tf_op | source)
XLA Modules:
  0.0 102.1 jit_solution(260260926394364053)
XLA Ops:
  0.0 0.0 copy-start.1
  0.0 1.1 %copy-done.1 = bf16[2304,128]{1,0:T(8,128)(2,1)S(1)} copy-done((bf16[2304,128]{1,0:T(8,128)(2,1)S(1)}, bf16[2304,128]{1,0:T(8,128)(2,1)}, u32[]{:S(2)}) %copy-start.1) | copy-done | bytes 589848
  1.1 0.0 copy-start.2
  1.1 0.9 copy-done.2
  2.0 0.4 shard_map.55
  2.4 0.0 copy-start
  2.4 1.4 %copy-done = bf16[4,16,144,128]{3,2,1,0:T(8,128)(2,1)} copy-done((bf16[4,16,144,128]{3,2,1,0:T(8,128)(2,1)}, bf16[4,16,144,128]{3,2,1,0:T(8,128)(2,1)S(1)}, u32[]{:S(2)}) %copy-start) | copy-done | bytes 2359320
  3.8 14.4 %all_to_all.15.refs_0_ = bf16[16,64,128]{2,1,0:T(8,128)(2,1)S(1)} all-to-all(bf16[16,64,128]{2,1,0:T(8,128)(2,1)S(1)} %get-tuple-element.7), channel_id=1, replica_groups=mesh['l'=2,'yh'=4,'yl'=2,'xl'=2,'xh'=2,'zh'=4,'zl'=2] {'yl','xl','xh','zl'}, dimensions={0} | all-to-all | bytes 524288 | tf_op jit(solution)/shard_map/all_to_all | solution.py:109
  18.1 8.1 %all-to-all-start.1 = ((bf16[64,144,128]{2,1,0:T(8,128)(2,1)}), bf16[64,144,128]{2,1,0:T(8,128)(2,1)S(1)}, u32[]{:S(2)}, u32[]{:S(2)}) async-start(bf16[64,144,128]{2,1,0:T(8,128)(2,1)} %bitcast.4), calls=%async_computation.1 | async-start | bytes 4718592 | tf_op jit(solution)/shard_map/all_to_all | solution.py:108
  26.3 9.8 %collective-permute-start.2 = (bf16[16,64,128]{2,1,0:T(8,128)(2,1)S(1)}, bf16[16,64,128]{2,1,0:T(8,128)(2,1)S(1)}, u32[]{:S(2)}, u32[]{:S(2)}) collective-permute-start(bf16[16,64,128]{2,1,0:T(8,128)(2,1)S(1)} %all_to_all.15.refs_0_), channel_id=1, source_target_pairs={{0,6},{2,4},{4,2},{6,0},{1,7},{3,5},{5,3},{7,1},{8,14},{10,12},{12... | collective-permute-start | bytes 786440 | tf_op jit(solution)/shard_map/ppermute | solution.py:110
  36.0 1.9 %collective-permute-start.1 = (bf16[16,64,128]{2,1,0:T(8,128)(2,1)S(1)}, bf16[16,64,128]{2,1,0:T(8,128)(2,1)S(1)}, u32[]{:S(2)}, u32[]{:S(2)}) collective-permute-start(bf16[16,64,128]{2,1,0:T(8,128)(2,1)S(1)} %all_to_all.15.refs_0_), channel_id=1, source_target_pairs={{0,4},{2,6},{4,0},{6,2},{1,5},{3,7},{5,1},{7,3},{8,12},{10,14},{12... | collective-permute-start | bytes 786440 | tf_op jit(solution)/shard_map/ppermute | solution.py:110
  38.0 4.0 %collective-permute-start = (bf16[16,64,128]{2,1,0:T(8,128)(2,1)S(1)}, bf16[16,64,128]{2,1,0:T(8,128)(2,1)S(1)}, u32[]{:S(2)}, u32[]{:S(2)}) collective-permute-start(bf16[16,64,128]{2,1,0:T(8,128)(2,1)S(1)} %all_to_all.15.refs_0_), channel_id=1, source_target_pairs={{0,2},{2,0},{4,6},{6,4},{1,3},{3,1},{5,7},{7,5},{8,10},{10,8},{12,... | collective-permute-start | bytes 786440 | tf_op jit(solution)/shard_map/ppermute | solution.py:110
  42.0 26.3 %collective-permute-done.2.refs_3_ = bf16[16,64,128]{2,1,0:T(8,128)(2,1)S(1)} collective-permute-done((bf16[16,64,128]{2,1,0:T(8,128)(2,1)S(1)}, bf16[16,64,128]{2,1,0:T(8,128)(2,1)S(1)}, u32[]{:S(2)}, u32[]{:S(2)}) %collective-permute-start.2) | collective-permute-done | bytes 262176 | tf_op jit(solution)/shard_map/ppermute | solution.py:110
  68.3 0.0 collective-permute-done.1.refs_2_
  68.3 11.7 %collective-permute-done.refs_1_ = bf16[16,64,128]{2,1,0:T(8,128)(2,1)S(1)} collective-permute-done((bf16[16,64,128]{2,1,0:T(8,128)(2,1)S(1)}, bf16[16,64,128]{2,1,0:T(8,128)(2,1)S(1)}, u32[]{:S(2)}, u32[]{:S(2)}) %collective-permute-start) | collective-permute-done | bytes 262176 | tf_op jit(solution)/shard_map/ppermute | solution.py:110
  80.0 0.0 all-to-all-done.1
  80.0 0.0 copy-start.3
  80.0 0.0 copy-start.4
  80.0 0.0 copy-start.5
  80.0 1.1 %shard_map.56 = f32[16,56,128]{2,1,0:T(8,128)S(1)} custom-call(s32[1]{0:T(128)} %bitcast.my_zh_ref, bf16[16,64,128]{2,1,0:T(8,128)(2,1)S(1)} %all_to_all.15.refs_0_, bf16[16,64,128]{2,1,0:T(8,128)(2,1)S(1)} %collective-permute-done.refs_1_, bf16[16,64,128]{2,1,0:T(8,128)(2,1)S(1)} %collective-permute-done.1.refs_2_, ...), custom_call_target="tpu_custom_call" | custom-call | tf_op jit(solution)/shard_map/pallas_call | solution.py:92
  81.1 13.1 %all_to_all.16 = f32[16,56,128]{2,1,0:T(8,128)S(1)} all-to-all(f32[16,56,128]{2,1,0:T(8,128)S(1)} %shard_map.56), channel_id=1, replica_groups=mesh['l'=2,'yh'=4,'yl'=2,'xl'=2,'xh'=2,'zh'=4,'zl'=2] {'yl','xl','xh','zl'}, dimensions={0} | all-to-all | bytes 917504 | tf_op jit(solution)/shard_map/all_to_all | solution.py:113
  94.3 7.1 %psum.7 = f32[56,128]{1,0:T(8,128)S(1)} all-reduce(f32[56,128]{1,0:T(8,128)S(1)} %reduce_sum.9), channel_id=1, replica_groups=mesh['l'=2,'yh'=4,'yl'=2,'xl'=2,'xh'=2,'zh'=4,'zl'=2] {'l'}, use_global_device_ids=true, to_apply=%region_1.0 | all-reduce | flops 7168 | bytes 57344 | tf_op jit(solution)/shard_map/psum | solution.py:114
  101.4 0.0 copy-done.3
  101.4 0.0 copy-done.4
  101.4 0.0 copy-done.5
  101.4 0.7 subtract_divide_fusion
  (1 shorter events, 0.0 us)
Async XLA Ops:
  0.0 1.1 %copy-start.1 = (bf16[2304,128]{1,0:T(8,128)(2,1)S(1)}, bf16[2304,128]{1,0:T(8,128)(2,1)}, u32[]{:S(2)}) copy-start(bf16[2304,128]{1,0:T(8,128)(2,1)} %b_ref.1) | copy-start | bytes 1769476
  1.1 0.9 copy-start.2
  2.4 1.4 %copy-start = (bf16[4,16,144,128]{3,2,1,0:T(8,128)(2,1)}, bf16[4,16,144,128]{3,2,1,0:T(8,128)(2,1)S(1)}, u32[]{:S(2)}) copy-start(bf16[4,16,144,128]{3,2,1,0:T(8,128)(2,1)S(1)} %get-tuple-element.8) | copy-start | bytes 7077892
  18.1 61.9 %all-to-all-start.1 = ((bf16[64,144,128]{2,1,0:T(8,128)(2,1)}), bf16[64,144,128]{2,1,0:T(8,128)(2,1)S(1)}, u32[]{:S(2)}, u32[]{:S(2)}) async-start(bf16[64,144,128]{2,1,0:T(8,128)(2,1)} %bitcast.4), calls=%async_computation.1 | async-start | bytes 4718592 | tf_op jit(solution)/shard_map/all_to_all | solution.py:108
  26.3 42.0 %collective-permute-start.2 = (bf16[16,64,128]{2,1,0:T(8,128)(2,1)S(1)}, bf16[16,64,128]{2,1,0:T(8,128)(2,1)S(1)}, u32[]{:S(2)}, u32[]{:S(2)}) collective-permute-start(bf16[16,64,128]{2,1,0:T(8,128)(2,1)S(1)} %all_to_all.15.refs_0_), channel_id=1, source_target_pairs={{0,6},{2,4},{4,2},{6,0},{1,7},{3,5},{5,3},{7,1},{8,14},{10,12},{12... | collective-permute-start | bytes 786440 | tf_op jit(solution)/shard_map/ppermute | solution.py:110
  36.0 32.3 %collective-permute-start.1 = (bf16[16,64,128]{2,1,0:T(8,128)(2,1)S(1)}, bf16[16,64,128]{2,1,0:T(8,128)(2,1)S(1)}, u32[]{:S(2)}, u32[]{:S(2)}) collective-permute-start(bf16[16,64,128]{2,1,0:T(8,128)(2,1)S(1)} %all_to_all.15.refs_0_), channel_id=1, source_target_pairs={{0,4},{2,6},{4,0},{6,2},{1,5},{3,7},{5,1},{7,3},{8,12},{10,14},{12... | collective-permute-start | bytes 786440 | tf_op jit(solution)/shard_map/ppermute | solution.py:110
  38.0 42.0 %collective-permute-start = (bf16[16,64,128]{2,1,0:T(8,128)(2,1)S(1)}, bf16[16,64,128]{2,1,0:T(8,128)(2,1)S(1)}, u32[]{:S(2)}, u32[]{:S(2)}) collective-permute-start(bf16[16,64,128]{2,1,0:T(8,128)(2,1)S(1)} %all_to_all.15.refs_0_), channel_id=1, source_target_pairs={{0,2},{2,0},{4,6},{6,4},{1,3},{3,1},{5,7},{7,5},{8,10},{10,8},{12,... | collective-permute-start | bytes 786440 | tf_op jit(solution)/shard_map/ppermute | solution.py:110
  80.0 21.4 %copy-start.3 = (f32[56,128]{1,0:T(8,128)S(1)}, f32[56,128]{1,0:T(8,128)}, u32[]{:S(2)}) copy-start(f32[56,128]{1,0:T(8,128)} %param.7) | copy-start | bytes 86020
  80.0 21.4 %copy-start.4 = (f32[128]{0:T(128)S(1)}, f32[128]{0:T(128)}, u32[]{:S(2)}) copy-start(f32[128]{0:T(128)} %param.9) | copy-start | bytes 1540
  80.0 21.4 %copy-start.5 = (f32[56]{0:T(128)S(1)}, f32[56]{0:T(128)}, u32[]{:S(2)}) copy-start(f32[56]{0:T(128)} %param.8) | copy-start | bytes 676

commit v4 on v3

v4 whole, which is shorter than its diff:
```python
import jax
import jax.numpy as jnp
from jax import lax
from jax.experimental import pallas as pl
from jax.experimental.pallas import tpu as pltpu
from jax.sharding import Mesh
from jax.sharding import PartitionSpec as P

PARTS = {"l": 2, "y2": 2, "y1": 2, "yl": 2, "xl": 2, "xh": 2, "zh": 4, "zl": 2}
NEAR = ("yl", "xl", "xh", "zl")
PIECES = 32
BLOCKS = 16
ROWS = 56
LANES = 128
HALF = LANES // 2
REST = 8
MAIN = PIECES * HALF
GROUPS = ROWS // 8
B_ROWS = HALF + REST
R_BLOCKS = 8
C_BLOCKS = 4
A_ROWS = 64
VMEM = 40 * 1024 * 1024
f32, bf16 = jnp.float32, jnp.bfloat16


def rolled(x, shift):
    return pltpu.roll(x, shift % LANES, 1) if shift % LANES else x


def pack_kernel(a_ref, b_ref, a_out, b_out):
    lane = lax.broadcasted_iota(jnp.int32, (8, LANES), 1)
    left_half = lax.broadcasted_iota(jnp.int32, (24, LANES), 1) < HALF
    a_tail = a_ref[:, MAIN:].astype(f32)
    b_tail = b_ref[MAIN:, :].astype(f32)
    for s in range(PIECES):
        tile = a_ref[:, s // 2 * LANES : (s // 2 + 1) * LANES].astype(f32)
        upper, lower = rolled(tile[:32], s % 2 * HALF), rolled(tile[32:], (s + 1) % 2 * HALF)
        corner = upper[24:]
        for g in range(GROUPS):
            rest = a_tail[8 * g : 8 * g + 8, s // 16 * LANES : (s // 16 + 1) * LANES]
            rest = rolled(rest, HALF + REST * g - REST * (s % 16))
            corner = jnp.where((lane >= HALF) & (lane // REST == HALF // REST + g), rest, corner)
        piece = jnp.concatenate([jnp.where(left_half, upper[:24], lower), corner], axis=0)
        a_out[s] = piece.astype(bf16)
        piece = jnp.concatenate([b_ref[s * HALF : (s + 1) * HALF, :].astype(f32), b_tail[s * REST : (s + 1) * REST]], axis=0)
        for far in range(2):
            b_out[far * PIECES + s] = piece.astype(bf16)


def pack(a, b):
    return pl.pallas_call(
        pack_kernel,
        out_shape=[
            jax.ShapeDtypeStruct((PIECES, 32, LANES), bf16),
            jax.ShapeDtypeStruct((2 * PIECES, B_ROWS, LANES), bf16),
        ],
        in_specs=[pl.BlockSpec(memory_space=pltpu.VMEM)] * 2,
        out_specs=[pl.BlockSpec(memory_space=pltpu.VMEM)] * 2,
        compiler_params=pltpu.CompilerParams(vmem_limit_bytes=VMEM),
    )(a, b)


def multiply_kernel(my_zh_ref, *refs):
    a_refs, (b_ref, out_ref, left, right, spread) = refs[:4], refs[4:]
    my_zh = my_zh_ref[0]
    left_half = lax.broadcasted_iota(jnp.int32, (32, LANES), 1) < HALF
    lane_group = lax.broadcasted_iota(jnp.int32, (8 * R_BLOCKS, LANES), 1) // REST
    main = BLOCKS * HALF
    corners = []
    b_rest = [[] for _ in range(C_BLOCKS)]
    for pair in range(BLOCKS // 2):
        flip, b3 = pair >> 1, pair & 1
        columns = slice(pair * LANES, (pair + 1) * LANES)
        corner = [[], []]
        for r in range(R_BLOCKS):
            p0 = a_refs[flip][4 * r + 2 * b3].astype(f32)
            p1 = a_refs[flip][4 * r + 2 * b3 + 1].astype(f32)
            upper = jnp.where(left_half, p0, rolled(p1, HALF))
            lower = jnp.where(left_half, rolled(p0, HALF), p1)
            left[A_ROWS * r : A_ROWS * r + 32, columns] = upper.astype(bf16)
            left[A_ROWS * r + 32 : A_ROWS * (r + 1), columns] = lower.astype(bf16)
            corner[0].append(p0[24:])
            corner[1].append(p1[24:])
        corners += [jnp.concatenate(c, axis=0) for c in corner]
        for b0 in range(2):
            block = 8 * b3 + 2 * (my_zh ^ flip) + b0
            at = (2 * pair + b0) * HALF
            for c in range(C_BLOCKS):
                piece = b_ref[C_BLOCKS * block + c]
                right[at : at + HALF, c * LANES : (c + 1) * LANES] = piece[:HALF]
                b_rest[c].append(piece.astype(f32)[HALF:])
    for c in range(C_BLOCKS):
        right[main:, c * LANES : (c + 1) * LANES] = jnp.concatenate(b_rest[c], axis=0).astype(bf16)
    for g in range(8):
        rest = jnp.zeros((8 * R_BLOCKS, LANES), f32)
        for t in range(BLOCKS if g < GROUPS else 0):
            rest = jnp.where(lane_group == t, rolled(corners[t], REST * (t - g) - HALF), rest)
        for r in range(R_BLOCKS):
            spread[A_ROWS * r + 8 * g : A_ROWS * r + 8 * g + 8, :] = rest[8 * r : 8 * r + 8]
    left[:, main:] = spread[...].astype(bf16)
    for r in range(R_BLOCKS):
        y1, near_row = divmod(r, 4)
        if r % 4 == 0:
            total = jnp.dot(left[A_ROWS * r : A_ROWS * (r + 4), :], right[...], preferred_element_type=f32)
        for c in range(C_BLOCKS):
            out_ref[C_BLOCKS * near_row + c, y1] = total[A_ROWS * near_row : A_ROWS * near_row + ROWS, c * LANES : (c + 1) * LANES]


def multiply(my_zh, a_slots, b_slots):
    depth = BLOCKS * B_ROWS
    return pl.pallas_call(
        multiply_kernel,
        out_shape=jax.ShapeDtypeStruct((16, 2, ROWS, LANES), f32),
        in_specs=[pl.BlockSpec(memory_space=pltpu.SMEM)] + [pl.BlockSpec(memory_space=pltpu.VMEM)] * 5,
        out_specs=pl.BlockSpec(memory_space=pltpu.VMEM),
        scratch_shapes=[
            pltpu.VMEM((R_BLOCKS * A_ROWS, depth), bf16),
            pltpu.VMEM((depth, C_BLOCKS * LANES), bf16),
            pltpu.VMEM((R_BLOCKS * A_ROWS, LANES), f32),
        ],
        compiler_params=pltpu.CompilerParams(vmem_limit_bytes=VMEM),
    )(my_zh, *a_slots, b_slots)


def body(amplitudes, integrals, other_terms, occ_energy, virt_energy):
    a, b = pack(amplitudes, integrals)
    b_slots = lax.all_to_all(b, ("y2", "y1") + NEAR, 0, 0, tiled=True)
    a = lax.all_to_all(a, ("y1",) + NEAR, 0, 0, tiled=True)
    a_slots = [a] + [lax.ppermute(a, "zh", [(i, i ^ d) for i in range(4)]) for d in (1, 2, 3)]
    my_zh = lax.axis_index("zh").astype(jnp.int32)[None]
    tiles = lax.all_to_all(multiply(my_zh, a_slots, b_slots), NEAR, 0, 0, tiled=True)
    tiles = jnp.sum(tiles, axis=0)
    tiles = lax.all_to_all(jnp.concatenate([tiles, tiles]), ("l", "y1"), 0, 0, tiled=True)
    denominator = occ_energy[:, None] - virt_energy[None, :]
    return (jnp.sum(tiles, axis=0) + other_terms) / denominator


def solution(mesh):
    fine = Mesh(mesh.devices.reshape(tuple(PARTS.values())), tuple(PARTS))
    row, col = ("y2", "y1", "yl", "xl"), ("xh", "zh", "zl")
    in_specs = (P(row, ("l",) + col), P(("l",) + row, col), P(row, col), P(row), P(col))
    return jax.shard_map(body, mesh=fine, in_specs=in_specs, out_specs=P(row, col), check_vma=False)
```

time: 103 us -> 104 us (level)
  blocking collectives: 34.6 us -> 54.2 us
  waiting for transfers between devices: 38 us -> 21.2 us
  starting transfers between devices: 23.8 us -> 22.3 us
  local copies, waits for them, and re-layouts: 3.42 us -> 2.02 us
  Pallas kernels: 1.45 us -> 2.7 us
    all_to_all x2 -> x3, blocking collectives: 27.5 us -> 54.2 us  [the longest x1 22.7 us: body(): lax.all_to_all(multiply(my_zh, a_slots, b_slots), NEAR, 0, 0, tiled=True)]
    ppermute x3, waiting for transfers between devices: 38 us -> 21.2 us  [body(): lax.ppermute(a, 'zh', [(i, i ^ d) for i in range(4)])]
    psum x1 -> x0, blocking collectives: 7.08 us -> none  [body(): ladder = lax.psum(jnp.sum(partial, axis=0), 'l')]
    all_to_all x1, starting transfers between devices: 8.13 us -> 6.64 us  [body(): b_slots = lax.all_to_all(b, ('y2', 'y1') + NEAR, 0, 0, tiled=True)]
    unnamed x12 -> x10, local copies, waits for them, and re-layouts: 3.42 us -> 2.02 us
    pallas_call x2, Pallas kernels: 1.45 us -> 2.7 us  [the longest x1 1.36 us: multiply(): pl.pallas_call(multiply_kernel, out_shape=jax.ShapeDtypeStruct((16, 2, RO...]
  transfers between devices with their start and end apart: 4 -> 4, of which waited for: 2 -> 1; matrix products, arithmetic and copies ran while one was open for 0% -> 0% of each run, Pallas kernels for 0% -> 0%
where the time goes in v4:
time: 104 us; the launch traced here: 103 us
  blocking collectives  54.2 us (52%)
  starting transfers between devices  22.3 us (21%)
  waiting for transfers between devices  21.2 us (20%)
  Pallas kernels  2.7 us (3%)
  local copies, waits for them, and re-layouts  2.02 us (2%)
    all_to_all x1, blocking collectives, body(): lax.all_to_all(multiply(my_zh, a_slots, b_slots), NEAR, 0, 0, tiled=True)  22.7 us
    ppermute x3, waiting for transfers between devices, body(): lax.ppermute(a, 'zh', [(i, i ^ d) for i in range(4)])  21.2 us
    all_to_all x1, blocking collectives, body(): a = lax.all_to_all(a, ('y1',) + NEAR, 0, 0, tiled=True)  19 us
    ppermute x3, starting transfers between devices, body(): lax.ppermute(a, 'zh', [(i, i ^ d) for i in range(4)])  15.7 us
    all_to_all x1, blocking collectives, body(): lax.all_to_all(jnp.concatenate([tiles, tiles]), ('l', 'y1'), 0, 0, tiled=...  12.4 us
    all_to_all x1, starting transfers between devices, body(): b_slots = lax.all_to_all(b, ('y2', 'y1') + NEAR, 0, 0, tiled=True)  6.64 us
  transfers between devices with their start and end apart: 4, of which 1 were waited for; matrix products, arithmetic and copies ran while one was open for 0% of the time, Pallas kernels for 0%

profile of v4, /device:TPU:1, one launch (start us, length us, event | category | flops | bytes accessed | tf_op | source)
XLA Modules:
  0.0 103.2 jit_solution(15570482558827840065)
XLA Ops:
  0.0 0.0 copy-start
  0.0 1.1 %copy-done = bf16[2304,128]{1,0:T(8,128)(2,1)S(1)} copy-done((bf16[2304,128]{1,0:T(8,128)(2,1)S(1)}, bf16[2304,128]{1,0:T(8,128)(2,1)}, u32[]{:S(2)}) %copy-start) | copy-done | bytes 589848
  1.1 0.0 copy-start.1
  1.1 0.9 copy-done.1
  2.0 1.3 %shard_map.55 = (bf16[32,32,128]{2,1,0:T(8,128)(2,1)S(1)}, bf16[64,72,128]{2,1,0:T(8,128)(2,1)}) custom-call(bf16[56,2304]{1,0:T(8,128)(2,1)S(1)} %copy-done.1, bf16[2304,128]{1,0:T(8,128)(2,1)S(1)} %copy-done), custom_call_target="tpu_custom_call" | custom-call | tf_op jit(solution)/shard_map/pallas_call | solution.py:52
  3.4 19.0 %all_to_all.20.refs_0_ = bf16[32,32,128]{2,1,0:T(8,128)(2,1)S(1)} all-to-all(bf16[32,32,128]{2,1,0:T(8,128)(2,1)S(1)} %get-tuple-element.7), channel_id=1, replica_groups=mesh['l'=2,'y2'=2,'y1'=2,'yl'=2,'xl'=2,'xh'=2,'zh'=4,'zl'=2] {'y1','yl',..., dimensions={0} | all-to-all | bytes 524288 | tf_op jit(solution)/shard_map/all_to_all | solution.py:129
  22.4 6.6 %all-to-all-start.1 = ((bf16[64,72,128]{2,1,0:T(8,128)(2,1)}), bf16[64,72,128]{2,1,0:T(8,128)(2,1)S(1)}, u32[]{:S(2)}, u32[]{:S(2)}) async-start(bf16[64,72,128]{2,1,0:T(8,128)(2,1)} %get-tuple-element.8), calls=%async_computation.1 | async-start | bytes 2359296 | tf_op jit(solution)/shard_map/all_to_all | solution.py:128
  29.0 9.8 %collective-permute-start.2 = (bf16[32,32,128]{2,1,0:T(8,128)(2,1)S(1)}, bf16[32,32,128]{2,1,0:T(8,128)(2,1)S(1)}, u32[]{:S(2)}, u32[]{:S(2)}) collective-permute-start(bf16[32,32,128]{2,1,0:T(8,128)(2,1)S(1)} %all_to_all.20.refs_0_), channel_id=1, source_target_pairs={{0,6},{2,4},{4,2},{6,0},{1,7},{3,5},{5,3},{7,1},{8,14},{10,12},{12... | collective-permute-start | bytes 786440 | tf_op jit(solution)/shard_map/ppermute | solution.py:130
  38.8 1.9 %collective-permute-start.1 = (bf16[32,32,128]{2,1,0:T(8,128)(2,1)S(1)}, bf16[32,32,128]{2,1,0:T(8,128)(2,1)S(1)}, u32[]{:S(2)}, u32[]{:S(2)}) collective-permute-start(bf16[32,32,128]{2,1,0:T(8,128)(2,1)S(1)} %all_to_all.20.refs_0_), channel_id=1, source_target_pairs={{0,4},{2,6},{4,0},{6,2},{1,5},{3,7},{5,1},{7,3},{8,12},{10,14},{12... | collective-permute-start | bytes 786440 | tf_op jit(solution)/shard_map/ppermute | solution.py:130
  40.7 4.0 %collective-permute-start = (bf16[32,32,128]{2,1,0:T(8,128)(2,1)S(1)}, bf16[32,32,128]{2,1,0:T(8,128)(2,1)S(1)}, u32[]{:S(2)}, u32[]{:S(2)}) collective-permute-start(bf16[32,32,128]{2,1,0:T(8,128)(2,1)S(1)} %all_to_all.20.refs_0_), channel_id=1, source_target_pairs={{0,2},{2,0},{4,6},{6,4},{1,3},{3,1},{5,7},{7,5},{8,10},{10,8},{12,... | collective-permute-start | bytes 786440 | tf_op jit(solution)/shard_map/ppermute | solution.py:130
  44.7 21.2 %collective-permute-done.2.refs_3_ = bf16[32,32,128]{2,1,0:T(8,128)(2,1)S(1)} collective-permute-done((bf16[32,32,128]{2,1,0:T(8,128)(2,1)S(1)}, bf16[32,32,128]{2,1,0:T(8,128)(2,1)S(1)}, u32[]{:S(2)}, u32[]{:S(2)}) %collective-permute-start.2) | collective-permute-done | bytes 262176 | tf_op jit(solution)/shard_map/ppermute | solution.py:130
  65.9 0.0 collective-permute-done.1.refs_2_
  65.9 0.0 collective-permute-done.refs_1_
  65.9 0.0 all-to-all-done.1.refs_4_
  65.9 1.4 %shard_map.56 = f32[16,2,56,128]{3,2,1,0:T(8,128)S(1)} custom-call(s32[1]{0:T(128)} %bitcast.my_zh_ref, bf16[32,32,128]{2,1,0:T(8,128)(2,1)S(1)} %all_to_all.20.refs_0_, bf16[32,32,128]{2,1,0:T(8,128)(2,1)S(1)} %collective-permute-done.refs_1_, bf16[32,32,128]{2,1,0:T(8,128)(2,1)S(1)} %collective-permute-done.1.refs_2_, ...), custom_call_target="tpu_custom_call" | custom-call | tf_op jit(solution)/shard_map/pallas_call | solution.py:112
  67.2 22.7 %all_to_all.21 = f32[16,2,56,128]{3,2,1,0:T(8,128)S(1)} all-to-all(f32[16,2,56,128]{3,2,1,0:T(8,128)S(1)} %shard_map.56), channel_id=1, replica_groups=mesh['l'=2,'y2'=2,'y1'=2,'yl'=2,'xl'=2,'xh'=2,'zh'=4,'zl'=2] {'yl','xl',..., dimensions={0} | all-to-all | bytes 1835008 | tf_op jit(solution)/shard_map/all_to_all | solution.py:132
  90.0 0.0 copy-start.2
  90.0 0.0 copy-start.3
  90.0 0.0 copy-start.4
  90.0 0.1 reduce_sum.18
  90.0 12.4 %all_to_all.22 = f32[4,56,128]{2,1,0:T(8,128)S(1)} all-to-all(f32[4,56,128]{2,1,0:T(8,128)S(1)} %pad_maximum_fusion), channel_id=1, replica_groups=mesh['l'=2,'y2'=2,'y1'=2,'yl'=2,'xl'=2,'xh'=2,'zh'=4,'zl'=2] {'l','y1'}, dimensions={0} | all-to-all | bytes 229376 | tf_op jit(solution)/shard_map/all_to_all | solution.py:134
  102.5 0.0 copy-done.2
  102.5 0.0 copy-done.3
  102.5 0.0 copy-done.4
  102.5 0.7 subtract_divide_fusion
  (2 shorter events, 0.0 us)
Async XLA Ops:
  0.0 1.1 %copy-start = (bf16[2304,128]{1,0:T(8,128)(2,1)S(1)}, bf16[2304,128]{1,0:T(8,128)(2,1)}, u32[]{:S(2)}) copy-start(bf16[2304,128]{1,0:T(8,128)(2,1)} %b_ref.1) | copy-start | bytes 1769476
  1.1 0.9 copy-start.1
  22.4 43.5 %all-to-all-start.1 = ((bf16[64,72,128]{2,1,0:T(8,128)(2,1)}), bf16[64,72,128]{2,1,0:T(8,128)(2,1)S(1)}, u32[]{:S(2)}, u32[]{:S(2)}) async-start(bf16[64,72,128]{2,1,0:T(8,128)(2,1)} %get-tuple-element.8), calls=%async_computation.1 | async-start | bytes 2359296 | tf_op jit(solution)/shard_map/all_to_all | solution.py:128
  29.0 36.8 %collective-permute-start.2 = (bf16[32,32,128]{2,1,0:T(8,128)(2,1)S(1)}, bf16[32,32,128]{2,1,0:T(8,128)(2,1)S(1)}, u32[]{:S(2)}, u32[]{:S(2)}) collective-permute-start(bf16[32,32,128]{2,1,0:T(8,128)(2,1)S(1)} %all_to_all.20.refs_0_), channel_id=1, source_target_pairs={{0,6},{2,4},{4,2},{6,0},{1,7},{3,5},{5,3},{7,1},{8,14},{10,12},{12... | collective-permute-start | bytes 786440 | tf_op jit(solution)/shard_map/ppermute | solution.py:130
  38.8 27.1 %collective-permute-start.1 = (bf16[32,32,128]{2,1,0:T(8,128)(2,1)S(1)}, bf16[32,32,128]{2,1,0:T(8,128)(2,1)S(1)}, u32[]{:S(2)}, u32[]{:S(2)}) collective-permute-start(bf16[32,32,128]{2,1,0:T(8,128)(2,1)S(1)} %all_to_all.20.refs_0_), channel_id=1, source_target_pairs={{0,4},{2,6},{4,0},{6,2},{1,5},{3,7},{5,1},{7,3},{8,12},{10,14},{12... | collective-permute-start | bytes 786440 | tf_op jit(solution)/shard_map/ppermute | solution.py:130
  40.7 25.2 %collective-permute-start = (bf16[32,32,128]{2,1,0:T(8,128)(2,1)S(1)}, bf16[32,32,128]{2,1,0:T(8,128)(2,1)S(1)}, u32[]{:S(2)}, u32[]{:S(2)}) collective-permute-start(bf16[32,32,128]{2,1,0:T(8,128)(2,1)S(1)} %all_to_all.20.refs_0_), channel_id=1, source_target_pairs={{0,2},{2,0},{4,6},{6,4},{1,3},{3,1},{5,7},{7,5},{8,10},{10,8},{12,... | collective-permute-start | bytes 786440 | tf_op jit(solution)/shard_map/ppermute | solution.py:130
  90.0 12.5 %copy-start.2 = (f32[56,128]{1,0:T(8,128)S(1)}, f32[56,128]{1,0:T(8,128)}, u32[]{:S(2)}) copy-start(f32[56,128]{1,0:T(8,128)} %param.7) | copy-start | bytes 86020
  90.0 12.5 %copy-start.3 = (f32[128]{0:T(128)S(1)}, f32[128]{0:T(128)}, u32[]{:S(2)}) copy-start(f32[128]{0:T(128)} %param.9) | copy-start | bytes 1540
  90.0 12.5 %copy-start.4 = (f32[56]{0:T(128)S(1)}, f32[56]{0:T(128)}, u32[]{:S(2)}) copy-start(f32[56]{0:T(128)} %param.8) | copy-start | bytes 676

commit v5 on v2

--- a/solution.py
+++ b/solution.py
@@ -18,7 +18,7 @@
 VMEM = 40 * 1024 * 1024
 
 
-def pack_kernel(a_ref, b_ref, out_ref):
+def pack_a_kernel(a_ref, out_ref):
     lane_group = lax.broadcasted_iota(jnp.int32, (8, LANES), 1) // REST
     tail = a_ref[:, MAIN:].astype(jnp.float32)
     for s in range(PIECES):
@@ -30,19 +30,25 @@
             shift = REST * (g - place) % LANES
             moved = pltpu.roll(tile, shift, 1) if shift else tile
             rest = jnp.where(lane_group == g, moved, rest)
-        out_ref[s, 0:A_ROWS, :] = jnp.concatenate([main, rest], axis=0).astype(jnp.bfloat16)
-        out_ref[s, A_ROWS : A_ROWS + LANES, :] = b_ref[s * LANES : (s + 1) * LANES, :]
-        out_ref[s, A_ROWS + LANES :, :] = b_ref[MAIN + s * REST : MAIN + (s + 1) * REST, :]
+        out_ref[s] = jnp.concatenate([main, rest], axis=0).astype(jnp.bfloat16)
 
 
-def pack(a, b):
+def pack_b_kernel(b_ref, out_ref):
+    for s in range(PIECES):
+        for far in range(4):
+            out_ref[far, s, 0:LANES, :] = b_ref[s * LANES : (s + 1) * LANES, :]
+            out_ref[far, s, LANES:, :] = b_ref[MAIN + s * REST : MAIN + (s + 1) * REST, :]
+
+
+def pack(kernel, block, shape):
     return pl.pallas_call(
-        pack_kernel,
-        out_shape=jax.ShapeDtypeStruct((PIECES, A_ROWS + B_ROWS, LANES), jnp.bfloat16),
-        in_specs=[pl.BlockSpec(memory_space=pltpu.VMEM)] * 2,
+        kernel,
+        out_shape=jax.ShapeDtypeStruct(shape, jnp.bfloat16),
+        in_specs=[pl.BlockSpec(memory_space=pltpu.VMEM)],
         out_specs=pl.BlockSpec(memory_space=pltpu.VMEM),
+        cost_estimate=pl.CostEstimate(flops=0, bytes_accessed=8 * block.size, transcendentals=0),
         compiler_params=pltpu.CompilerParams(vmem_limit_bytes=VMEM),
-    )(a, b)
+    )(block)
 
 
 def multiply_kernel(my_zh_ref, *refs):
@@ -100,10 +106,11 @@
 
 
 def body(amplitudes, integrals, other_terms, occ_energy, virt_energy):
-    pieces = lax.all_to_all(pack(amplitudes, integrals), NEAR, 0, 0, tiled=True)
-    a, b = pieces[:, :A_ROWS], pieces[:, A_ROWS:]
+    a = pack(pack_a_kernel, amplitudes, (PIECES, A_ROWS, LANES))
+    b = pack(pack_b_kernel, integrals, (4, PIECES, B_ROWS, LANES))
+    b_slots = lax.all_to_all(b.reshape((4 * PIECES,) + b.shape[2:]), ("yh",) + NEAR, 0, 0, tiled=True).reshape(b.shape)
+    a = lax.all_to_all(a, NEAR, 0, 0, tiled=True)
     a_slots = [a] + [lax.ppermute(a, "zh", [(i, i ^ d) for i in range(4)]) for d in (1, 2, 3)]
-    b_slots = lax.all_to_all(jnp.broadcast_to(b[None], (4,) + b.shape), "yh", 0, 0, tiled=True)
     my_zh = lax.axis_index("zh").astype(jnp.int32)[None]
     partial = multiply(my_zh, a_slots, b_slots)
     partial = lax.all_to_all(partial, NEAR, 0, 0, tiled=True)

time: 106 us -> 101 us (0.953)
  blocking collectives: 39.1 us -> 16.9 us
  starting transfers between devices: 22.4 us -> 31.7 us
  waiting for transfers between devices: 38.3 us -> 45.5 us
    ppermute x3, waiting for transfers between devices: 21.8 us -> 41.6 us  [body(): lax.ppermute(a, 'zh', [(i, i ^ d) for i in range(4)])]
    all_to_all x1 -> x0, blocking collectives: 19.3 us -> none  [body(): pieces = lax.all_to_all(pack(amplitudes, integrals), NEAR, 0, 0, tiled=True)]
    all_to_all x1 -> x2, waiting for transfers between devices: 16.5 us -> 3.92 us  [the longest x1 3.92 us: body(): a = lax.all_to_all(a, NEAR, 0, 0, tiled=True)]
    all_to_all x1 -> x2, starting transfers between devices: 6.76 us -> 16 us  [the longest x1 8.23 us: body(): lax.all_to_all(b.reshape((4 * PIECES,) + b.shape[2:]), ('yh',) + NEAR, 0,...]
    all_to_all x1, blocking collectives: 13.8 us -> 10.2 us  [body(): partial = lax.all_to_all(partial, NEAR, 0, 0, tiled=True)]
    broadcast_in_dim x1 -> x0, local copies, waits for them, and re-layouts: 1.72 us -> none  [body(): jnp.broadcast_to(b[None], (4,) + b.shape)]
    unnamed x10 -> x12, local copies, waits for them, and re-layouts: 2.02 us -> 3.41 us
  transfers between devices with their start and end apart: 4 -> 5, of which waited for: 3 -> 3; matrix products, arithmetic and copies ran while one was open for 0% -> 0% of each run, Pallas kernels for 0% -> 0%
where the time goes in v5:
time: 101 us
  waiting for transfers between devices  45.5 us (45%)
  starting transfers between devices  31.7 us (31%)
  blocking collectives  16.9 us (17%)
  local copies, waits for them, and re-layouts  3.41 us (3%)
  Pallas kernels  2.23 us (2%)
    ppermute x3, waiting for transfers between devices, body(): lax.ppermute(a, 'zh', [(i, i ^ d) for i in range(4)])  41.6 us
    ppermute x3, starting transfers between devices, body(): lax.ppermute(a, 'zh', [(i, i ^ d) for i in range(4)])  15.7 us
    all_to_all x1, blocking collectives, body(): partial = lax.all_to_all(partial, NEAR, 0, 0, tiled=True)  10.2 us
    all_to_all x1, starting transfers between devices, body(): lax.all_to_all(b.reshape((4 * PIECES,) + b.shape[2:]), ('yh',) + NEAR, 0,...  8.23 us
    all_to_all x1, starting transfers between devices, body(): a = lax.all_to_all(a, NEAR, 0, 0, tiled=True)  7.77 us
    psum x1, blocking collectives, body(): ladder = lax.psum(jnp.sum(partial, axis=0), 'l')  6.75 us
    all_to_all x1, waiting for transfers between devices, body(): a = lax.all_to_all(a, NEAR, 0, 0, tiled=True)  3.92 us
    unnamed x12, local copies, waits for them, and re-layouts  3.41 us
  transfers between devices with their start and end apart: 5, of which 3 were waited for; matrix products, arithmetic and copies ran while one was open for 0% of the time, Pallas kernels for 0%

profile of v5, /device:TPU:1, one launch (start us, length us, event | category | flops | bytes accessed | tf_op | source)
XLA Modules:
  0.0 100.6 jit_solution(2468871771554038870)
XLA Ops:
  0.0 0.0 copy-start.2
  0.0 0.9 copy-done.2
  0.9 0.8 shard_map.55
  1.8 7.8 %all-to-all-start = ((bf16[16,64,128]{2,1,0:T(8,128)(2,1)}), bf16[16,64,128]{2,1,0:T(8,128)(2,1)S(1)}, u32[]{:S(2)}, u32[]{:S(2)}) async-start(bf16[16,64,128]{2,1,0:T(8,128)(2,1)} %shard_map.55), calls=%async_computation | async-start | bytes 524288 | tf_op jit(solution)/shard_map/all_to_all | solution.py:112
  9.6 0.0 copy-start.1
  9.6 1.1 %copy-done.1 = bf16[2304,128]{1,0:T(8,128)(2,1)S(1)} copy-done((bf16[2304,128]{1,0:T(8,128)(2,1)S(1)}, bf16[2304,128]{1,0:T(8,128)(2,1)}, u32[]{:S(2)}) %copy-start.1) | copy-done | bytes 589848
  10.6 0.3 shard_map.56
  10.9 0.0 copy-start
  10.9 1.4 %copy-done = bf16[4,16,144,128]{3,2,1,0:T(8,128)(2,1)} copy-done((bf16[4,16,144,128]{3,2,1,0:T(8,128)(2,1)}, bf16[4,16,144,128]{3,2,1,0:T(8,128)(2,1)S(1)}, u32[]{:S(2)}) %copy-start) | copy-done | bytes 2359320
  12.3 3.9 %all-to-all-done.refs_0_ = bf16[16,64,128]{2,1,0:T(8,128)(2,1)S(1)} async-done(((bf16[16,64,128]{2,1,0:T(8,128)(2,1)}), bf16[16,64,128]{2,1,0:T(8,128)(2,1)S(1)}, u32[]{:S(2)}, u32[]{:S(2)}) %all-to-all-start) | async-done | bytes 262176 | tf_op jit(solution)/shard_map/all_to_all | solution.py:112
  16.3 8.2 %all-to-all-start.1 = ((bf16[64,144,128]{2,1,0:T(8,128)(2,1)}), bf16[64,144,128]{2,1,0:T(8,128)(2,1)S(1)}, u32[]{:S(2)}, u32[]{:S(2)}) async-start(bf16[64,144,128]{2,1,0:T(8,128)(2,1)} %bitcast.4), calls=%async_computation.1 | async-start | bytes 4718592 | tf_op jit(solution)/shard_map/all_to_all | solution.py:111
  24.5 5.8 %collective-permute-start = (bf16[16,64,128]{2,1,0:T(8,128)(2,1)S(1)}, bf16[16,64,128]{2,1,0:T(8,128)(2,1)S(1)}, u32[]{:S(2)}, u32[]{:S(2)}) collective-permute-start(bf16[16,64,128]{2,1,0:T(8,128)(2,1)S(1)} %all-to-all-done.refs_0_), channel_id=1, source_target_pairs={{0,2},{2,0},{4,6},{6,4},{1,3},{3,1},{5,7},{7,5},{8,10},{10,8},{12,... | collective-permute-start | bytes 786440 | tf_op jit(solution)/shard_map/ppermute | solution.py:113
  30.3 7.9 %collective-permute-start.1 = (bf16[16,64,128]{2,1,0:T(8,128)(2,1)S(1)}, bf16[16,64,128]{2,1,0:T(8,128)(2,1)S(1)}, u32[]{:S(2)}, u32[]{:S(2)}) collective-permute-start(bf16[16,64,128]{2,1,0:T(8,128)(2,1)S(1)} %all-to-all-done.refs_0_), channel_id=1, source_target_pairs={{0,4},{2,6},{4,0},{6,2},{1,5},{3,7},{5,1},{7,3},{8,12},{10,14},{12... | collective-permute-start | bytes 786440 | tf_op jit(solution)/shard_map/ppermute | solution.py:113
  38.3 1.9 %collective-permute-start.2 = (bf16[16,64,128]{2,1,0:T(8,128)(2,1)S(1)}, bf16[16,64,128]{2,1,0:T(8,128)(2,1)S(1)}, u32[]{:S(2)}, u32[]{:S(2)}) collective-permute-start(bf16[16,64,128]{2,1,0:T(8,128)(2,1)S(1)} %all-to-all-done.refs_0_), channel_id=1, source_target_pairs={{0,6},{2,4},{4,2},{6,0},{1,7},{3,5},{5,3},{7,1},{8,14},{10,12},{12... | collective-permute-start | bytes 786440 | tf_op jit(solution)/shard_map/ppermute | solution.py:113
  40.2 0.0 collective-permute-done.refs_1_
  40.2 38.2 %collective-permute-done.1.refs_2_ = bf16[16,64,128]{2,1,0:T(8,128)(2,1)S(1)} collective-permute-done((bf16[16,64,128]{2,1,0:T(8,128)(2,1)S(1)}, bf16[16,64,128]{2,1,0:T(8,128)(2,1)S(1)}, u32[]{:S(2)}, u32[]{:S(2)}) %collective-permute-start.1) | collective-permute-done | bytes 262176 | tf_op jit(solution)/shard_map/ppermute | solution.py:113
  78.4 3.4 %collective-permute-done.2.refs_3_ = bf16[16,64,128]{2,1,0:T(8,128)(2,1)S(1)} collective-permute-done((bf16[16,64,128]{2,1,0:T(8,128)(2,1)S(1)}, bf16[16,64,128]{2,1,0:T(8,128)(2,1)S(1)}, u32[]{:S(2)}, u32[]{:S(2)}) %collective-permute-start.2) | collective-permute-done | bytes 262176 | tf_op jit(solution)/shard_map/ppermute | solution.py:113
  81.8 0.0 all-to-all-done.1
  81.8 0.0 copy-start.3
  81.8 0.0 copy-start.4
  81.8 0.0 copy-start.5
  81.8 1.1 %shard_map.57 = f32[16,56,128]{2,1,0:T(8,128)S(1)} custom-call(s32[1]{0:T(128)} %bitcast.my_zh_ref, bf16[16,64,128]{2,1,0:T(8,128)(2,1)S(1)} %all-to-all-done.refs_0_, bf16[16,64,128]{2,1,0:T(8,128)(2,1)S(1)} %collective-permute-done.refs_1_, bf16[16,64,128]{2,1,0:T(8,128)(2,1)S(1)} %collective-permute-done.1.refs_2_, ...), custom_call_target="tpu_custom_call" | custom-call | tf_op jit(solution)/shard_map/pallas_call | solution.py:94
  82.9 10.2 %all_to_all.15 = f32[16,56,128]{2,1,0:T(8,128)S(1)} all-to-all(f32[16,56,128]{2,1,0:T(8,128)S(1)} %shard_map.57), channel_id=1, replica_groups=mesh['l'=2,'yh'=4,'yl'=2,'xl'=2,'xh'=2,'zh'=4,'zl'=2] {'yl','xl','xh','zl'}, dimensions={0} | all-to-all | bytes 917504 | tf_op jit(solution)/shard_map/all_to_all | solution.py:116
  93.1 6.7 %psum.7 = f32[56,128]{1,0:T(8,128)S(1)} all-reduce(f32[56,128]{1,0:T(8,128)S(1)} %reduce_sum.9), channel_id=1, replica_groups=mesh['l'=2,'yh'=4,'yl'=2,'xl'=2,'xh'=2,'zh'=4,'zl'=2] {'l'}, use_global_device_ids=true, to_apply=%region_1.0 | all-reduce | flops 7168 | bytes 57344 | tf_op jit(solution)/shard_map/psum | solution.py:117
  99.9 0.0 copy-done.3
  99.9 0.0 copy-done.4
  99.9 0.0 copy-done.5
  99.9 0.7 subtract_divide_fusion
  (1 shorter events, 0.0 us)
Async XLA Ops:
  0.0 0.9 copy-start.2
  1.8 14.5 %all-to-all-start = ((bf16[16,64,128]{2,1,0:T(8,128)(2,1)}), bf16[16,64,128]{2,1,0:T(8,128)(2,1)S(1)}, u32[]{:S(2)}, u32[]{:S(2)}) async-start(bf16[16,64,128]{2,1,0:T(8,128)(2,1)} %shard_map.55), calls=%async_computation | async-start | bytes 524288 | tf_op jit(solution)/shard_map/all_to_all | solution.py:112
  9.6 1.1 %copy-start.1 = (bf16[2304,128]{1,0:T(8,128)(2,1)S(1)}, bf16[2304,128]{1,0:T(8,128)(2,1)}, u32[]{:S(2)}) copy-start(bf16[2304,128]{1,0:T(8,128)(2,1)} %b_ref.1) | copy-start | bytes 1769476
  10.9 1.4 %copy-start = (bf16[4,16,144,128]{3,2,1,0:T(8,128)(2,1)}, bf16[4,16,144,128]{3,2,1,0:T(8,128)(2,1)S(1)}, u32[]{:S(2)}) copy-start(bf16[4,16,144,128]{3,2,1,0:T(8,128)(2,1)S(1)} %shard_map.56) | copy-start | bytes 7077892
  16.3 65.5 %all-to-all-start.1 = ((bf16[64,144,128]{2,1,0:T(8,128)(2,1)}), bf16[64,144,128]{2,1,0:T(8,128)(2,1)S(1)}, u32[]{:S(2)}, u32[]{:S(2)}) async-start(bf16[64,144,128]{2,1,0:T(8,128)(2,1)} %bitcast.4), calls=%async_computation.1 | async-start | bytes 4718592 | tf_op jit(solution)/shard_map/all_to_all | solution.py:111
  24.5 15.7 %collective-permute-start = (bf16[16,64,128]{2,1,0:T(8,128)(2,1)S(1)}, bf16[16,64,128]{2,1,0:T(8,128)(2,1)S(1)}, u32[]{:S(2)}, u32[]{:S(2)}) collective-permute-start(bf16[16,64,128]{2,1,0:T(8,128)(2,1)S(1)} %all-to-all-done.refs_0_), channel_id=1, source_target_pairs={{0,2},{2,0},{4,6},{6,4},{1,3},{3,1},{5,7},{7,5},{8,10},{10,8},{12,... | collective-permute-start | bytes 786440 | tf_op jit(solution)/shard_map/ppermute | solution.py:113
  30.3 48.1 %collective-permute-start.1 = (bf16[16,64,128]{2,1,0:T(8,128)(2,1)S(1)}, bf16[16,64,128]{2,1,0:T(8,128)(2,1)S(1)}, u32[]{:S(2)}, u32[]{:S(2)}) collective-permute-start(bf16[16,64,128]{2,1,0:T(8,128)(2,1)S(1)} %all-to-all-done.refs_0_), channel_id=1, source_target_pairs={{0,4},{2,6},{4,0},{6,2},{1,5},{3,7},{5,1},{7,3},{8,12},{10,14},{12... | collective-permute-start | bytes 786440 | tf_op jit(solution)/shard_map/ppermute | solution.py:113
  38.3 43.5 %collective-permute-start.2 = (bf16[16,64,128]{2,1,0:T(8,128)(2,1)S(1)}, bf16[16,64,128]{2,1,0:T(8,128)(2,1)S(1)}, u32[]{:S(2)}, u32[]{:S(2)}) collective-permute-start(bf16[16,64,128]{2,1,0:T(8,128)(2,1)S(1)} %all-to-all-done.refs_0_), channel_id=1, source_target_pairs={{0,6},{2,4},{4,2},{6,0},{1,7},{3,5},{5,3},{7,1},{8,14},{10,12},{12... | collective-permute-start | bytes 786440 | tf_op jit(solution)/shard_map/ppermute | solution.py:113
  81.8 18.1 %copy-start.3 = (f32[56,128]{1,0:T(8,128)S(1)}, f32[56,128]{1,0:T(8,128)}, u32[]{:S(2)}) copy-start(f32[56,128]{1,0:T(8,128)} %param.7) | copy-start | bytes 86020
  81.8 18.1 %copy-start.4 = (f32[128]{0:T(128)S(1)}, f32[128]{0:T(128)}, u32[]{:S(2)}) copy-start(f32[128]{0:T(128)} %param.9) | copy-start | bytes 1540
  81.8 18.1 %copy-start.5 = (f32[56]{0:T(128)S(1)}, f32[56]{0:T(128)}, u32[]{:S(2)}) copy-start(f32[56]{0:T(128)} %param.8) | copy-start | bytes 676

commit v6 on v5

v6 whole, which is shorter than its diff:
```python
import jax
import jax.numpy as jnp
from jax import lax
from jax.experimental import pallas as pl
from jax.experimental.pallas import tpu as pltpu
from jax.sharding import Mesh
from jax.sharding import PartitionSpec as P

PARTS = {"l": 2, "yh": 4, "yl": 2, "xl": 2, "xh": 2, "zh": 4, "zl": 2}
NEAR = ("yl", "xl", "xh")
PIECES = 8
BLOCKS = 16
ROWS = 56
LANES = 128
WIDE = 2 * LANES
REST = 32
MAIN = PIECES * WIDE
GROUPS = ROWS // 8
PLACES = LANES // REST
A_ROWS = 128
B_ROWS = WIDE + REST
R_ROWS = 64
VMEM = 40 * 1024 * 1024
f32, bf16 = jnp.float32, jnp.bfloat16


def rolled(x, shift):
    return pltpu.roll(x, shift % LANES, 1) if shift % LANES else x


def pack_a_kernel(a_ref, out_ref):
    lane_group = lax.broadcasted_iota(jnp.int32, (8, LANES), 1) // REST
    tail = a_ref[:, MAIN:].astype(f32)
    for s in range(PIECES):
        parts = [a_ref[:, (2 * s + i) * LANES : (2 * s + i + 1) * LANES].astype(f32) for i in range(2)]
        half, place = divmod(s, PLACES)
        rest = [jnp.zeros((8, LANES), f32)] * 2
        for g in range(GROUPS):
            q, u = divmod(g, PLACES)
            tile = tail[8 * g : 8 * g + 8, half * LANES : (half + 1) * LANES]
            rest[q] = jnp.where(lane_group == u, rolled(tile, REST * (u - place)), rest[q])
        piece = jnp.concatenate(parts + rest, axis=0).astype(bf16)
        for zl in range(2):
            out_ref[2 * s + zl] = piece


def pack_b_kernel(b_ref, out_ref):
    for s in range(PIECES):
        for far in range(4):
            out_ref[far * PIECES + s, 0:WIDE, :] = b_ref[s * WIDE : (s + 1) * WIDE, :]
            out_ref[far * PIECES + s, WIDE:, :] = b_ref[MAIN + s * REST : MAIN + (s + 1) * REST, :]


def pack(kernel, block, shape):
    return pl.pallas_call(
        kernel,
        out_shape=jax.ShapeDtypeStruct(shape, bf16),
        in_specs=[pl.BlockSpec(memory_space=pltpu.VMEM)],
        out_specs=pl.BlockSpec(memory_space=pltpu.VMEM),
        cost_estimate=pl.CostEstimate(flops=0, bytes_accessed=8 * block.size, transcendentals=0),
        compiler_params=pltpu.CompilerParams(vmem_limit_bytes=VMEM),
    )(block)


def multiply_kernel(my_zh_ref, *refs):
    a_refs, (b_ref, out_ref, left, right, spread) = refs[:4], refs[4:]
    my_zh = my_zh_ref[0]
    lane_group = lax.broadcasted_iota(jnp.int32, (4 * 8, LANES), 1) // REST
    main = BLOCKS * WIDE
    corners = []
    for t in range(BLOCKS):
        flip, b3, b0 = t >> 2, (t >> 1) & 1, t & 1
        block = 8 * b3 + 2 * (my_zh ^ flip) + b0
        corner = [[], []]
        for r in range(4):
            piece = a_refs[flip][4 * r + 2 * b3 + b0]
            wide = piece.astype(f32)
            rows = slice(R_ROWS * r, R_ROWS * (r + 1))
            left[rows, t * WIDE : t * WIDE + LANES] = piece[:R_ROWS]
            left[rows, t * WIDE + LANES : (t + 1) * WIDE] = wide[ROWS : ROWS + R_ROWS].astype(bf16)
            corner[0].append(wide[2 * ROWS : 2 * ROWS + 8])
            corner[1].append(wide[2 * ROWS + 8 :])
        corners.append([jnp.concatenate(c, axis=0) for c in corner])
        for c in range(2):
            columns = slice(c * LANES, (c + 1) * LANES)
            right[t * WIDE : (t + 1) * WIDE, columns] = b_ref[2 * block + c, 0:WIDE, :]
            right[main + t * REST : main + (t + 1) * REST, columns] = b_ref[2 * block + c, WIDE:, :]
    spread[...] = jnp.zeros_like(spread)
    for tile in range(BLOCKS // PLACES):
        for g in range(GROUPS):
            q, u = divmod(g, PLACES)
            rest = jnp.zeros((4 * 8, LANES), f32)
            for place in range(PLACES):
                moved = rolled(corners[PLACES * tile + place][q], REST * (place - u))
                rest = jnp.where(lane_group == place, moved, rest)
            for r in range(4):
                spread[R_ROWS * r + 8 * g : R_ROWS * r + 8 * g + 8, tile * LANES : (tile + 1) * LANES] = rest[8 * r : 8 * r + 8]
    left[:, main:] = spread[...].astype(bf16)
    total = jnp.dot(left[...], right[...], preferred_element_type=f32)
    for r in range(4):
        for c in range(2):
            out_ref[2 * r + c] = total[R_ROWS * r : R_ROWS * r + ROWS, c * LANES : (c + 1) * LANES]


def multiply(my_zh, a_slots, b_slots):
    depth = BLOCKS * B_ROWS
    return pl.pallas_call(
        multiply_kernel,
        out_shape=jax.ShapeDtypeStruct((PIECES, ROWS, LANES), f32),
        in_specs=[pl.BlockSpec(memory_space=pltpu.SMEM)] + [pl.BlockSpec(memory_space=pltpu.VMEM)] * 5,
        out_specs=pl.BlockSpec(memory_space=pltpu.VMEM),
        scratch_shapes=[
            pltpu.VMEM((4 * R_ROWS, depth), bf16),
            pltpu.VMEM((depth, 2 * LANES), bf16),
            pltpu.VMEM((4 * R_ROWS, BLOCKS * REST), f32),
        ],
        compiler_params=pltpu.CompilerParams(vmem_limit_bytes=VMEM),
    )(my_zh, *a_slots, b_slots)


def body(amplitudes, integrals, other_terms, occ_energy, virt_energy):
    a = pack(pack_a_kernel, amplitudes, (2 * PIECES, A_ROWS, LANES))
    b = pack(pack_b_kernel, integrals, (4 * PIECES, B_ROWS, LANES))
    b_slots = lax.all_to_all(b, ("yh",) + NEAR, 0, 0, tiled=True)
    a = lax.all_to_all(a, NEAR + ("zl",), 0, 0, tiled=True)
    a_slots = [a] + [lax.ppermute(a, "zh", [(i, i ^ d) for i in range(4)]) for d in (1, 2, 3)]
    my_zh = lax.axis_index("zh").astype(jnp.int32)[None]
    partial = multiply(my_zh, a_slots, b_slots)
    partial = lax.all_to_all(partial, NEAR, 0, 0, tiled=True)
    ladder = lax.psum(jnp.sum(partial, axis=0), "l")
    denominator = occ_energy[:, None] - virt_energy[None, :]
    return (ladder + other_terms) / denominator


def solution(mesh):
    fine = Mesh(mesh.devices.reshape(tuple(PARTS.values())), tuple(PARTS))
    row, col = ("yh", "yl", "xl"), ("xh", "zh", "zl")
    in_specs = (P(row, ("l",) + col), P(("l",) + row, col), P(row, col), P(row), P(col))
    return jax.shard_map(body, mesh=fine, in_specs=in_specs, out_specs=P(row, col), check_vma=False)
```

time: 101 us -> 106 us (1.050)
  blocking collectives: 16.9 us -> 23 us
  waiting for transfers between devices: 45.5 us -> 41.5 us
  Pallas kernels: 2.23 us -> 3.83 us
    ppermute x3, waiting for transfers between devices: 41.6 us -> 35.8 us  [body(): lax.ppermute(a, 'zh', [(i, i ^ d) for i in range(4)])]
    psum x1, blocking collectives: 6.75 us -> 11 us  [body(): ladder = lax.psum(jnp.sum(partial, axis=0), 'l')]
    all_to_all x1, blocking collectives: 10.2 us -> 12 us  [body(): partial = lax.all_to_all(partial, NEAR, 0, 0, tiled=True)]
    all_to_all x2, waiting for transfers between devices: 3.92 us -> 5.69 us  [the longest x1 5.04 us: body(): a = lax.all_to_all(a, NEAR + ('zl',), 0, 0, tiled=True)]
    pallas_call x1, Pallas kernels: 1.1 us -> 2.64 us  [multiply(): pl.pallas_call(multiply_kernel, out_shape=jax.ShapeDtypeStruct((PIECES, R...]
where the time goes in v6:
time: 106 us; the launch traced here: 105 us
  waiting for transfers between devices  41.5 us (39%)
  starting transfers between devices  32.5 us (31%)
  blocking collectives  23 us (22%)
  Pallas kernels  3.83 us (4%)
  local copies, waits for them, and re-layouts  3.41 us (3%)
    ppermute x3, waiting for transfers between devices, body(): lax.ppermute(a, 'zh', [(i, i ^ d) for i in range(4)])  35.8 us
    ppermute x3, starting transfers between devices, body(): lax.ppermute(a, 'zh', [(i, i ^ d) for i in range(4)])  15.7 us
    all_to_all x1, blocking collectives, body(): partial = lax.all_to_all(partial, NEAR, 0, 0, tiled=True)  12 us
    psum x1, blocking collectives, body(): ladder = lax.psum(jnp.sum(partial, axis=0), 'l')  11 us
    all_to_all x1, starting transfers between devices, body(): b_slots = lax.all_to_all(b, ('yh',) + NEAR, 0, 0, tiled=True)  9.07 us
    all_to_all x1, starting transfers between devices, body(): a = lax.all_to_all(a, NEAR + ('zl',), 0, 0, tiled=True)  7.77 us
    all_to_all x1, waiting for transfers between devices, body(): a = lax.all_to_all(a, NEAR + ('zl',), 0, 0, tiled=True)  5.04 us
    unnamed x12, local copies, waits for them, and re-layouts  3.41 us
  transfers between devices with their start and end apart: 5, of which 3 were waited for; matrix products, arithmetic and copies ran while one was open for 0% of the time, Pallas kernels for 0%

profile of v6, /device:TPU:1, one launch (start us, length us, event | category | flops | bytes accessed | tf_op | source)
XLA Modules:
  0.0 105.1 jit_solution(14327333678644409317)
XLA Ops:
  0.0 0.0 copy-start.2
  0.0 0.9 copy-done.2
  0.9 0.9 shard_map.55
  1.8 7.8 %all-to-all-start = ((bf16[16,128,128]{2,1,0:T(8,128)(2,1)}), bf16[16,128,128]{2,1,0:T(8,128)(2,1)S(1)}, u32[]{:S(2)}, u32[]{:S(2)}) async-start(bf16[16,128,128]{2,1,0:T(8,128)(2,1)} %shard_map.55), calls=%async_computation | async-start | bytes 1048576 | tf_op jit(solution)/shard_map/all_to_all | solution.py:125
  9.6 0.0 copy-start.1
  9.6 1.1 %copy-done.1 = bf16[2304,128]{1,0:T(8,128)(2,1)S(1)} copy-done((bf16[2304,128]{1,0:T(8,128)(2,1)S(1)}, bf16[2304,128]{1,0:T(8,128)(2,1)}, u32[]{:S(2)}) %copy-start.1) | copy-done | bytes 589848
  10.7 0.3 shard_map.56
  11.0 0.0 copy-start
  11.0 1.4 %copy-done = bf16[32,288,128]{2,1,0:T(8,128)(2,1)} copy-done((bf16[32,288,128]{2,1,0:T(8,128)(2,1)}, bf16[32,288,128]{2,1,0:T(8,128)(2,1)S(1)}, u32[]{:S(2)}) %copy-start) | copy-done | bytes 2359320
  12.4 5.0 %all-to-all-done.refs_0_ = bf16[16,128,128]{2,1,0:T(8,128)(2,1)S(1)} async-done(((bf16[16,128,128]{2,1,0:T(8,128)(2,1)}), bf16[16,128,128]{2,1,0:T(8,128)(2,1)S(1)}, u32[]{:S(2)}, u32[]{:S(2)}) %all-to-all-start) | async-done | bytes 524320 | tf_op jit(solution)/shard_map/all_to_all | solution.py:125
  17.4 9.1 %all-to-all-start.1 = ((bf16[32,288,128]{2,1,0:T(8,128)(2,1)}), bf16[32,288,128]{2,1,0:T(8,128)(2,1)S(1)}, u32[]{:S(2)}, u32[]{:S(2)}) async-start(bf16[32,288,128]{2,1,0:T(8,128)(2,1)} %copy-done), calls=%async_computation.1 | async-start | bytes 4718592 | tf_op jit(solution)/shard_map/all_to_all | solution.py:124
  26.5 5.8 %collective-permute-start = (bf16[16,128,128]{2,1,0:T(8,128)(2,1)S(1)}, bf16[16,128,128]{2,1,0:T(8,128)(2,1)S(1)}, u32[]{:S(2)}, u32[]{:S(2)}) collective-permute-start(bf16[16,128,128]{2,1,0:T(8,128)(2,1)S(1)} %all-to-all-done.refs_0_), channel_id=1, source_target_pairs={{0,2},{2,0},{4,6},{6,4},{1,3},{3,1},{5,7},{7,5},{8,10},{10,8},{12,... | collective-permute-start | bytes 1572872 | tf_op jit(solution)/shard_map/ppermute | solution.py:126
  32.3 7.9 %collective-permute-start.1 = (bf16[16,128,128]{2,1,0:T(8,128)(2,1)S(1)}, bf16[16,128,128]{2,1,0:T(8,128)(2,1)}, u32[]{:S(2)}, u32[]{:S(2)}) collective-permute-start(bf16[16,128,128]{2,1,0:T(8,128)(2,1)S(1)} %all-to-all-done.refs_0_), channel_id=1, source_target_pairs={{0,4},{2,6},{4,0},{6,2},{1,5},{3,7},{5,1},{7,3},{8,12},{10,14},{12... | collective-permute-start | bytes 1572872 | tf_op jit(solution)/shard_map/ppermute | solution.py:126
  40.3 1.9 %collective-permute-start.2 = (bf16[16,128,128]{2,1,0:T(8,128)(2,1)S(1)}, bf16[16,128,128]{2,1,0:T(8,128)(2,1)}, u32[]{:S(2)}, u32[]{:S(2)}) collective-permute-start(bf16[16,128,128]{2,1,0:T(8,128)(2,1)S(1)} %all-to-all-done.refs_0_), channel_id=1, source_target_pairs={{0,6},{2,4},{4,2},{6,0},{1,7},{3,5},{5,3},{7,1},{8,14},{10,12},{12... | collective-permute-start | bytes 1572872 | tf_op jit(solution)/shard_map/ppermute | solution.py:126
  42.2 35.8 %collective-permute-done.refs_1_ = bf16[16,128,128]{2,1,0:T(8,128)(2,1)S(1)} collective-permute-done((bf16[16,128,128]{2,1,0:T(8,128)(2,1)S(1)}, bf16[16,128,128]{2,1,0:T(8,128)(2,1)S(1)}, u32[]{:S(2)}, u32[]{:S(2)}) %collective-permute-start) | collective-permute-done | bytes 524320 | tf_op jit(solution)/shard_map/ppermute | solution.py:126
  78.0 0.0 collective-permute-done.1.refs_2_
  78.0 0.0 collective-permute-done.2.refs_3_
  78.1 0.7 all-to-all-done.1.refs_4_
  78.7 0.0 copy-start.3
  78.7 0.0 copy-start.4
  78.7 0.0 copy-start.5
  78.7 2.6 %shard_map.57 = f32[8,56,128]{2,1,0:T(8,128)S(1)} custom-call(s32[1]{0:T(128)} %bitcast.my_zh_ref, bf16[16,128,128]{2,1,0:T(8,128)(2,1)S(1)} %all-to-all-done.refs_0_, bf16[16,128,128]{2,1,0:T(8,128)(2,1)S(1)} %collective-permute-done.refs_1_, bf16[16,128,128]{2,1,0:T(8,128)(2,1)} %collective-permute-done.1.refs_2_, ...), custom_call_target="tpu_custom_call" | custom-call | tf_op jit(solution)/shard_map/pallas_call | solution.py:107
  81.4 12.0 %all_to_all.15 = f32[8,56,128]{2,1,0:T(8,128)S(1)} all-to-all(f32[8,56,128]{2,1,0:T(8,128)S(1)} %shard_map.57), channel_id=1, replica_groups=mesh['l'=2,'yh'=4,'yl'=2,'xl'=2,'xh'=2,'zh'=4,'zl'=2] {'yl','xl','xh'}, dimensions={0} | all-to-all | bytes 458752 | tf_op jit(solution)/shard_map/all_to_all | solution.py:129
  93.4 11.0 %psum.7 = f32[56,128]{1,0:T(8,128)S(1)} all-reduce(f32[56,128]{1,0:T(8,128)S(1)} %reduce_sum.9), channel_id=1, replica_groups=mesh['l'=2,'yh'=4,'yl'=2,'xl'=2,'xh'=2,'zh'=4,'zl'=2] {'l'}, use_global_device_ids=true, to_apply=%region_1.0 | all-reduce | flops 7168 | bytes 57344 | tf_op jit(solution)/shard_map/psum | solution.py:130
  104.4 0.0 copy-done.3
  104.4 0.0 copy-done.4
  104.4 0.0 copy-done.5
  104.4 0.7 subtract_divide_fusion
  (1 shorter events, 0.0 us)
Async XLA Ops:
  0.0 0.9 copy-start.2
  1.8 15.6 %all-to-all-start = ((bf16[16,128,128]{2,1,0:T(8,128)(2,1)}), bf16[16,128,128]{2,1,0:T(8,128)(2,1)S(1)}, u32[]{:S(2)}, u32[]{:S(2)}) async-start(bf16[16,128,128]{2,1,0:T(8,128)(2,1)} %shard_map.55), calls=%async_computation | async-start | bytes 1048576 | tf_op jit(solution)/shard_map/all_to_all | solution.py:125
  9.6 1.1 %copy-start.1 = (bf16[2304,128]{1,0:T(8,128)(2,1)S(1)}, bf16[2304,128]{1,0:T(8,128)(2,1)}, u32[]{:S(2)}) copy-start(bf16[2304,128]{1,0:T(8,128)(2,1)} %b_ref.1) | copy-start | bytes 1769476
  11.0 1.4 %copy-start = (bf16[32,288,128]{2,1,0:T(8,128)(2,1)}, bf16[32,288,128]{2,1,0:T(8,128)(2,1)S(1)}, u32[]{:S(2)}) copy-start(bf16[32,288,128]{2,1,0:T(8,128)(2,1)S(1)} %shard_map.56) | copy-start | bytes 7077892
  17.4 61.3 %all-to-all-start.1 = ((bf16[32,288,128]{2,1,0:T(8,128)(2,1)}), bf16[32,288,128]{2,1,0:T(8,128)(2,1)S(1)}, u32[]{:S(2)}, u32[]{:S(2)}) async-start(bf16[32,288,128]{2,1,0:T(8,128)(2,1)} %copy-done), calls=%async_computation.1 | async-start | bytes 4718592 | tf_op jit(solution)/shard_map/all_to_all | solution.py:124
  26.5 51.5 %collective-permute-start = (bf16[16,128,128]{2,1,0:T(8,128)(2,1)S(1)}, bf16[16,128,128]{2,1,0:T(8,128)(2,1)S(1)}, u32[]{:S(2)}, u32[]{:S(2)}) collective-permute-start(bf16[16,128,128]{2,1,0:T(8,128)(2,1)S(1)} %all-to-all-done.refs_0_), channel_id=1, source_target_pairs={{0,2},{2,0},{4,6},{6,4},{1,3},{3,1},{5,7},{7,5},{8,10},{10,8},{12,... | collective-permute-start | bytes 1572872 | tf_op jit(solution)/shard_map/ppermute | solution.py:126
  32.3 45.7 %collective-permute-start.1 = (bf16[16,128,128]{2,1,0:T(8,128)(2,1)S(1)}, bf16[16,128,128]{2,1,0:T(8,128)(2,1)}, u32[]{:S(2)}, u32[]{:S(2)}) collective-permute-start(bf16[16,128,128]{2,1,0:T(8,128)(2,1)S(1)} %all-to-all-done.refs_0_), channel_id=1, source_target_pairs={{0,4},{2,6},{4,0},{6,2},{1,5},{3,7},{5,1},{7,3},{8,12},{10,14},{12... | collective-permute-start | bytes 1572872 | tf_op jit(solution)/shard_map/ppermute | solution.py:126
  40.3 37.8 %collective-permute-start.2 = (bf16[16,128,128]{2,1,0:T(8,128)(2,1)S(1)}, bf16[16,128,128]{2,1,0:T(8,128)(2,1)}, u32[]{:S(2)}, u32[]{:S(2)}) collective-permute-start(bf16[16,128,128]{2,1,0:T(8,128)(2,1)S(1)} %all-to-all-done.refs_0_), channel_id=1, source_target_pairs={{0,6},{2,4},{4,2},{6,0},{1,7},{3,5},{5,3},{7,1},{8,14},{10,12},{12... | collective-permute-start | bytes 1572872 | tf_op jit(solution)/shard_map/ppermute | solution.py:126
  78.7 25.7 %copy-start.3 = (f32[56,128]{1,0:T(8,128)S(1)}, f32[56,128]{1,0:T(8,128)}, u32[]{:S(2)}) copy-start(f32[56,128]{1,0:T(8,128)} %param.7) | copy-start | bytes 86020
  78.7 25.7 %copy-start.4 = (f32[128]{0:T(128)S(1)}, f32[128]{0:T(128)}, u32[]{:S(2)}) copy-start(f32[128]{0:T(128)} %param.9) | copy-start | bytes 1540
  78.7 25.7 %copy-start.5 = (f32[56]{0:T(128)S(1)}, f32[56]{0:T(128)}, u32[]{:S(2)}) copy-start(f32[56]{0:T(128)} %param.8) | copy-start | bytes 676

commit v7 on v5

--- a/solution.py
+++ b/solution.py
@@ -36,8 +36,8 @@
 def pack_b_kernel(b_ref, out_ref):
     for s in range(PIECES):
         for far in range(4):
-            out_ref[far, s, 0:LANES, :] = b_ref[s * LANES : (s + 1) * LANES, :]
-            out_ref[far, s, LANES:, :] = b_ref[MAIN + s * REST : MAIN + (s + 1) * REST, :]
+            out_ref[s, far, 0:LANES, :] = b_ref[s * LANES : (s + 1) * LANES, :]
+            out_ref[s, far, LANES:, :] = b_ref[MAIN + s * REST : MAIN + (s + 1) * REST, :]
 
 
 def pack(kernel, block, shape):
@@ -69,8 +69,8 @@
         for c in range(4):
             columns = slice(c * LANES, (c + 1) * LANES)
             piece = 4 * (2 * b1 + b0) + c
-            right[t * LANES : (t + 1) * LANES, columns] = b_ref[2 * b3 + b2, piece, 0:LANES, :]
-            right[MAIN + t * REST : MAIN + (t + 1) * REST, columns] = b_ref[2 * b3 + b2, piece, LANES:, :]
+            right[t * LANES : (t + 1) * LANES, columns] = b_ref[piece, 2 * b3 + b2, 0:LANES, :]
+            right[MAIN + t * REST : MAIN + (t + 1) * REST, columns] = b_ref[piece, 2 * b3 + b2, LANES:, :]
     spread[...] = jnp.zeros_like(spread)
     for half in range(2):
         for g in range(ROWS // 8):
@@ -107,8 +107,8 @@
 
 def body(amplitudes, integrals, other_terms, occ_energy, virt_energy):
     a = pack(pack_a_kernel, amplitudes, (PIECES, A_ROWS, LANES))
-    b = pack(pack_b_kernel, integrals, (4, PIECES, B_ROWS, LANES))
-    b_slots = lax.all_to_all(b.reshape((4 * PIECES,) + b.shape[2:]), ("yh",) + NEAR, 0, 0, tiled=True).reshape(b.shape)
+    b = pack(pack_b_kernel, integrals, (PIECES, 4, B_ROWS, LANES))
+    b_slots = lax.all_to_all(b.reshape((4 * PIECES,) + b.shape[2:]), NEAR + ("yh",), 0, 0, tiled=True).reshape(b.shape)
     a = lax.all_to_all(a, NEAR, 0, 0, tiled=True)
     a_slots = [a] + [lax.ppermute(a, "zh", [(i, i ^ d) for i in range(4)]) for d in (1, 2, 3)]
     my_zh = lax.axis_index("zh").astype(jnp.int32)[None]

time: 101 us -> 101 us (level)
  waiting for transfers between devices: 45.5 us -> 41.3 us
  blocking collectives: 16.9 us -> 20.5 us
    ppermute x3, waiting for transfers between devices: 41.6 us -> 36.9 us  [body(): lax.ppermute(a, 'zh', [(i, i ^ d) for i in range(4)])]
    all_to_all x1, blocking collectives: 10.2 us -> 13.5 us  [body(): partial = lax.all_to_all(partial, NEAR, 0, 0, tiled=True)]
where the time goes in v7:
time: 101 us; the launch traced here: 100 us
  waiting for transfers between devices  41.3 us (41%)
  starting transfers between devices  31.7 us (31%)
  blocking collectives  20.5 us (20%)
  local copies, waits for them, and re-layouts  3.41 us (3%)
  Pallas kernels  2.25 us (2%)
    ppermute x3, waiting for transfers between devices, body(): lax.ppermute(a, 'zh', [(i, i ^ d) for i in range(4)])  36.9 us
    ppermute x3, starting transfers between devices, body(): lax.ppermute(a, 'zh', [(i, i ^ d) for i in range(4)])  15.7 us
    all_to_all x1, blocking collectives, body(): partial = lax.all_to_all(partial, NEAR, 0, 0, tiled=True)  13.5 us
    all_to_all x1, starting transfers between devices, body(): lax.all_to_all(b.reshape((4 * PIECES,) + b.shape[2:]), NEAR + ('yh',), 0,...  8.23 us
    all_to_all x1, starting transfers between devices, body(): a = lax.all_to_all(a, NEAR, 0, 0, tiled=True)  7.77 us
    psum x1, blocking collectives, body(): ladder = lax.psum(jnp.sum(partial, axis=0), 'l')  7.07 us
    all_to_all x1, waiting for transfers between devices, body(): a = lax.all_to_all(a, NEAR, 0, 0, tiled=True)  3.92 us
    unnamed x12, local copies, waits for them, and re-layouts  3.41 us
  transfers between devices with their start and end apart: 5, of which 3 were waited for; matrix products, arithmetic and copies ran while one was open for 0% of the time, Pallas kernels for 0%

profile of v7, /device:TPU:1, one launch (start us, length us, event | category | flops | bytes accessed | tf_op | source)
XLA Modules:
  0.0 100.0 jit_solution(17869732160507236945)
XLA Ops:
  0.0 0.0 copy-start.2
  0.0 0.9 copy-done.2
  0.9 0.8 shard_map.55
  1.8 7.8 %all-to-all-start = ((bf16[16,64,128]{2,1,0:T(8,128)(2,1)}), bf16[16,64,128]{2,1,0:T(8,128)(2,1)S(1)}, u32[]{:S(2)}, u32[]{:S(2)}) async-start(bf16[16,64,128]{2,1,0:T(8,128)(2,1)} %shard_map.55), calls=%async_computation | async-start | bytes 524288 | tf_op jit(solution)/shard_map/all_to_all | solution.py:112
  9.6 0.0 copy-start.1
  9.6 1.1 %copy-done.1 = bf16[2304,128]{1,0:T(8,128)(2,1)S(1)} copy-done((bf16[2304,128]{1,0:T(8,128)(2,1)S(1)}, bf16[2304,128]{1,0:T(8,128)(2,1)}, u32[]{:S(2)}) %copy-start.1) | copy-done | bytes 589848
  10.6 0.3 shard_map.56
  10.9 0.0 copy-start
  10.9 1.4 %copy-done = bf16[16,4,144,128]{3,2,1,0:T(8,128)(2,1)} copy-done((bf16[16,4,144,128]{3,2,1,0:T(8,128)(2,1)}, bf16[16,4,144,128]{3,2,1,0:T(8,128)(2,1)S(1)}, u32[]{:S(2)}) %copy-start) | copy-done | bytes 2359320
  12.3 3.9 %all-to-all-done.refs_0_ = bf16[16,64,128]{2,1,0:T(8,128)(2,1)S(1)} async-done(((bf16[16,64,128]{2,1,0:T(8,128)(2,1)}), bf16[16,64,128]{2,1,0:T(8,128)(2,1)S(1)}, u32[]{:S(2)}, u32[]{:S(2)}) %all-to-all-start) | async-done | bytes 262176 | tf_op jit(solution)/shard_map/all_to_all | solution.py:112
  16.3 8.2 %all-to-all-start.1 = ((bf16[64,144,128]{2,1,0:T(8,128)(2,1)}), bf16[64,144,128]{2,1,0:T(8,128)(2,1)S(1)}, u32[]{:S(2)}, u32[]{:S(2)}) async-start(bf16[64,144,128]{2,1,0:T(8,128)(2,1)} %bitcast.4), calls=%async_computation.1 | async-start | bytes 4718592 | tf_op jit(solution)/shard_map/all_to_all | solution.py:111
  24.5 5.8 %collective-permute-start = (bf16[16,64,128]{2,1,0:T(8,128)(2,1)S(1)}, bf16[16,64,128]{2,1,0:T(8,128)(2,1)S(1)}, u32[]{:S(2)}, u32[]{:S(2)}) collective-permute-start(bf16[16,64,128]{2,1,0:T(8,128)(2,1)S(1)} %all-to-all-done.refs_0_), channel_id=1, source_target_pairs={{0,2},{2,0},{4,6},{6,4},{1,3},{3,1},{5,7},{7,5},{8,10},{10,8},{12,... | collective-permute-start | bytes 786440 | tf_op jit(solution)/shard_map/ppermute | solution.py:113
  30.3 7.9 %collective-permute-start.1 = (bf16[16,64,128]{2,1,0:T(8,128)(2,1)S(1)}, bf16[16,64,128]{2,1,0:T(8,128)(2,1)S(1)}, u32[]{:S(2)}, u32[]{:S(2)}) collective-permute-start(bf16[16,64,128]{2,1,0:T(8,128)(2,1)S(1)} %all-to-all-done.refs_0_), channel_id=1, source_target_pairs={{0,4},{2,6},{4,0},{6,2},{1,5},{3,7},{5,1},{7,3},{8,12},{10,14},{12... | collective-permute-start | bytes 786440 | tf_op jit(solution)/shard_map/ppermute | solution.py:113
  38.3 1.9 %collective-permute-start.2 = (bf16[16,64,128]{2,1,0:T(8,128)(2,1)S(1)}, bf16[16,64,128]{2,1,0:T(8,128)(2,1)S(1)}, u32[]{:S(2)}, u32[]{:S(2)}) collective-permute-start(bf16[16,64,128]{2,1,0:T(8,128)(2,1)S(1)} %all-to-all-done.refs_0_), channel_id=1, source_target_pairs={{0,6},{2,4},{4,2},{6,0},{1,7},{3,5},{5,3},{7,1},{8,14},{10,12},{12... | collective-permute-start | bytes 786440 | tf_op jit(solution)/shard_map/ppermute | solution.py:113
  40.2 0.0 collective-permute-done.refs_1_
  40.2 36.9 %collective-permute-done.1.refs_2_ = bf16[16,64,128]{2,1,0:T(8,128)(2,1)S(1)} collective-permute-done((bf16[16,64,128]{2,1,0:T(8,128)(2,1)S(1)}, bf16[16,64,128]{2,1,0:T(8,128)(2,1)S(1)}, u32[]{:S(2)}, u32[]{:S(2)}) %collective-permute-start.1) | collective-permute-done | bytes 262176 | tf_op jit(solution)/shard_map/ppermute | solution.py:113
  77.1 0.0 collective-permute-done.2.refs_3_
  77.1 0.5 all-to-all-done.1
  77.6 0.0 copy-start.3
  77.6 0.0 copy-start.4
  77.6 0.0 copy-start.5
  77.6 1.1 %shard_map.57 = f32[16,56,128]{2,1,0:T(8,128)S(1)} custom-call(s32[1]{0:T(128)} %bitcast.my_zh_ref, bf16[16,64,128]{2,1,0:T(8,128)(2,1)S(1)} %all-to-all-done.refs_0_, bf16[16,64,128]{2,1,0:T(8,128)(2,1)S(1)} %collective-permute-done.refs_1_, bf16[16,64,128]{2,1,0:T(8,128)(2,1)S(1)} %collective-permute-done.1.refs_2_, ...), custom_call_target="tpu_custom_call" | custom-call | tf_op jit(solution)/shard_map/pallas_call | solution.py:94
  78.7 13.5 %all_to_all.15 = f32[16,56,128]{2,1,0:T(8,128)S(1)} all-to-all(f32[16,56,128]{2,1,0:T(8,128)S(1)} %shard_map.57), channel_id=1, replica_groups=mesh['l'=2,'yh'=4,'yl'=2,'xl'=2,'xh'=2,'zh'=4,'zl'=2] {'yl','xl','xh','zl'}, dimensions={0} | all-to-all | bytes 917504 | tf_op jit(solution)/shard_map/all_to_all | solution.py:116
  92.2 7.1 %psum.7 = f32[56,128]{1,0:T(8,128)S(1)} all-reduce(f32[56,128]{1,0:T(8,128)S(1)} %reduce_sum.9), channel_id=1, replica_groups=mesh['l'=2,'yh'=4,'yl'=2,'xl'=2,'xh'=2,'zh'=4,'zl'=2] {'l'}, use_global_device_ids=true, to_apply=%region_1.0 | all-reduce | flops 7168 | bytes 57344 | tf_op jit(solution)/shard_map/psum | solution.py:117
  99.3 0.0 copy-done.3
  99.3 0.0 copy-done.4
  99.3 0.0 copy-done.5
  99.3 0.7 subtract_divide_fusion
  (1 shorter events, 0.0 us)
Async XLA Ops:
  0.0 0.9 copy-start.2
  1.8 14.5 %all-to-all-start = ((bf16[16,64,128]{2,1,0:T(8,128)(2,1)}), bf16[16,64,128]{2,1,0:T(8,128)(2,1)S(1)}, u32[]{:S(2)}, u32[]{:S(2)}) async-start(bf16[16,64,128]{2,1,0:T(8,128)(2,1)} %shard_map.55), calls=%async_computation | async-start | bytes 524288 | tf_op jit(solution)/shard_map/all_to_all | solution.py:112
  9.6 1.1 %copy-start.1 = (bf16[2304,128]{1,0:T(8,128)(2,1)S(1)}, bf16[2304,128]{1,0:T(8,128)(2,1)}, u32[]{:S(2)}) copy-start(bf16[2304,128]{1,0:T(8,128)(2,1)} %b_ref.1) | copy-start | bytes 1769476
  10.9 1.4 %copy-start = (bf16[16,4,144,128]{3,2,1,0:T(8,128)(2,1)}, bf16[16,4,144,128]{3,2,1,0:T(8,128)(2,1)S(1)}, u32[]{:S(2)}) copy-start(bf16[16,4,144,128]{3,2,1,0:T(8,128)(2,1)S(1)} %shard_map.56) | copy-start | bytes 7077892
  16.3 61.3 %all-to-all-start.1 = ((bf16[64,144,128]{2,1,0:T(8,128)(2,1)}), bf16[64,144,128]{2,1,0:T(8,128)(2,1)S(1)}, u32[]{:S(2)}, u32[]{:S(2)}) async-start(bf16[64,144,128]{2,1,0:T(8,128)(2,1)} %bitcast.4), calls=%async_computation.1 | async-start | bytes 4718592 | tf_op jit(solution)/shard_map/all_to_all | solution.py:111
  24.5 15.7 %collective-permute-start = (bf16[16,64,128]{2,1,0:T(8,128)(2,1)S(1)}, bf16[16,64,128]{2,1,0:T(8,128)(2,1)S(1)}, u32[]{:S(2)}, u32[]{:S(2)}) collective-permute-start(bf16[16,64,128]{2,1,0:T(8,128)(2,1)S(1)} %all-to-all-done.refs_0_), channel_id=1, source_target_pairs={{0,2},{2,0},{4,6},{6,4},{1,3},{3,1},{5,7},{7,5},{8,10},{10,8},{12,... | collective-permute-start | bytes 786440 | tf_op jit(solution)/shard_map/ppermute | solution.py:113
  30.3 46.8 %collective-permute-start.1 = (bf16[16,64,128]{2,1,0:T(8,128)(2,1)S(1)}, bf16[16,64,128]{2,1,0:T(8,128)(2,1)S(1)}, u32[]{:S(2)}, u32[]{:S(2)}) collective-permute-start(bf16[16,64,128]{2,1,0:T(8,128)(2,1)S(1)} %all-to-all-done.refs_0_), channel_id=1, source_target_pairs={{0,4},{2,6},{4,0},{6,2},{1,5},{3,7},{5,1},{7,3},{8,12},{10,14},{12... | collective-permute-start | bytes 786440 | tf_op jit(solution)/shard_map/ppermute | solution.py:113
  38.3 38.8 %collective-permute-start.2 = (bf16[16,64,128]{2,1,0:T(8,128)(2,1)S(1)}, bf16[16,64,128]{2,1,0:T(8,128)(2,1)S(1)}, u32[]{:S(2)}, u32[]{:S(2)}) collective-permute-start(bf16[16,64,128]{2,1,0:T(8,128)(2,1)S(1)} %all-to-all-done.refs_0_), channel_id=1, source_target_pairs={{0,6},{2,4},{4,2},{6,0},{1,7},{3,5},{5,3},{7,1},{8,14},{10,12},{12... | collective-permute-start | bytes 786440 | tf_op jit(solution)/shard_map/ppermute | solution.py:113
  77.6 21.7 %copy-start.3 = (f32[56,128]{1,0:T(8,128)S(1)}, f32[56,128]{1,0:T(8,128)}, u32[]{:S(2)}) copy-start(f32[56,128]{1,0:T(8,128)} %param.7) | copy-start | bytes 86020
  77.6 21.7 %copy-start.4 = (f32[128]{0:T(128)S(1)}, f32[128]{0:T(128)}, u32[]{:S(2)}) copy-start(f32[128]{0:T(128)} %param.9) | copy-start | bytes 1540
  77.6 21.7 %copy-start.5 = (f32[56]{0:T(128)S(1)}, f32[56]{0:T(128)}, u32[]{:S(2)}) copy-start(f32[56]{0:T(128)} %param.8) | copy-start | bytes 676

commit v8 on v7

--- a/solution.py
+++ b/solution.py
@@ -114,7 +114,8 @@
     my_zh = lax.axis_index("zh").astype(jnp.int32)[None]
     partial = multiply(my_zh, a_slots, b_slots)
     partial = lax.all_to_all(partial, NEAR, 0, 0, tiled=True)
-    ladder = lax.psum(jnp.sum(partial, axis=0), "l")
+    mine = jnp.sum(partial, axis=0)
+    ladder = mine + lax.ppermute(mine, "l", [(0, 1), (1, 0)])
     denominator = occ_energy[:, None] - virt_energy[None, :]
     return (ladder + other_terms) / denominator
 

time: 101 us -> 100 us (0.990)
  blocking collectives: 20.5 us -> 13.5 us
  starting transfers between devices: 31.7 us -> 37.4 us
    psum x1 -> x0, blocking collectives: 7.07 us -> none  [body(): ladder = lax.psum(jnp.sum(partial, axis=0), 'l')]
    ppermute x0 -> x1, starting transfers between devices: none -> 5.75 us  [body(): ladder = mine + lax.ppermute(mine, 'l', [(0, 1), (1, 0)])]
  transfers between devices with their start and end apart: 5 -> 6, of which waited for: 3 -> 4; matrix products, arithmetic and copies ran while one was open for 0% -> 0% of each run, Pallas kernels for 0% -> 0%
where the time goes in v8:
time: 100 us; the launch traced here: 99.5 us
  waiting for transfers between devices  42.1 us (42%)
  starting transfers between devices  37.4 us (37%)
  blocking collectives  13.5 us (14%)
  local copies, waits for them, and re-layouts  3.42 us (3%)
  Pallas kernels  2.23 us (2%)
    ppermute x3, waiting for transfers between devices, body(): lax.ppermute(a, 'zh', [(i, i ^ d) for i in range(4)])  36.9 us
    ppermute x3, starting transfers between devices, body(): lax.ppermute(a, 'zh', [(i, i ^ d) for i in range(4)])  15.7 us
    all_to_all x1, blocking collectives, body(): partial = lax.all_to_all(partial, NEAR, 0, 0, tiled=True)  13.5 us
    all_to_all x1, starting transfers between devices, body(): lax.all_to_all(b.reshape((4 * PIECES,) + b.shape[2:]), NEAR + ('yh',), 0,...  8.23 us
    all_to_all x1, starting transfers between devices, body(): a = lax.all_to_all(a, NEAR, 0, 0, tiled=True)  7.77 us
    ppermute x1, starting transfers between devices, body(): ladder = mine + lax.ppermute(mine, 'l', [(0, 1), (1, 0)])  5.75 us
    all_to_all x1, waiting for transfers between devices, body(): a = lax.all_to_all(a, NEAR, 0, 0, tiled=True)  3.92 us
    unnamed x12, local copies, waits for them, and re-layouts  3.42 us
  transfers between devices with their start and end apart: 6, of which 4 were waited for; matrix products, arithmetic and copies ran while one was open for 0% of the time, Pallas kernels for 0%

profile of v8, /device:TPU:1, one launch (start us, length us, event | category | flops | bytes accessed | tf_op | source)
XLA Modules:
  0.0 99.5 jit_solution(2351844618220740303)
XLA Ops:
  0.0 0.0 copy-start.2
  0.0 0.9 copy-done.2
  0.9 0.8 shard_map.55
  1.8 7.8 %all-to-all-start = ((bf16[16,64,128]{2,1,0:T(8,128)(2,1)}), bf16[16,64,128]{2,1,0:T(8,128)(2,1)S(1)}, u32[]{:S(2)}, u32[]{:S(2)}) async-start(bf16[16,64,128]{2,1,0:T(8,128)(2,1)} %shard_map.55), calls=%async_computation | async-start | bytes 524288 | tf_op jit(solution)/shard_map/all_to_all | solution.py:112
  9.5 0.0 copy-start.1
  9.6 1.1 %copy-done.1 = bf16[2304,128]{1,0:T(8,128)(2,1)S(1)} copy-done((bf16[2304,128]{1,0:T(8,128)(2,1)S(1)}, bf16[2304,128]{1,0:T(8,128)(2,1)}, u32[]{:S(2)}) %copy-start.1) | copy-done | bytes 589848
  10.6 0.3 shard_map.56
  10.9 0.0 copy-start
  10.9 1.4 %copy-done = bf16[16,4,144,128]{3,2,1,0:T(8,128)(2,1)} copy-done((bf16[16,4,144,128]{3,2,1,0:T(8,128)(2,1)}, bf16[16,4,144,128]{3,2,1,0:T(8,128)(2,1)S(1)}, u32[]{:S(2)}) %copy-start) | copy-done | bytes 2359320
  12.3 3.9 %all-to-all-done.refs_0_ = bf16[16,64,128]{2,1,0:T(8,128)(2,1)S(1)} async-done(((bf16[16,64,128]{2,1,0:T(8,128)(2,1)}), bf16[16,64,128]{2,1,0:T(8,128)(2,1)S(1)}, u32[]{:S(2)}, u32[]{:S(2)}) %all-to-all-start) | async-done | bytes 262176 | tf_op jit(solution)/shard_map/all_to_all | solution.py:112
  16.3 8.2 %all-to-all-start.1 = ((bf16[64,144,128]{2,1,0:T(8,128)(2,1)}), bf16[64,144,128]{2,1,0:T(8,128)(2,1)S(1)}, u32[]{:S(2)}, u32[]{:S(2)}) async-start(bf16[64,144,128]{2,1,0:T(8,128)(2,1)} %bitcast.4), calls=%async_computation.1 | async-start | bytes 4718592 | tf_op jit(solution)/shard_map/all_to_all | solution.py:111
  24.5 5.8 %collective-permute-start = (bf16[16,64,128]{2,1,0:T(8,128)(2,1)S(1)}, bf16[16,64,128]{2,1,0:T(8,128)(2,1)S(1)}, u32[]{:S(2)}, u32[]{:S(2)}) collective-permute-start(bf16[16,64,128]{2,1,0:T(8,128)(2,1)S(1)} %all-to-all-done.refs_0_), channel_id=1, source_target_pairs={{0,2},{2,0},{4,6},{6,4},{1,3},{3,1},{5,7},{7,5},{8,10},{10,8},{12,... | collective-permute-start | bytes 786440 | tf_op jit(solution)/shard_map/ppermute | solution.py:113
  30.3 7.9 %collective-permute-start.1 = (bf16[16,64,128]{2,1,0:T(8,128)(2,1)S(1)}, bf16[16,64,128]{2,1,0:T(8,128)(2,1)S(1)}, u32[]{:S(2)}, u32[]{:S(2)}) collective-permute-start(bf16[16,64,128]{2,1,0:T(8,128)(2,1)S(1)} %all-to-all-done.refs_0_), channel_id=1, source_target_pairs={{0,4},{2,6},{4,0},{6,2},{1,5},{3,7},{5,1},{7,3},{8,12},{10,14},{12... | collective-permute-start | bytes 786440 | tf_op jit(solution)/shard_map/ppermute | solution.py:113
  38.3 1.9 %collective-permute-start.2 = (bf16[16,64,128]{2,1,0:T(8,128)(2,1)S(1)}, bf16[16,64,128]{2,1,0:T(8,128)(2,1)S(1)}, u32[]{:S(2)}, u32[]{:S(2)}) collective-permute-start(bf16[16,64,128]{2,1,0:T(8,128)(2,1)S(1)} %all-to-all-done.refs_0_), channel_id=1, source_target_pairs={{0,6},{2,4},{4,2},{6,0},{1,7},{3,5},{5,3},{7,1},{8,14},{10,12},{12... | collective-permute-start | bytes 786440 | tf_op jit(solution)/shard_map/ppermute | solution.py:113
  40.2 0.0 collective-permute-done.refs_1_
  40.2 36.9 %collective-permute-done.1.refs_2_ = bf16[16,64,128]{2,1,0:T(8,128)(2,1)S(1)} collective-permute-done((bf16[16,64,128]{2,1,0:T(8,128)(2,1)S(1)}, bf16[16,64,128]{2,1,0:T(8,128)(2,1)S(1)}, u32[]{:S(2)}, u32[]{:S(2)}) %collective-permute-start.1) | collective-permute-done | bytes 262176 | tf_op jit(solution)/shard_map/ppermute | solution.py:113
  77.1 0.0 collective-permute-done.2.refs_3_
  77.1 0.5 all-to-all-done.1
  77.6 0.0 copy-start.3
  77.6 0.0 copy-start.4
  77.6 0.0 copy-start.5
  77.6 1.1 %shard_map.57 = f32[16,56,128]{2,1,0:T(8,128)S(1)} custom-call(s32[1]{0:T(128)} %bitcast.my_zh_ref, bf16[16,64,128]{2,1,0:T(8,128)(2,1)S(1)} %all-to-all-done.refs_0_, bf16[16,64,128]{2,1,0:T(8,128)(2,1)S(1)} %collective-permute-done.refs_1_, bf16[16,64,128]{2,1,0:T(8,128)(2,1)S(1)} %collective-permute-done.1.refs_2_, ...), custom_call_target="tpu_custom_call" | custom-call | tf_op jit(solution)/shard_map/pallas_call | solution.py:94
  78.7 13.5 %all_to_all.15 = f32[16,56,128]{2,1,0:T(8,128)S(1)} all-to-all(f32[16,56,128]{2,1,0:T(8,128)S(1)} %shard_map.57), channel_id=1, replica_groups=mesh['l'=2,'yh'=4,'yl'=2,'xl'=2,'xh'=2,'zh'=4,'zl'=2] {'yl','xl','xh','zl'}, dimensions={0} | all-to-all | bytes 917504 | tf_op jit(solution)/shard_map/all_to_all | solution.py:116
  92.2 5.7 %collective-permute-start.3 = (f32[56,128]{1,0:T(8,128)S(1)}, f32[56,128]{1,0:T(8,128)S(1)}, u32[]{:S(2)}, u32[]{:S(2)}) collective-permute-start(f32[56,128]{1,0:T(8,128)S(1)} %reduce_sum.9), channel_id=1, source_target_pairs={{0,256},{256,0},{1,257},{257,1},{2,258},{258,2},{3,259},{259,3},{4... | collective-permute-start | bytes 86024 | tf_op jit(solution)/shard_map/ppermute | solution.py:118
  98.0 0.8 collective-permute-done.3
  98.8 0.0 copy-done.3
  98.8 0.0 copy-done.4
  98.8 0.0 copy-done.5
  98.8 0.7 subtract_divide_fusion
  (1 shorter events, 0.0 us)
Async XLA Ops:
  0.0 0.9 copy-start.2
  1.8 14.5 %all-to-all-start = ((bf16[16,64,128]{2,1,0:T(8,128)(2,1)}), bf16[16,64,128]{2,1,0:T(8,128)(2,1)S(1)}, u32[]{:S(2)}, u32[]{:S(2)}) async-start(bf16[16,64,128]{2,1,0:T(8,128)(2,1)} %shard_map.55), calls=%async_computation | async-start | bytes 524288 | tf_op jit(solution)/shard_map/all_to_all | solution.py:112
  9.5 1.1 %copy-start.1 = (bf16[2304,128]{1,0:T(8,128)(2,1)S(1)}, bf16[2304,128]{1,0:T(8,128)(2,1)}, u32[]{:S(2)}) copy-start(bf16[2304,128]{1,0:T(8,128)(2,1)} %b_ref.1) | copy-start | bytes 1769476
  10.9 1.4 %copy-start = (bf16[16,4,144,128]{3,2,1,0:T(8,128)(2,1)}, bf16[16,4,144,128]{3,2,1,0:T(8,128)(2,1)S(1)}, u32[]{:S(2)}) copy-start(bf16[16,4,144,128]{3,2,1,0:T(8,128)(2,1)S(1)} %shard_map.56) | copy-start | bytes 7077892
  16.3 61.3 %all-to-all-start.1 = ((bf16[64,144,128]{2,1,0:T(8,128)(2,1)}), bf16[64,144,128]{2,1,0:T(8,128)(2,1)S(1)}, u32[]{:S(2)}, u32[]{:S(2)}) async-start(bf16[64,144,128]{2,1,0:T(8,128)(2,1)} %bitcast.4), calls=%async_computation.1 | async-start | bytes 4718592 | tf_op jit(solution)/shard_map/all_to_all | solution.py:111
  24.5 15.7 %collective-permute-start = (bf16[16,64,128]{2,1,0:T(8,128)(2,1)S(1)}, bf16[16,64,128]{2,1,0:T(8,128)(2,1)S(1)}, u32[]{:S(2)}, u32[]{:S(2)}) collective-permute-start(bf16[16,64,128]{2,1,0:T(8,128)(2,1)S(1)} %all-to-all-done.refs_0_), channel_id=1, source_target_pairs={{0,2},{2,0},{4,6},{6,4},{1,3},{3,1},{5,7},{7,5},{8,10},{10,8},{12,... | collective-permute-start | bytes 786440 | tf_op jit(solution)/shard_map/ppermute | solution.py:113
  30.3 46.8 %collective-permute-start.1 = (bf16[16,64,128]{2,1,0:T(8,128)(2,1)S(1)}, bf16[16,64,128]{2,1,0:T(8,128)(2,1)S(1)}, u32[]{:S(2)}, u32[]{:S(2)}) collective-permute-start(bf16[16,64,128]{2,1,0:T(8,128)(2,1)S(1)} %all-to-all-done.refs_0_), channel_id=1, source_target_pairs={{0,4},{2,6},{4,0},{6,2},{1,5},{3,7},{5,1},{7,3},{8,12},{10,14},{12... | collective-permute-start | bytes 786440 | tf_op jit(solution)/shard_map/ppermute | solution.py:113
  38.3 38.8 %collective-permute-start.2 = (bf16[16,64,128]{2,1,0:T(8,128)(2,1)S(1)}, bf16[16,64,128]{2,1,0:T(8,128)(2,1)S(1)}, u32[]{:S(2)}, u32[]{:S(2)}) collective-permute-start(bf16[16,64,128]{2,1,0:T(8,128)(2,1)S(1)} %all-to-all-done.refs_0_), channel_id=1, source_target_pairs={{0,6},{2,4},{4,2},{6,0},{1,7},{3,5},{5,3},{7,1},{8,14},{10,12},{12... | collective-permute-start | bytes 786440 | tf_op jit(solution)/shard_map/ppermute | solution.py:113
  77.6 21.2 %copy-start.3 = (f32[56,128]{1,0:T(8,128)S(1)}, f32[56,128]{1,0:T(8,128)}, u32[]{:S(2)}) copy-start(f32[56,128]{1,0:T(8,128)} %param.7) | copy-start | bytes 86020
  77.6 21.2 %copy-start.4 = (f32[128]{0:T(128)S(1)}, f32[128]{0:T(128)}, u32[]{:S(2)}) copy-start(f32[128]{0:T(128)} %param.9) | copy-start | bytes 1540
  77.6 21.2 %copy-start.5 = (f32[56]{0:T(128)S(1)}, f32[56]{0:T(128)}, u32[]{:S(2)}) copy-start(f32[56]{0:T(128)} %param.8) | copy-start | bytes 676
  92.2 6.6 %collective-permute-start.3 = (f32[56,128]{1,0:T(8,128)S(1)}, f32[56,128]{1,0:T(8,128)S(1)}, u32[]{:S(2)}, u32[]{:S(2)}) collective-permute-start(f32[56,128]{1,0:T(8,128)S(1)} %reduce_sum.9), channel_id=1, source_target_pairs={{0,256},{256,0},{1,257},{257,1},{2,258},{258,2},{3,259},{259,3},{4... | collective-permute-start | bytes 86024 | tf_op jit(solution)/shard_map/ppermute | solution.py:118

commit v9 on v8

--- a/solution.py
+++ b/solution.py
@@ -18,7 +18,7 @@
 VMEM = 40 * 1024 * 1024
 
 
-def pack_a_kernel(a_ref, out_ref):
+def pack_a_kernel(a_ref, b_tail_ref, out_ref):
     lane_group = lax.broadcasted_iota(jnp.int32, (8, LANES), 1) // REST
     tail = a_ref[:, MAIN:].astype(jnp.float32)
     for s in range(PIECES):
@@ -30,30 +30,40 @@
             shift = REST * (g - place) % LANES
             moved = pltpu.roll(tile, shift, 1) if shift else tile
             rest = jnp.where(lane_group == g, moved, rest)
-        out_ref[s] = jnp.concatenate([main, rest], axis=0).astype(jnp.bfloat16)
+        out_ref[s, 0:A_ROWS, :] = jnp.concatenate([main, rest], axis=0).astype(jnp.bfloat16)
+        out_ref[s, A_ROWS:, :] = b_tail_ref[s * REST : (s + 1) * REST, :]
+
+
+def pack_a(a, b_tail):
+    return pl.pallas_call(
+        pack_a_kernel,
+        out_shape=jax.ShapeDtypeStruct((PIECES, A_ROWS + REST, LANES), jnp.bfloat16),
+        in_specs=[pl.BlockSpec(memory_space=pltpu.VMEM)] * 2,
+        out_specs=pl.BlockSpec(memory_space=pltpu.VMEM),
+        compiler_params=pltpu.CompilerParams(vmem_limit_bytes=VMEM),
+    )(a, b_tail)
 
 
 def pack_b_kernel(b_ref, out_ref):
     for s in range(PIECES):
         for far in range(4):
-            out_ref[s, far, 0:LANES, :] = b_ref[s * LANES : (s + 1) * LANES, :]
-            out_ref[s, far, LANES:, :] = b_ref[MAIN + s * REST : MAIN + (s + 1) * REST, :]
+            out_ref[s, far] = b_ref[s * LANES : (s + 1) * LANES, :]
 
 
-def pack(kernel, block, shape):
+def pack_b(b):
     return pl.pallas_call(
-        kernel,
-        out_shape=jax.ShapeDtypeStruct(shape, jnp.bfloat16),
+        pack_b_kernel,
+        out_shape=jax.ShapeDtypeStruct((PIECES, 4, LANES, LANES), jnp.bfloat16),
         in_specs=[pl.BlockSpec(memory_space=pltpu.VMEM)],
         out_specs=pl.BlockSpec(memory_space=pltpu.VMEM),
-        cost_estimate=pl.CostEstimate(flops=0, bytes_accessed=8 * block.size, transcendentals=0),
+        cost_estimate=pl.CostEstimate(flops=0, bytes_accessed=8 * b.size, transcendentals=0),
         compiler_params=pltpu.CompilerParams(vmem_limit_bytes=VMEM),
-    )(block)
+    )(b)
 
 
-def multiply_kernel(my_zh_ref, *refs):
-    a_refs, (b_ref, out_ref, left, right, spread) = refs[:4], refs[4:]
-    my_zh = my_zh_ref[0]
+def multiply_kernel(place_ref, *refs):
+    a_refs, (b_ref, b_tail_ref, out_ref, left, right, spread) = refs[:4], refs[4:]
+    my_zh, my_yh = place_ref[0], place_ref[1]
     lane_group = lax.broadcasted_iota(jnp.int32, (4 * 8, LANES), 1) // REST
     tails = []
     for t in range(PIECES):
@@ -69,8 +79,8 @@
         for c in range(4):
             columns = slice(c * LANES, (c + 1) * LANES)
             piece = 4 * (2 * b1 + b0) + c
-            right[t * LANES : (t + 1) * LANES, columns] = b_ref[piece, 2 * b3 + b2, 0:LANES, :]
-            right[MAIN + t * REST : MAIN + (t + 1) * REST, columns] = b_ref[piece, 2 * b3 + b2, LANES:, :]
+            right[t * LANES : (t + 1) * LANES, columns] = b_ref[piece, 2 * b3 + b2]
+            right[MAIN + t * REST : MAIN + (t + 1) * REST, columns] = b_tail_ref[(2 * b3 + b2) ^ my_yh, piece]
     spread[...] = jnp.zeros_like(spread)
     for half in range(2):
         for g in range(ROWS // 8):
@@ -89,12 +99,12 @@
             out_ref[4 * r + c] = total[A_ROWS * r : A_ROWS * r + ROWS, c * LANES : (c + 1) * LANES]
 
 
-def multiply(my_zh, a_slots, b_slots):
+def multiply(place, a_slots, b_slots, b_tails):
     depth = PIECES * (LANES + REST)
     return pl.pallas_call(
         multiply_kernel,
         out_shape=jax.ShapeDtypeStruct((PIECES, ROWS, LANES), jnp.float32),
-        in_specs=[pl.BlockSpec(memory_space=pltpu.SMEM)] + [pl.BlockSpec(memory_space=pltpu.VMEM)] * 5,
+        in_specs=[pl.BlockSpec(memory_space=pltpu.SMEM)] + [pl.BlockSpec(memory_space=pltpu.VMEM)] * 6,
         out_specs=pl.BlockSpec(memory_space=pltpu.VMEM),
         scratch_shapes=[
             pltpu.VMEM((4 * A_ROWS, depth), jnp.bfloat16),
@@ -102,17 +112,19 @@
             pltpu.VMEM((4 * A_ROWS, 2 * LANES), jnp.float32),
         ],
         compiler_params=pltpu.CompilerParams(vmem_limit_bytes=VMEM),
-    )(my_zh, *a_slots, b_slots)
+    )(place, *a_slots, b_slots, b_tails)
 
 
 def body(amplitudes, integrals, other_terms, occ_energy, virt_energy):
-    a = pack(pack_a_kernel, amplitudes, (PIECES, A_ROWS, LANES))
-    b = pack(pack_b_kernel, integrals, (PIECES, 4, B_ROWS, LANES))
+    near = lax.all_to_all(pack_a(amplitudes, integrals[MAIN:]), NEAR, 0, 0, tiled=True)
+    a, b_tail = near[:, :A_ROWS], near[:, A_ROWS:]
+    b = pack_b(integrals)
     b_slots = lax.all_to_all(b.reshape((4 * PIECES,) + b.shape[2:]), NEAR + ("yh",), 0, 0, tiled=True).reshape(b.shape)
-    a = lax.all_to_all(a, NEAR, 0, 0, tiled=True)
-    a_slots = [a] + [lax.ppermute(a, "zh", [(i, i ^ d) for i in range(4)]) for d in (1, 2, 3)]
-    my_zh = lax.axis_index("zh").astype(jnp.int32)[None]
-    partial = multiply(my_zh, a_slots, b_slots)
+    flips = [[(i, i ^ d) for i in range(4)] for d in (1, 2, 3)]
+    b_tails = jnp.stack([b_tail] + [lax.ppermute(b_tail, "yh", flip) for flip in flips])
+    a_slots = [a] + [lax.ppermute(a, "zh", flip) for flip in flips]
+    place = jnp.stack([lax.axis_index("zh"), lax.axis_index("yh")]).astype(jnp.int32)
+    partial = multiply(place, a_slots, b_slots, b_tails)
     partial = lax.all_to_all(partial, NEAR, 0, 0, tiled=True)
     mine = jnp.sum(partial, axis=0)
     ladder = mine + lax.ppermute(mine, "l", [(0, 1), (1, 0)])

time: 100 us -> 110 us (1.10)
  starting transfers between devices: 37.4 us -> 52.9 us
  waiting for transfers between devices: 42.1 us -> 32.8 us
  Pallas kernels: 2.23 us -> 4.1 us
    ppermute x3 -> x6, starting transfers between devices: 15.7 us -> 29 us  [the longest x3 15.7 us: body(): a_slots = [a] + [lax.ppermute(a, 'zh', flip) for flip in flips]]
    ppermute x3 -> x6, waiting for transfers between devices: 36.9 us -> 27.7 us  [the longest x3 27.7 us: body(): lax.ppermute(b_tail, 'yh', flip)]
    ppermute x1, starting transfers between devices: 5.75 us -> 7.36 us  [body(): ladder = mine + lax.ppermute(mine, 'l', [(0, 1), (1, 0)])]
    unnamed x12 -> x10, local copies, waits for them, and re-layouts: 3.42 us -> 2.03 us
    pallas_call x2, Pallas kernels: 1.12 us -> 2.46 us  [the longest x1 1.61 us: pack_b(): pl.pallas_call(pack_b_kernel, out_shape=jax.ShapeDtypeStruct((PIECES, 4,...]
    all_to_all x1, blocking collectives: 13.5 us -> 14.6 us  [body(): partial = lax.all_to_all(partial, NEAR, 0, 0, tiled=True)]
  transfers between devices with their start and end apart: 6 -> 9, of which waited for: 4 -> 4; matrix products, arithmetic and copies ran while one was open for 0% -> 1% of each run, Pallas kernels for 0% -> 1%
where the time goes in v9:
time: 110 us; the launch traced here: 109 us
  starting transfers between devices  52.9 us (48%)
  waiting for transfers between devices  32.8 us (30%)
  blocking collectives  14.6 us (13%)
  Pallas kernels  4.1 us (4%)
  local copies, waits for them, and re-layouts  2.91 us (3%)
  other arithmetic  1.68 us (2%)
    ppermute x3, waiting for transfers between devices, body(): lax.ppermute(b_tail, 'yh', flip)  27.7 us
    ppermute x3, starting transfers between devices, body(): a_slots = [a] + [lax.ppermute(a, 'zh', flip) for flip in flips]  15.7 us
    all_to_all x1, blocking collectives, body(): partial = lax.all_to_all(partial, NEAR, 0, 0, tiled=True)  14.6 us
    ppermute x3, starting transfers between devices, body(): lax.ppermute(b_tail, 'yh', flip)  13.3 us
    all_to_all x1, starting transfers between devices, body(): lax.all_to_all(b.reshape((4 * PIECES,) + b.shape[2:]), NEAR + ('yh',), 0,...  8.78 us
    all_to_all x1, starting transfers between devices, body(): lax.all_to_all(pack_a(amplitudes, integrals[MAIN:]), NEAR, 0, 0, tiled=True)  7.77 us
    ppermute x1, starting transfers between devices, body(): ladder = mine + lax.ppermute(mine, 'l', [(0, 1), (1, 0)])  7.36 us
    all_to_all x1, waiting for transfers between devices, body(): lax.all_to_all(pack_a(amplitudes, integrals[MAIN:]), NEAR, 0, 0, tiled=True)  4.26 us
  transfers between devices with their start and end apart: 9, of which 4 were waited for; matrix products, arithmetic and copies ran while one was open for 1% of the time, Pallas kernels for 1%

profile of v9, /device:TPU:1, one launch (start us, length us, event | category | flops | bytes accessed | tf_op | source)
XLA Modules:
  0.0 109.2 jit_solution(16248885893529044403)
XLA Ops:
  0.0 0.8 slice.9.b_tail_ref
  0.8 0.9 copy-done.1
  1.8 0.9 shard_map.55
  2.6 7.8 %all-to-all-start = ((bf16[16,80,128]{2,1,0:T(8,128)(2,1)}), bf16[16,80,128]{2,1,0:T(8,128)(2,1)S(1)}, u32[]{:S(2)}, u32[]{:S(2)}) async-start(bf16[16,80,128]{2,1,0:T(8,128)(2,1)} %shard_map.55), calls=%async_computation | async-start | bytes 655360 | tf_op jit(solution)/shard_map/all_to_all | solution.py:119
  10.4 0.0 copy-start
  10.4 1.1 copy-done
  11.5 1.6 %shard_map.56 = bf16[16,4,128,128]{3,2,1,0:T(8,128)(2,1)} custom-call(bf16[2304,128]{1,0:T(8,128)(2,1)S(1)} %copy-done), custom_call_target="tpu_custom_call" | custom-call | bytes 2359296 | tf_op jit(solution)/shard_map/pallas_call | solution.py:54
  13.1 4.3 %all-to-all-done = bf16[16,80,128]{2,1,0:T(8,128)(2,1)S(1)} async-done(((bf16[16,80,128]{2,1,0:T(8,128)(2,1)}), bf16[16,80,128]{2,1,0:T(8,128)(2,1)S(1)}, u32[]{:S(2)}, u32[]{:S(2)}) %all-to-all-start) | async-done | bytes 327712 | tf_op jit(solution)/shard_map/all_to_all | solution.py:119
  17.4 8.8 %all-to-all-start.1 = ((bf16[64,128,128]{2,1,0:T(8,128)(2,1)}), bf16[64,128,128]{2,1,0:T(8,128)(2,1)S(1)}, u32[]{:S(2)}, u32[]{:S(2)}) async-start(bf16[64,128,128]{2,1,0:T(8,128)(2,1)} %bitcast.2), calls=%async_computation.1 | async-start | bytes 4194304 | tf_op jit(solution)/shard_map/all_to_all | solution.py:122
  26.2 6.8 %collective-permute-start.4 = (bf16[16,16,128]{2,1,0:T(8,128)(2,1)S(1)}, bf16[16,16,128]{2,1,0:T(8,128)(2,1)}, u32[]{:S(2)}, u32[]{:S(2)}) collective-permute-start(bf16[16,16,128]{2,1,0:T(8,128)(2,1)S(1)} %get-tuple-element.6), channel_id=1, source_target_pairs={{0,128},{64,192},{128,0},{192,64},{1,129},{65,193},{129,1},{193,65... | collective-permute-start | bytes 196616 | tf_op jit(solution)/shard_map/ppermute | solution.py:124
  33.0 9.8 %collective-permute-start.2 = (bf16[16,64,128]{2,1,0:T(8,128)(2,1)S(1)}, bf16[16,64,128]{2,1,0:T(8,128)(2,1)S(1)}, u32[]{:S(2)}, u32[]{:S(2)}) collective-permute-start(bf16[16,64,128]{2,1,0:T(8,128)(2,1)S(1)} %slice.12.refs_0_), channel_id=1, source_target_pairs={{0,6},{2,4},{4,2},{6,0},{1,7},{3,5},{5,3},{7,1},{8,14},{10,12},{12... | collective-permute-start | bytes 786440 | tf_op jit(solution)/shard_map/ppermute | solution.py:125
  42.8 1.9 %collective-permute-start.1 = (bf16[16,64,128]{2,1,0:T(8,128)(2,1)S(1)}, bf16[16,64,128]{2,1,0:T(8,128)(2,1)S(1)}, u32[]{:S(2)}, u32[]{:S(2)}) collective-permute-start(bf16[16,64,128]{2,1,0:T(8,128)(2,1)S(1)} %slice.12.refs_0_), channel_id=1, source_target_pairs={{0,4},{2,6},{4,0},{6,2},{1,5},{3,7},{5,1},{7,3},{8,12},{10,14},{12... | collective-permute-start | bytes 786440 | tf_op jit(solution)/shard_map/ppermute | solution.py:125
  44.7 4.0 %collective-permute-start = (bf16[16,64,128]{2,1,0:T(8,128)(2,1)S(1)}, bf16[16,64,128]{2,1,0:T(8,128)(2,1)S(1)}, u32[]{:S(2)}, u32[]{:S(2)}) collective-permute-start(bf16[16,64,128]{2,1,0:T(8,128)(2,1)S(1)} %slice.12.refs_0_), channel_id=1, source_target_pairs={{0,2},{2,0},{4,6},{6,4},{1,3},{3,1},{5,7},{7,5},{8,10},{10,8},{12,... | collective-permute-start | bytes 786440 | tf_op jit(solution)/shard_map/ppermute | solution.py:125
  48.7 2.2 %collective-permute-start.3 = (bf16[16,16,128]{2,1,0:T(8,128)(2,1)S(1)}, bf16[16,16,128]{2,1,0:T(8,128)(2,1)S(1)}, u32[]{:S(2)}, u32[]{:S(2)}) collective-permute-start(bf16[16,16,128]{2,1,0:T(8,128)(2,1)S(1)} %get-tuple-element.6), channel_id=1, source_target_pairs={{0,64},{64,0},{128,192},{192,128},{1,65},{65,1},{129,193},{193,129... | collective-permute-start | bytes 196616 | tf_op jit(solution)/shard_map/ppermute | solution.py:124
  50.9 24.7 %collective-permute-done.4 = bf16[16,16,128]{2,1,0:T(8,128)(2,1)} collective-permute-done((bf16[16,16,128]{2,1,0:T(8,128)(2,1)S(1)}, bf16[16,16,128]{2,1,0:T(8,128)(2,1)}, u32[]{:S(2)}, u32[]{:S(2)}) %collective-permute-start.4) | collective-permute-done | bytes 65568 | tf_op jit(solution)/shard_map/ppermute | solution.py:124
  75.6 4.3 %collective-permute-start.5 = (bf16[16,16,128]{2,1,0:T(8,128)(2,1)S(1)}, bf16[16,16,128]{2,1,0:T(8,128)(2,1)S(1)}, u32[]{:S(2)}, u32[]{:S(2)}) collective-permute-start(bf16[16,16,128]{2,1,0:T(8,128)(2,1)S(1)} %get-tuple-element.6), channel_id=1, source_target_pairs={{0,192},{64,128},{128,64},{192,0},{1,193},{65,129},{129,65},{193,1... | collective-permute-start | bytes 196616 | tf_op jit(solution)/shard_map/ppermute | solution.py:124
  79.9 0.1 pad_add_fusion.place_ref
  80.0 0.0 collective-permute-done.3
  80.0 3.0 %collective-permute-done.5 = bf16[16,16,128]{2,1,0:T(8,128)(2,1)S(1)} collective-permute-done((bf16[16,16,128]{2,1,0:T(8,128)(2,1)S(1)}, bf16[16,16,128]{2,1,0:T(8,128)(2,1)S(1)}, u32[]{:S(2)}, u32[]{:S(2)}) %collective-permute-start.5) | collective-permute-done | bytes 65568 | tf_op jit(solution)/shard_map/ppermute | solution.py:124
  83.0 0.9 pad_maximum_fusion.refs_5_
  83.9 0.0 collective-permute-done.2.refs_3_
  83.9 0.0 collective-permute-done.1.refs_2_
  83.9 0.0 collective-permute-done.refs_1_
  83.9 0.0 all-to-all-done.1
  83.9 0.0 copy-start.2
  84.0 0.0 copy-start.3
  84.0 0.0 copy-start.4
  84.0 1.6 %shard_map.57 = f32[16,56,128]{2,1,0:T(8,128)S(1)} custom-call(s32[2]{0:T(128)S(1)} %pad_add_fusion.place_ref, bf16[16,64,128]{2,1,0:T(8,128)(2,1)S(1)} %slice.12.refs_0_, bf16[16,64,128]{2,1,0:T(8,128)(2,1)S(1)} %collective-permute-done.refs_1_, bf16[16,64,128]{2,1,0:T(8,128)(2,1)S(1)} %collective-permute-done.1.refs_2_, ...), custom_call_target="tpu_custom_call" | custom-call | tf_op jit(solution)/shard_map/pallas_call | solution.py:104
  85.6 14.6 %all_to_all.15 = f32[16,56,128]{2,1,0:T(8,128)S(1)} all-to-all(f32[16,56,128]{2,1,0:T(8,128)S(1)} %shard_map.57), channel_id=1, replica_groups=mesh['l'=2,'yh'=4,'yl'=2,'xl'=2,'xh'=2,'zh'=4,'zl'=2] {'yl','xl','xh','zl'}, dimensions={0} | all-to-all | bytes 917504 | tf_op jit(solution)/shard_map/all_to_all | solution.py:128
  100.3 7.4 %collective-permute-start.6 = (f32[56,128]{1,0:T(8,128)S(1)}, f32[56,128]{1,0:T(8,128)S(1)}, u32[]{:S(2)}, u32[]{:S(2)}) collective-permute-start(f32[56,128]{1,0:T(8,128)S(1)} %reduce_sum.9), channel_id=1, source_target_pairs={{0,256},{256,0},{1,257},{257,1},{2,258},{258,2},{3,259},{259,3},{4... | collective-permute-start | bytes 86024 | tf_op jit(solution)/shard_map/ppermute | solution.py:130
  107.6 0.8 collective-permute-done.6
  108.5 0.7 subtract_divide_fusion
  (7 shorter events, 0.1 us)
Async XLA Ops:
  0.8 0.9 copy-start.1
  2.6 14.7 %all-to-all-start = ((bf16[16,80,128]{2,1,0:T(8,128)(2,1)}), bf16[16,80,128]{2,1,0:T(8,128)(2,1)S(1)}, u32[]{:S(2)}, u32[]{:S(2)}) async-start(bf16[16,80,128]{2,1,0:T(8,128)(2,1)} %shard_map.55), calls=%async_computation | async-start | bytes 655360 | tf_op jit(solution)/shard_map/all_to_all | solution.py:119
  10.4 1.1 copy-start
  17.4 66.6 %all-to-all-start.1 = ((bf16[64,128,128]{2,1,0:T(8,128)(2,1)}), bf16[64,128,128]{2,1,0:T(8,128)(2,1)S(1)}, u32[]{:S(2)}, u32[]{:S(2)}) async-start(bf16[64,128,128]{2,1,0:T(8,128)(2,1)} %bitcast.2), calls=%async_computation.1 | async-start | bytes 4194304 | tf_op jit(solution)/shard_map/all_to_all | solution.py:122
  26.2 49.5 %collective-permute-start.4 = (bf16[16,16,128]{2,1,0:T(8,128)(2,1)S(1)}, bf16[16,16,128]{2,1,0:T(8,128)(2,1)}, u32[]{:S(2)}, u32[]{:S(2)}) collective-permute-start(bf16[16,16,128]{2,1,0:T(8,128)(2,1)S(1)} %get-tuple-element.6), channel_id=1, source_target_pairs={{0,128},{64,192},{128,0},{192,64},{1,129},{65,193},{129,1},{193,65... | collective-permute-start | bytes 196616 | tf_op jit(solution)/shard_map/ppermute | solution.py:124
  33.0 50.9 %collective-permute-start.2 = (bf16[16,64,128]{2,1,0:T(8,128)(2,1)S(1)}, bf16[16,64,128]{2,1,0:T(8,128)(2,1)S(1)}, u32[]{:S(2)}, u32[]{:S(2)}) collective-permute-start(bf16[16,64,128]{2,1,0:T(8,128)(2,1)S(1)} %slice.12.refs_0_), channel_id=1, source_target_pairs={{0,6},{2,4},{4,2},{6,0},{1,7},{3,5},{5,3},{7,1},{8,14},{10,12},{12... | collective-permute-start | bytes 786440 | tf_op jit(solution)/shard_map/ppermute | solution.py:125
  42.8 41.1 %collective-permute-start.1 = (bf16[16,64,128]{2,1,0:T(8,128)(2,1)S(1)}, bf16[16,64,128]{2,1,0:T(8,128)(2,1)S(1)}, u32[]{:S(2)}, u32[]{:S(2)}) collective-permute-start(bf16[16,64,128]{2,1,0:T(8,128)(2,1)S(1)} %slice.12.refs_0_), channel_id=1, source_target_pairs={{0,4},{2,6},{4,0},{6,2},{1,5},{3,7},{5,1},{7,3},{8,12},{10,14},{12... | collective-permute-start | bytes 786440 | tf_op jit(solution)/shard_map/ppermute | solution.py:125
  44.7 39.2 %collective-permute-start = (bf16[16,64,128]{2,1,0:T(8,128)(2,1)S(1)}, bf16[16,64,128]{2,1,0:T(8,128)(2,1)S(1)}, u32[]{:S(2)}, u32[]{:S(2)}) collective-permute-start(bf16[16,64,128]{2,1,0:T(8,128)(2,1)S(1)} %slice.12.refs_0_), channel_id=1, source_target_pairs={{0,2},{2,0},{4,6},{6,4},{1,3},{3,1},{5,7},{7,5},{8,10},{10,8},{12,... | collective-permute-start | bytes 786440 | tf_op jit(solution)/shard_map/ppermute | solution.py:125
  48.7 31.3 %collective-permute-start.3 = (bf16[16,16,128]{2,1,0:T(8,128)(2,1)S(1)}, bf16[16,16,128]{2,1,0:T(8,128)(2,1)S(1)}, u32[]{:S(2)}, u32[]{:S(2)}) collective-permute-start(bf16[16,16,128]{2,1,0:T(8,128)(2,1)S(1)} %get-tuple-element.6), channel_id=1, source_target_pairs={{0,64},{64,0},{128,192},{192,128},{1,65},{65,1},{129,193},{193,129... | collective-permute-start | bytes 196616 | tf_op jit(solution)/shard_map/ppermute | solution.py:124
  75.6 7.4 %collective-permute-start.5 = (bf16[16,16,128]{2,1,0:T(8,128)(2,1)S(1)}, bf16[16,16,128]{2,1,0:T(8,128)(2,1)S(1)}, u32[]{:S(2)}, u32[]{:S(2)}) collective-permute-start(bf16[16,16,128]{2,1,0:T(8,128)(2,1)S(1)} %get-tuple-element.6), channel_id=1, source_target_pairs={{0,192},{64,128},{128,64},{192,0},{1,193},{65,129},{129,65},{193,1... | collective-permute-start | bytes 196616 | tf_op jit(solution)/shard_map/ppermute | solution.py:124
  83.9 24.5 %copy-start.2 = (f32[56,128]{1,0:T(8,128)S(1)}, f32[56,128]{1,0:T(8,128)}, u32[]{:S(2)}) copy-start(f32[56,128]{1,0:T(8,128)} %param.7) | copy-start | bytes 86020
  84.0 24.5 %copy-start.3 = (f32[128]{0:T(128)S(1)}, f32[128]{0:T(128)}, u32[]{:S(2)}) copy-start(f32[128]{0:T(128)} %param.9) | copy-start | bytes 1540
  84.0 24.5 %copy-start.4 = (f32[56]{0:T(128)S(1)}, f32[56]{0:T(128)}, u32[]{:S(2)}) copy-start(f32[56]{0:T(128)} %param.8) | copy-start | bytes 676
  100.3 8.2 %collective-permute-start.6 = (f32[56,128]{1,0:T(8,128)S(1)}, f32[56,128]{1,0:T(8,128)S(1)}, u32[]{:S(2)}, u32[]{:S(2)}) collective-permute-start(f32[56,128]{1,0:T(8,128)S(1)} %reduce_sum.9), channel_id=1, source_target_pairs={{0,256},{256,0},{1,257},{257,1},{2,258},{258,2},{3,259},{259,3},{4... | collective-permute-start | bytes 86024 | tf_op jit(solution)/shard_map/ppermute | solution.py:130

commit v10 on v8

--- a/solution.py
+++ b/solution.py
@@ -71,6 +71,9 @@
             piece = 4 * (2 * b1 + b0) + c
             right[t * LANES : (t + 1) * LANES, columns] = b_ref[piece, 2 * b3 + b2, 0:LANES, :]
             right[MAIN + t * REST : MAIN + (t + 1) * REST, columns] = b_ref[piece, 2 * b3 + b2, LANES:, :]
+        if t == PIECES // 2 - 1:
+            part = slice(0, MAIN // 2)
+            total = jnp.dot(left[:, part], right[part, :], preferred_element_type=jnp.float32)
     spread[...] = jnp.zeros_like(spread)
     for half in range(2):
         for g in range(ROWS // 8):
@@ -83,7 +86,8 @@
             for r in range(4):
                 spread[A_ROWS * r + 8 * g : A_ROWS * r + 8 * g + 8, half * LANES : (half + 1) * LANES] = rest[8 * r : 8 * r + 8]
     left[:, MAIN:] = spread[...].astype(jnp.bfloat16)
-    total = jnp.dot(left[...], right[...], preferred_element_type=jnp.float32)
+    part = slice(MAIN // 2, PIECES * (LANES + REST))
+    total = total + jnp.dot(left[:, part], right[part, :], preferred_element_type=jnp.float32)
     for r in range(4):
         for c in range(4):
             out_ref[4 * r + c] = total[A_ROWS * r : A_ROWS * r + ROWS, c * LANES : (c + 1) * LANES]

time: 100 us -> 100 us (level)
  no operation moved by 1% of the time
where the time goes in v10:
time: 100 us; the launch traced here: 99.5 us
  waiting for transfers between devices  42.1 us (42%)
  starting transfers between devices  37.4 us (37%)
  blocking collectives  13.5 us (14%)
  local copies, waits for them, and re-layouts  3.42 us (3%)
  Pallas kernels  2.19 us (2%)
    ppermute x3, waiting for transfers between devices, body(): lax.ppermute(a, 'zh', [(i, i ^ d) for i in range(4)])  36.9 us
    ppermute x3, starting transfers between devices, body(): lax.ppermute(a, 'zh', [(i, i ^ d) for i in range(4)])  15.7 us
    all_to_all x1, blocking collectives, body(): partial = lax.all_to_all(partial, NEAR, 0, 0, tiled=True)  13.5 us
    all_to_all x1, starting transfers between devices, body(): lax.all_to_all(b.reshape((4 * PIECES,) + b.shape[2:]), NEAR + ('yh',), 0,...  8.23 us
    all_to_all x1, starting transfers between devices, body(): a = lax.all_to_all(a, NEAR, 0, 0, tiled=True)  7.77 us
    ppermute x1, starting transfers between devices, body(): ladder = mine + lax.ppermute(mine, 'l', [(0, 1), (1, 0)])  5.75 us
    all_to_all x1, waiting for transfers between devices, body(): a = lax.all_to_all(a, NEAR, 0, 0, tiled=True)  3.92 us
    unnamed x12, local copies, waits for them, and re-layouts  3.42 us
  transfers between devices with their start and end apart: 6, of which 4 were waited for; matrix products, arithmetic and copies ran while one was open for 0% of the time, Pallas kernels for 0%

profile of v10, /device:TPU:1, one launch (start us, length us, event | category | flops | bytes accessed | tf_op | source)
XLA Modules:
  0.0 99.5 jit_solution(2860130724884153587)
XLA Ops:
  0.0 0.0 copy-start.2
  0.0 0.9 copy-done.2
  0.9 0.8 shard_map.55
  1.8 7.8 %all-to-all-start = ((bf16[16,64,128]{2,1,0:T(8,128)(2,1)}), bf16[16,64,128]{2,1,0:T(8,128)(2,1)S(1)}, u32[]{:S(2)}, u32[]{:S(2)}) async-start(bf16[16,64,128]{2,1,0:T(8,128)(2,1)} %shard_map.55), calls=%async_computation | async-start | bytes 524288 | tf_op jit(solution)/shard_map/all_to_all | solution.py:116
  9.5 0.0 copy-start.1
  9.6 1.1 %copy-done.1 = bf16[2304,128]{1,0:T(8,128)(2,1)S(1)} copy-done((bf16[2304,128]{1,0:T(8,128)(2,1)S(1)}, bf16[2304,128]{1,0:T(8,128)(2,1)}, u32[]{:S(2)}) %copy-start.1) | copy-done | bytes 589848
  10.6 0.3 shard_map.56
  10.9 0.0 copy-start
  10.9 1.4 %copy-done = bf16[16,4,144,128]{3,2,1,0:T(8,128)(2,1)} copy-done((bf16[16,4,144,128]{3,2,1,0:T(8,128)(2,1)}, bf16[16,4,144,128]{3,2,1,0:T(8,128)(2,1)S(1)}, u32[]{:S(2)}) %copy-start) | copy-done | bytes 2359320
  12.3 3.9 %all-to-all-done.refs_0_ = bf16[16,64,128]{2,1,0:T(8,128)(2,1)S(1)} async-done(((bf16[16,64,128]{2,1,0:T(8,128)(2,1)}), bf16[16,64,128]{2,1,0:T(8,128)(2,1)S(1)}, u32[]{:S(2)}, u32[]{:S(2)}) %all-to-all-start) | async-done | bytes 262176 | tf_op jit(solution)/shard_map/all_to_all | solution.py:116
  16.3 8.2 %all-to-all-start.1 = ((bf16[64,144,128]{2,1,0:T(8,128)(2,1)}), bf16[64,144,128]{2,1,0:T(8,128)(2,1)S(1)}, u32[]{:S(2)}, u32[]{:S(2)}) async-start(bf16[64,144,128]{2,1,0:T(8,128)(2,1)} %bitcast.4), calls=%async_computation.1 | async-start | bytes 4718592 | tf_op jit(solution)/shard_map/all_to_all | solution.py:115
  24.5 5.8 %collective-permute-start = (bf16[16,64,128]{2,1,0:T(8,128)(2,1)S(1)}, bf16[16,64,128]{2,1,0:T(8,128)(2,1)S(1)}, u32[]{:S(2)}, u32[]{:S(2)}) collective-permute-start(bf16[16,64,128]{2,1,0:T(8,128)(2,1)S(1)} %all-to-all-done.refs_0_), channel_id=1, source_target_pairs={{0,2},{2,0},{4,6},{6,4},{1,3},{3,1},{5,7},{7,5},{8,10},{10,8},{12,... | collective-permute-start | bytes 786440 | tf_op jit(solution)/shard_map/ppermute | solution.py:117
  30.3 7.9 %collective-permute-start.1 = (bf16[16,64,128]{2,1,0:T(8,128)(2,1)S(1)}, bf16[16,64,128]{2,1,0:T(8,128)(2,1)S(1)}, u32[]{:S(2)}, u32[]{:S(2)}) collective-permute-start(bf16[16,64,128]{2,1,0:T(8,128)(2,1)S(1)} %all-to-all-done.refs_0_), channel_id=1, source_target_pairs={{0,4},{2,6},{4,0},{6,2},{1,5},{3,7},{5,1},{7,3},{8,12},{10,14},{12... | collective-permute-start | bytes 786440 | tf_op jit(solution)/shard_map/ppermute | solution.py:117
  38.3 1.9 %collective-permute-start.2 = (bf16[16,64,128]{2,1,0:T(8,128)(2,1)S(1)}, bf16[16,64,128]{2,1,0:T(8,128)(2,1)S(1)}, u32[]{:S(2)}, u32[]{:S(2)}) collective-permute-start(bf16[16,64,128]{2,1,0:T(8,128)(2,1)S(1)} %all-to-all-done.refs_0_), channel_id=1, source_target_pairs={{0,6},{2,4},{4,2},{6,0},{1,7},{3,5},{5,3},{7,1},{8,14},{10,12},{12... | collective-permute-start | bytes 786440 | tf_op jit(solution)/shard_map/ppermute | solution.py:117
  40.2 0.0 collective-permute-done.refs_1_
  40.2 36.9 %collective-permute-done.1.refs_2_ = bf16[16,64,128]{2,1,0:T(8,128)(2,1)S(1)} collective-permute-done((bf16[16,64,128]{2,1,0:T(8,128)(2,1)S(1)}, bf16[16,64,128]{2,1,0:T(8,128)(2,1)S(1)}, u32[]{:S(2)}, u32[]{:S(2)}) %collective-permute-start.1) | collective-permute-done | bytes 262176 | tf_op jit(solution)/shard_map/ppermute | solution.py:117
  77.1 0.0 collective-permute-done.2.refs_3_
  77.1 0.5 all-to-all-done.1
  77.6 0.0 copy-start.3
  77.6 0.0 copy-start.4
  77.6 0.0 copy-start.5
  77.6 1.1 %shard_map.57 = f32[16,56,128]{2,1,0:T(8,128)S(1)} custom-call(s32[1]{0:T(128)} %bitcast.my_zh_ref, bf16[16,64,128]{2,1,0:T(8,128)(2,1)S(1)} %all-to-all-done.refs_0_, bf16[16,64,128]{2,1,0:T(8,128)(2,1)S(1)} %collective-permute-done.refs_1_, bf16[16,64,128]{2,1,0:T(8,128)(2,1)S(1)} %collective-permute-done.1.refs_2_, ...), custom_call_target="tpu_custom_call" | custom-call | tf_op jit(solution)/shard_map/pallas_call | solution.py:98
  78.7 13.5 %all_to_all.15 = f32[16,56,128]{2,1,0:T(8,128)S(1)} all-to-all(f32[16,56,128]{2,1,0:T(8,128)S(1)} %shard_map.57), channel_id=1, replica_groups=mesh['l'=2,'yh'=4,'yl'=2,'xl'=2,'xh'=2,'zh'=4,'zl'=2] {'yl','xl','xh','zl'}, dimensions={0} | all-to-all | bytes 917504 | tf_op jit(solution)/shard_map/all_to_all | solution.py:120
  92.2 5.7 %collective-permute-start.3 = (f32[56,128]{1,0:T(8,128)S(1)}, f32[56,128]{1,0:T(8,128)S(1)}, u32[]{:S(2)}, u32[]{:S(2)}) collective-permute-start(f32[56,128]{1,0:T(8,128)S(1)} %reduce_sum.9), channel_id=1, source_target_pairs={{0,256},{256,0},{1,257},{257,1},{2,258},{258,2},{3,259},{259,3},{4... | collective-permute-start | bytes 86024 | tf_op jit(solution)/shard_map/ppermute | solution.py:122
  97.9 0.8 collective-permute-done.3
  98.8 0.0 copy-done.3
  98.8 0.0 copy-done.4
  98.8 0.0 copy-done.5
  98.8 0.7 subtract_divide_fusion
  (1 shorter events, 0.0 us)
Async XLA Ops:
  0.0 0.9 copy-start.2
  1.8 14.5 %all-to-all-start = ((bf16[16,64,128]{2,1,0:T(8,128)(2,1)}), bf16[16,64,128]{2,1,0:T(8,128)(2,1)S(1)}, u32[]{:S(2)}, u32[]{:S(2)}) async-start(bf16[16,64,128]{2,1,0:T(8,128)(2,1)} %shard_map.55), calls=%async_computation | async-start | bytes 524288 | tf_op jit(solution)/shard_map/all_to_all | solution.py:116
  9.5 1.1 %copy-start.1 = (bf16[2304,128]{1,0:T(8,128)(2,1)S(1)}, bf16[2304,128]{1,0:T(8,128)(2,1)}, u32[]{:S(2)}) copy-start(bf16[2304,128]{1,0:T(8,128)(2,1)} %b_ref.1) | copy-start | bytes 1769476
  10.9 1.4 %copy-start = (bf16[16,4,144,128]{3,2,1,0:T(8,128)(2,1)}, bf16[16,4,144,128]{3,2,1,0:T(8,128)(2,1)S(1)}, u32[]{:S(2)}) copy-start(bf16[16,4,144,128]{3,2,1,0:T(8,128)(2,1)S(1)} %shard_map.56) | copy-start | bytes 7077892
  16.3 61.3 %all-to-all-start.1 = ((bf16[64,144,128]{2,1,0:T(8,128)(2,1)}), bf16[64,144,128]{2,1,0:T(8,128)(2,1)S(1)}, u32[]{:S(2)}, u32[]{:S(2)}) async-start(bf16[64,144,128]{2,1,0:T(8,128)(2,1)} %bitcast.4), calls=%async_computation.1 | async-start | bytes 4718592 | tf_op jit(solution)/shard_map/all_to_all | solution.py:115
  24.5 15.7 %collective-permute-start = (bf16[16,64,128]{2,1,0:T(8,128)(2,1)S(1)}, bf16[16,64,128]{2,1,0:T(8,128)(2,1)S(1)}, u32[]{:S(2)}, u32[]{:S(2)}) collective-permute-start(bf16[16,64,128]{2,1,0:T(8,128)(2,1)S(1)} %all-to-all-done.refs_0_), channel_id=1, source_target_pairs={{0,2},{2,0},{4,6},{6,4},{1,3},{3,1},{5,7},{7,5},{8,10},{10,8},{12,... | collective-permute-start | bytes 786440 | tf_op jit(solution)/shard_map/ppermute | solution.py:117
  30.3 46.8 %collective-permute-start.1 = (bf16[16,64,128]{2,1,0:T(8,128)(2,1)S(1)}, bf16[16,64,128]{2,1,0:T(8,128)(2,1)S(1)}, u32[]{:S(2)}, u32[]{:S(2)}) collective-permute-start(bf16[16,64,128]{2,1,0:T(8,128)(2,1)S(1)} %all-to-all-done.refs_0_), channel_id=1, source_target_pairs={{0,4},{2,6},{4,0},{6,2},{1,5},{3,7},{5,1},{7,3},{8,12},{10,14},{12... | collective-permute-start | bytes 786440 | tf_op jit(solution)/shard_map/ppermute | solution.py:117
  38.3 38.8 %collective-permute-start.2 = (bf16[16,64,128]{2,1,0:T(8,128)(2,1)S(1)}, bf16[16,64,128]{2,1,0:T(8,128)(2,1)S(1)}, u32[]{:S(2)}, u32[]{:S(2)}) collective-permute-start(bf16[16,64,128]{2,1,0:T(8,128)(2,1)S(1)} %all-to-all-done.refs_0_), channel_id=1, source_target_pairs={{0,6},{2,4},{4,2},{6,0},{1,7},{3,5},{5,3},{7,1},{8,14},{10,12},{12... | collective-permute-start | bytes 786440 | tf_op jit(solution)/shard_map/ppermute | solution.py:117
  77.6 21.2 %copy-start.3 = (f32[56,128]{1,0:T(8,128)S(1)}, f32[56,128]{1,0:T(8,128)}, u32[]{:S(2)}) copy-start(f32[56,128]{1,0:T(8,128)} %param.7) | copy-start | bytes 86020
  77.6 21.2 %copy-start.4 = (f32[128]{0:T(128)S(1)}, f32[128]{0:T(128)}, u32[]{:S(2)}) copy-start(f32[128]{0:T(128)} %param.9) | copy-start | bytes 1540
  77.6 21.2 %copy-start.5 = (f32[56]{0:T(128)S(1)}, f32[56]{0:T(128)}, u32[]{:S(2)}) copy-start(f32[56]{0:T(128)} %param.8) | copy-start | bytes 676
  92.2 6.6 %collective-permute-start.3 = (f32[56,128]{1,0:T(8,128)S(1)}, f32[56,128]{1,0:T(8,128)S(1)}, u32[]{:S(2)}, u32[]{:S(2)}) collective-permute-start(f32[56,128]{1,0:T(8,128)S(1)} %reduce_sum.9), channel_id=1, source_target_pairs={{0,256},{256,0},{1,257},{257,1},{2,258},{258,2},{3,259},{259,3},{4... | collective-permute-start | bytes 86024 | tf_op jit(solution)/shard_map/ppermute | solution.py:122

commit v11 on v8

--- a/solution.py
+++ b/solution.py
@@ -58,7 +58,7 @@
     tails = []
     for t in range(PIECES):
         flip, b3, b0 = t >> 2, (t >> 1) & 1, t & 1
-        zh = my_zh ^ flip
+        zh = (my_zh + 4 - flip) & 3
         b2, b1 = zh >> 1, zh & 1
         tail = []
         for r in range(4):
@@ -110,7 +110,7 @@
     b = pack(pack_b_kernel, integrals, (PIECES, 4, B_ROWS, LANES))
     b_slots = lax.all_to_all(b.reshape((4 * PIECES,) + b.shape[2:]), NEAR + ("yh",), 0, 0, tiled=True).reshape(b.shape)
     a = lax.all_to_all(a, NEAR, 0, 0, tiled=True)
-    a_slots = [a] + [lax.ppermute(a, "zh", [(i, i ^ d) for i in range(4)]) for d in (1, 2, 3)]
+    a_slots = [a] + [lax.ppermute(a, "zh", [(i, (i + d) % 4) for i in range(4)]) for d in (1, 2, 3)]
     my_zh = lax.axis_index("zh").astype(jnp.int32)[None]
     partial = multiply(my_zh, a_slots, b_slots)
     partial = lax.all_to_all(partial, NEAR, 0, 0, tiled=True)

time: 100 us -> 101 us (1.010)
    ppermute x3, starting transfers between devices: 15.7 us -> 17.1 us  [body(): lax.ppermute(a, 'zh', [(i, (i + d) % 4) for i in range(4)])]
where the time goes in v11:
time: 101 us; the launch traced here: 100 us
  waiting for transfers between devices  41.4 us (41%)
  starting transfers between devices  37.9 us (38%)
  blocking collectives  14.3 us (14%)
  local copies, waits for them, and re-layouts  3.43 us (3%)
  Pallas kernels  2.24 us (2%)
    ppermute x3, waiting for transfers between devices, body(): lax.ppermute(a, 'zh', [(i, (i + d) % 4) for i in range(4)])  36.7 us
    ppermute x3, starting transfers between devices, body(): lax.ppermute(a, 'zh', [(i, (i + d) % 4) for i in range(4)])  17.1 us
    all_to_all x1, blocking collectives, body(): partial = lax.all_to_all(partial, NEAR, 0, 0, tiled=True)  14.3 us
    all_to_all x1, starting transfers between devices, body(): lax.all_to_all(b.reshape((4 * PIECES,) + b.shape[2:]), NEAR + ('yh',), 0,...  8.23 us
    all_to_all x1, starting transfers between devices, body(): a = lax.all_to_all(a, NEAR, 0, 0, tiled=True)  7.77 us
    ppermute x1, starting transfers between devices, body(): ladder = mine + lax.ppermute(mine, 'l', [(0, 1), (1, 0)])  4.81 us
    all_to_all x1, waiting for transfers between devices, body(): a = lax.all_to_all(a, NEAR, 0, 0, tiled=True)  3.92 us
    unnamed x12, local copies, waits for them, and re-layouts  3.43 us
  transfers between devices with their start and end apart: 6, of which 4 were waited for; matrix products, arithmetic and copies ran while one was open for 0% of the time, Pallas kernels for 0%

profile of v11, /device:TPU:1, one launch (start us, length us, event | category | flops | bytes accessed | tf_op | source)
XLA Modules:
  0.0 100.2 jit_solution(14983364163818671663)
XLA Ops:
  0.0 0.0 copy-start.2
  0.0 0.9 copy-done.2
  0.9 0.8 shard_map.55
  1.8 7.8 %all-to-all-start = ((bf16[16,64,128]{2,1,0:T(8,128)(2,1)}), bf16[16,64,128]{2,1,0:T(8,128)(2,1)S(1)}, u32[]{:S(2)}, u32[]{:S(2)}) async-start(bf16[16,64,128]{2,1,0:T(8,128)(2,1)} %shard_map.55), calls=%async_computation | async-start | bytes 524288 | tf_op jit(solution)/shard_map/all_to_all | solution.py:112
  9.5 0.0 copy-start.1
  9.6 1.1 %copy-done.1 = bf16[2304,128]{1,0:T(8,128)(2,1)S(1)} copy-done((bf16[2304,128]{1,0:T(8,128)(2,1)S(1)}, bf16[2304,128]{1,0:T(8,128)(2,1)}, u32[]{:S(2)}) %copy-start.1) | copy-done | bytes 589848
  10.6 0.3 shard_map.56
  10.9 0.0 copy-start
  10.9 1.4 %copy-done = bf16[16,4,144,128]{3,2,1,0:T(8,128)(2,1)} copy-done((bf16[16,4,144,128]{3,2,1,0:T(8,128)(2,1)}, bf16[16,4,144,128]{3,2,1,0:T(8,128)(2,1)S(1)}, u32[]{:S(2)}) %copy-start) | copy-done | bytes 2359320
  12.3 3.9 %all-to-all-done.refs_0_ = bf16[16,64,128]{2,1,0:T(8,128)(2,1)S(1)} async-done(((bf16[16,64,128]{2,1,0:T(8,128)(2,1)}), bf16[16,64,128]{2,1,0:T(8,128)(2,1)S(1)}, u32[]{:S(2)}, u32[]{:S(2)}) %all-to-all-start) | async-done | bytes 262176 | tf_op jit(solution)/shard_map/all_to_all | solution.py:112
  16.3 8.2 %all-to-all-start.1 = ((bf16[64,144,128]{2,1,0:T(8,128)(2,1)}), bf16[64,144,128]{2,1,0:T(8,128)(2,1)S(1)}, u32[]{:S(2)}, u32[]{:S(2)}) async-start(bf16[64,144,128]{2,1,0:T(8,128)(2,1)} %bitcast.4), calls=%async_computation.1 | async-start | bytes 4718592 | tf_op jit(solution)/shard_map/all_to_all | solution.py:111
  24.5 5.8 %collective-permute-start = (bf16[16,64,128]{2,1,0:T(8,128)(2,1)S(1)}, bf16[16,64,128]{2,1,0:T(8,128)(2,1)S(1)}, u32[]{:S(2)}, u32[]{:S(2)}) collective-permute-start(bf16[16,64,128]{2,1,0:T(8,128)(2,1)S(1)} %all-to-all-done.refs_0_), channel_id=1, source_target_pairs={{0,2},{2,4},{4,6},{6,0},{1,3},{3,5},{5,7},{7,1},{8,10},{10,12},{12... | collective-permute-start | bytes 786440 | tf_op jit(solution)/shard_map/ppermute | solution.py:113
  30.3 7.9 %collective-permute-start.1 = (bf16[16,64,128]{2,1,0:T(8,128)(2,1)S(1)}, bf16[16,64,128]{2,1,0:T(8,128)(2,1)S(1)}, u32[]{:S(2)}, u32[]{:S(2)}) collective-permute-start(bf16[16,64,128]{2,1,0:T(8,128)(2,1)S(1)} %all-to-all-done.refs_0_), channel_id=1, source_target_pairs={{0,4},{2,6},{4,0},{6,2},{1,5},{3,7},{5,1},{7,3},{8,12},{10,14},{12... | collective-permute-start | bytes 786440 | tf_op jit(solution)/shard_map/ppermute | solution.py:113
  38.3 3.4 %collective-permute-start.2 = (bf16[16,64,128]{2,1,0:T(8,128)(2,1)S(1)}, bf16[16,64,128]{2,1,0:T(8,128)(2,1)S(1)}, u32[]{:S(2)}, u32[]{:S(2)}) collective-permute-start(bf16[16,64,128]{2,1,0:T(8,128)(2,1)S(1)} %all-to-all-done.refs_0_), channel_id=1, source_target_pairs={{0,6},{2,0},{4,2},{6,4},{1,7},{3,1},{5,3},{7,5},{8,14},{10,8},{12,... | collective-permute-start | bytes 786440 | tf_op jit(solution)/shard_map/ppermute | solution.py:113
  41.6 14.4 %collective-permute-done.refs_1_ = bf16[16,64,128]{2,1,0:T(8,128)(2,1)S(1)} collective-permute-done((bf16[16,64,128]{2,1,0:T(8,128)(2,1)S(1)}, bf16[16,64,128]{2,1,0:T(8,128)(2,1)S(1)}, u32[]{:S(2)}, u32[]{:S(2)}) %collective-permute-start) | collective-permute-done | bytes 262176 | tf_op jit(solution)/shard_map/ppermute | solution.py:113
  56.1 22.3 %collective-permute-done.1.refs_2_ = bf16[16,64,128]{2,1,0:T(8,128)(2,1)S(1)} collective-permute-done((bf16[16,64,128]{2,1,0:T(8,128)(2,1)S(1)}, bf16[16,64,128]{2,1,0:T(8,128)(2,1)S(1)}, u32[]{:S(2)}, u32[]{:S(2)}) %collective-permute-start.1) | collective-permute-done | bytes 262176 | tf_op jit(solution)/shard_map/ppermute | solution.py:113
  78.3 0.0 collective-permute-done.2.refs_3_
  78.3 0.0 all-to-all-done.1
  78.3 0.0 copy-start.3
  78.3 0.0 copy-start.4
  78.3 0.0 copy-start.5
  78.3 1.1 %shard_map.57 = f32[16,56,128]{2,1,0:T(8,128)S(1)} custom-call(s32[1]{0:T(128)} %bitcast.my_zh_ref, bf16[16,64,128]{2,1,0:T(8,128)(2,1)S(1)} %all-to-all-done.refs_0_, bf16[16,64,128]{2,1,0:T(8,128)(2,1)S(1)} %collective-permute-done.refs_1_, bf16[16,64,128]{2,1,0:T(8,128)(2,1)S(1)} %collective-permute-done.1.refs_2_, ...), custom_call_target="tpu_custom_call" | custom-call | tf_op jit(solution)/shard_map/pallas_call | solution.py:94
  79.5 14.3 %all_to_all.15 = f32[16,56,128]{2,1,0:T(8,128)S(1)} all-to-all(f32[16,56,128]{2,1,0:T(8,128)S(1)} %shard_map.57), channel_id=1, replica_groups=mesh['l'=2,'yh'=4,'yl'=2,'xl'=2,'xh'=2,'zh'=4,'zl'=2] {'yl','xl','xh','zl'}, dimensions={0} | all-to-all | bytes 917504 | tf_op jit(solution)/shard_map/all_to_all | solution.py:116
  93.8 4.8 %collective-permute-start.3 = (f32[56,128]{1,0:T(8,128)S(1)}, f32[56,128]{1,0:T(8,128)S(1)}, u32[]{:S(2)}, u32[]{:S(2)}) collective-permute-start(f32[56,128]{1,0:T(8,128)S(1)} %reduce_sum.9), channel_id=1, source_target_pairs={{0,256},{256,0},{1,257},{257,1},{2,258},{258,2},{3,259},{259,3},{4... | collective-permute-start | bytes 86024 | tf_op jit(solution)/shard_map/ppermute | solution.py:118
  98.6 0.8 collective-permute-done.3
  99.5 0.0 copy-done.3
  99.5 0.0 copy-done.4
  99.5 0.0 copy-done.5
  99.5 0.7 subtract_divide_fusion
  (1 shorter events, 0.0 us)
Async XLA Ops:
  0.0 0.9 copy-start.2
  1.8 14.5 %all-to-all-start = ((bf16[16,64,128]{2,1,0:T(8,128)(2,1)}), bf16[16,64,128]{2,1,0:T(8,128)(2,1)S(1)}, u32[]{:S(2)}, u32[]{:S(2)}) async-start(bf16[16,64,128]{2,1,0:T(8,128)(2,1)} %shard_map.55), calls=%async_computation | async-start | bytes 524288 | tf_op jit(solution)/shard_map/all_to_all | solution.py:112
  9.5 1.1 %copy-start.1 = (bf16[2304,128]{1,0:T(8,128)(2,1)S(1)}, bf16[2304,128]{1,0:T(8,128)(2,1)}, u32[]{:S(2)}) copy-start(bf16[2304,128]{1,0:T(8,128)(2,1)} %b_ref.1) | copy-start | bytes 1769476
  10.9 1.4 %copy-start = (bf16[16,4,144,128]{3,2,1,0:T(8,128)(2,1)}, bf16[16,4,144,128]{3,2,1,0:T(8,128)(2,1)S(1)}, u32[]{:S(2)}) copy-start(bf16[16,4,144,128]{3,2,1,0:T(8,128)(2,1)S(1)} %shard_map.56) | copy-start | bytes 7077892
  16.3 62.1 %all-to-all-start.1 = ((bf16[64,144,128]{2,1,0:T(8,128)(2,1)}), bf16[64,144,128]{2,1,0:T(8,128)(2,1)S(1)}, u32[]{:S(2)}, u32[]{:S(2)}) async-start(bf16[64,144,128]{2,1,0:T(8,128)(2,1)} %bitcast.4), calls=%async_computation.1 | async-start | bytes 4718592 | tf_op jit(solution)/shard_map/all_to_all | solution.py:111
  24.5 31.6 %collective-permute-start = (bf16[16,64,128]{2,1,0:T(8,128)(2,1)S(1)}, bf16[16,64,128]{2,1,0:T(8,128)(2,1)S(1)}, u32[]{:S(2)}, u32[]{:S(2)}) collective-permute-start(bf16[16,64,128]{2,1,0:T(8,128)(2,1)S(1)} %all-to-all-done.refs_0_), channel_id=1, source_target_pairs={{0,2},{2,4},{4,6},{6,0},{1,3},{3,5},{5,7},{7,1},{8,10},{10,12},{12... | collective-permute-start | bytes 786440 | tf_op jit(solution)/shard_map/ppermute | solution.py:113
  30.3 48.0 %collective-permute-start.1 = (bf16[16,64,128]{2,1,0:T(8,128)(2,1)S(1)}, bf16[16,64,128]{2,1,0:T(8,128)(2,1)S(1)}, u32[]{:S(2)}, u32[]{:S(2)}) collective-permute-start(bf16[16,64,128]{2,1,0:T(8,128)(2,1)S(1)} %all-to-all-done.refs_0_), channel_id=1, source_target_pairs={{0,4},{2,6},{4,0},{6,2},{1,5},{3,7},{5,1},{7,3},{8,12},{10,14},{12... | collective-permute-start | bytes 786440 | tf_op jit(solution)/shard_map/ppermute | solution.py:113
  38.3 40.1 %collective-permute-start.2 = (bf16[16,64,128]{2,1,0:T(8,128)(2,1)S(1)}, bf16[16,64,128]{2,1,0:T(8,128)(2,1)S(1)}, u32[]{:S(2)}, u32[]{:S(2)}) collective-permute-start(bf16[16,64,128]{2,1,0:T(8,128)(2,1)S(1)} %all-to-all-done.refs_0_), channel_id=1, source_target_pairs={{0,6},{2,0},{4,2},{6,4},{1,7},{3,1},{5,3},{7,5},{8,14},{10,8},{12,... | collective-permute-start | bytes 786440 | tf_op jit(solution)/shard_map/ppermute | solution.py:113
  78.3 21.2 %copy-start.3 = (f32[56,128]{1,0:T(8,128)S(1)}, f32[56,128]{1,0:T(8,128)}, u32[]{:S(2)}) copy-start(f32[56,128]{1,0:T(8,128)} %param.7) | copy-start | bytes 86020
  78.3 21.2 %copy-start.4 = (f32[128]{0:T(128)S(1)}, f32[128]{0:T(128)}, u32[]{:S(2)}) copy-start(f32[128]{0:T(128)} %param.9) | copy-start | bytes 1540
  78.3 21.2 %copy-start.5 = (f32[56]{0:T(128)S(1)}, f32[56]{0:T(128)}, u32[]{:S(2)}) copy-start(f32[56]{0:T(128)} %param.8) | copy-start | bytes 676
  93.8 5.6 %collective-permute-start.3 = (f32[56,128]{1,0:T(8,128)S(1)}, f32[56,128]{1,0:T(8,128)S(1)}, u32[]{:S(2)}, u32[]{:S(2)}) collective-permute-start(f32[56,128]{1,0:T(8,128)S(1)} %reduce_sum.9), channel_id=1, source_target_pairs={{0,256},{256,0},{1,257},{257,1},{2,258},{258,2},{3,259},{259,3},{4... | collective-permute-start | bytes 86024 | tf_op jit(solution)/shard_map/ppermute | solution.py:118
